TPU v7x, 32 devices: a whole 2x2x4 slice. The times are simulated.
32 devices in a mesh: dp: 8 (over y, x, core), mp: 4 (over z).
Axes of the slice: x: 2, y: 2, z: 4, core: 2. Of those that a mesh axis runs over, the one named last changes fastest.
Arguments:
- tokens: bfloat16 [8192, 2048], P(('dp', 'mp')), may hold values from -8 to 8
- cotangent: bfloat16 [8192, 2048], P(('dp', 'mp')), may hold values from -6 to 6
- lengths: int32 [8, 4], P('dp'), may hold values from 1 to 512, 1024 in all within a row
- live_mask: int32 [8192], P(('dp', 'mp')), may hold values 0 or 1
- mixer_gain: float32 [2048], replicated, may hold values from 0.5 to 1.5
- value_proj: bfloat16 [2048, 2560], P(None, 'mp'), may hold values from -0.125 to 0.125
- gate_proj: bfloat16 [2048, 2560], P(None, 'mp'), may hold values from -0.125 to 0.125
- conv_taps: float32 [4, 2560], P(None, 'mp'), may hold values from -3 to 3
- conv_bias: float32 [2560], P('mp'), may hold values from -3 to 3
- rate_weight: float32 [16, 160, 160], P('mp'), may hold values from -0.5 to 0.5
- rate_bias: float32 [2560], P('mp'), may hold values from -3 to 3
- inlet_weight: float32 [16, 160, 160], P('mp'), may hold values from -0.5 to 0.5
- inlet_bias: float32 [2560], P('mp'), may hold values from -3 to 3
- decay_param: float32 [2560], P('mp'), may hold values from 1 to 6
- mixer_out: bfloat16 [2560, 2048], P('mp'), may hold values from -0.3125 to 0.3125
- dense_gain: float32 [2048], replicated, may hold values from 0.5 to 1.5
- dense_gate: bfloat16 [2048, 6144], P(None, 'mp'), may hold values from -0.125 to 0.125
- dense_value: bfloat16 [2048, 6144], P(None, 'mp'), may hold values from -0.125 to 0.125
- dense_down: bfloat16 [6144, 2048], P('mp'), may hold values from -0.15625 to 0.15625
Outputs:
- layer_out: bfloat16 [8192, 2048], P(('dp', 'mp'))
- input_grad: bfloat16 [8192, 2048], P(('dp', 'mp'))
- mixer_gain_grad: float32 [2048], replicated
- value_proj_grad: float32 [2048, 2560], P('dp', 'mp')
- gate_proj_grad: float32 [2048, 2560], P('dp', 'mp')
- conv_taps_grad: float32 [4, 2560], P(None, 'mp')
- conv_bias_grad: float32 [2560], P('mp')
- rate_weight_grad: float32 [16, 160, 160], P('mp')
- rate_bias_grad: float32 [2560], P('mp')
- inlet_weight_grad: float32 [16, 160, 160], P('mp')
- inlet_bias_grad: float32 [2560], P('mp')
- decay_param_grad: float32 [2560], P('mp')
- mixer_out_grad: float32 [2560, 2048], P('mp', 'dp')
- dense_gain_grad: float32 [2048], replicated
- dense_gate_grad: float32 [2048, 6144], P('dp', 'mp')
- dense_value_grad: float32 [2048, 6144], P('dp', 'mp')
- dense_down_grad: float32 [6144, 2048], P('mp', 'dp')
- branch_rms: float32 [3], replicated
Inputs may be any that keep to these rules, and one draw needn't show every extreme that they name: Each row holds 4 lengths summing to 1024; the longest of each row is exactly 512.
All inputs are finite; a program needn't handle non-finite values. No bound on the sum of `live_mask` on one device may be relied on, other than what follows from the above.
Results may differ from a plain program's by a relative error of at most 0.011.
Values may be sent and summed in bfloat16 or wider, within the bound.
A program may use at most 320 MiB of HBM per device.

v0:
```python
import jax
import jax.numpy as jnp
from jax import lax
from jax.sharding import PartitionSpec as P

EPS = 1e-06
HIGHEST = lax.Precision.HIGHEST


def doc_offsets(lengths_row, rows_total):
    doc_ends = jnp.cumsum(lengths_row)
    positions = jnp.arange(rows_total, dtype=jnp.int32)
    before = (doc_ends[None, :] <= positions[:, None]).astype(jnp.int32)
    starts = jnp.sum(before * lengths_row[None, :], axis=1)
    return positions - starts


def scaled_norm(values, gain_vec):
    return (
        values
        * lax.rsqrt(jnp.mean(values * values, axis=1, keepdims=True) + EPS)
        * gain_vec[None, :]
    )


def combine(first_pair, second_pair):
    first_mult, first_add = first_pair
    second_mult, second_add = second_pair
    return (first_mult * second_mult, second_mult * first_add + second_add)


def recurrent(
    value_pre,
    gate_pre,
    conv_taps,
    conv_bias,
    rate_weight,
    rate_bias,
    inlet_weight,
    inlet_bias,
    decay_param,
    offsets,
):
    rows_total, columns = value_pre.shape
    convolved = jnp.zeros_like(value_pre) + conv_bias[None, :]
    for tap_index in range(conv_taps.shape[0]):
        shifted = jnp.concatenate(
            [jnp.zeros((tap_index, columns), value_pre.dtype), value_pre[: rows_total - tap_index]],
            axis=0,
        )
        convolved = (
            convolved
            + jnp.where((offsets >= tap_index)[:, None], shifted, 0.0)
            * conv_taps[tap_index][None, :]
        )
    head_count, head_width = (rate_weight.shape[0], rate_weight.shape[1])
    blocks = convolved.reshape(rows_total, head_count, head_width)
    forget_gate = jax.nn.sigmoid(
        jnp.einsum("thi,hij->thj", blocks, rate_weight, precision=HIGHEST).reshape(
            rows_total, columns
        )
        + rate_bias[None, :]
    )
    input_gate = jax.nn.sigmoid(
        jnp.einsum("thi,hij->thj", blocks, inlet_weight, precision=HIGHEST).reshape(
            rows_total, columns
        )
        + inlet_bias[None, :]
    )
    log_decay = -8.0 * forget_gate * jax.nn.softplus(-decay_param)[None, :]
    carried = jnp.where((offsets > 0)[:, None], jnp.exp(log_decay), 0.0)
    normalizer = jnp.sqrt(-jnp.expm1(2.0 * log_decay))
    unused, states = lax.associative_scan(
        combine, (carried, normalizer * input_gate * convolved), axis=0
    )
    return states * jax.nn.gelu(gate_pre)


def dense_product(left, right):
    return jnp.dot(left, right, preferred_element_type=jnp.float32)


def rows_times_cols(left, right):
    return lax.dot_general(
        left, right, (((1,), (1,)), ((), ())), preferred_element_type=jnp.float32
    )


def rows_inner(left, right):
    return lax.dot_general(
        left, right, (((0,), (0,)), ((), ())), preferred_element_type=jnp.float32
    )


def gated_unit(gate_linear, value_linear):
    return jax.nn.gelu(gate_linear) * value_linear


def local(
    tokens,
    cotangent,
    lengths,
    live_mask,
    mixer_gain,
    value_proj,
    gate_proj,
    conv_taps,
    conv_bias,
    rate_weight,
    rate_bias,
    inlet_weight,
    inlet_bias,
    decay_param,
    mixer_out,
    dense_gain,
    dense_gate,
    dense_value,
    dense_down,
):
    residual = tokens.astype(jnp.float32)
    columns = residual.shape[1]
    normed_first, norm_back_in = jax.vjp(scaled_norm, residual, mixer_gain)
    normed_in = normed_first.astype(jnp.bfloat16)
    normed_all = lax.all_gather(normed_in, "mp", axis=0, tiled=True)
    rows_total = normed_all.shape[0]
    offsets = doc_offsets(lengths[0], rows_total)
    value_pre = dense_product(normed_all, value_proj)
    gate_pre = dense_product(normed_all, gate_proj)

    def mixer_fn(
        value_arg,
        gate_arg,
        taps_arg,
        shift_arg,
        rate_arg,
        rate_offset,
        inlet_arg,
        inlet_offset,
        decay_arg,
    ):
        return recurrent(
            value_arg,
            gate_arg,
            taps_arg,
            shift_arg,
            rate_arg,
            rate_offset,
            inlet_arg,
            inlet_offset,
            decay_arg,
            offsets,
        )

    mixed_float, mixer_back = jax.vjp(
        mixer_fn,
        value_pre,
        gate_pre,
        conv_taps,
        conv_bias,
        rate_weight,
        rate_bias,
        inlet_weight,
        inlet_bias,
        decay_param,
    )
    mixed_act = mixed_float.astype(jnp.bfloat16)
    mixer_part = lax.psum_scatter(
        dense_product(mixed_act, mixer_out), "mp", scatter_dimension=0, tiled=True
    )
    middle = residual + mixer_part
    normed_float, norm_back_mid = jax.vjp(scaled_norm, middle, dense_gain)
    normed_mid = normed_float.astype(jnp.bfloat16)
    normed_mid_all = lax.all_gather(normed_mid, "mp", axis=0, tiled=True)
    gate_linear = dense_product(normed_mid_all, dense_gate)
    value_linear = dense_product(normed_mid_all, dense_value)
    hidden_float, gated_back = jax.vjp(gated_unit, gate_linear, value_linear)
    hidden = hidden_float.astype(jnp.bfloat16)
    dense_part = lax.psum_scatter(
        dense_product(hidden, dense_down), "mp", scatter_dimension=0, tiled=True
    )
    layer_out = (middle + dense_part).astype(jnp.bfloat16)
    weights_live = live_mask.astype(jnp.float32)
    squares = jnp.stack(
        [
            jnp.sum(weights_live * jnp.sum(residual * residual, axis=1)),
            jnp.sum(weights_live * jnp.sum(mixer_part * mixer_part, axis=1)),
            jnp.sum(weights_live * jnp.sum(dense_part * dense_part, axis=1)),
        ]
    )
    live_count = jnp.sum(weights_live)
    stat_pair = lax.psum((squares, live_count), ("dp", "mp"))
    block_rows = lax.all_gather(cotangent, "mp", axis=0, tiled=True)
    hidden_grad = rows_times_cols(block_rows, dense_down)
    down_grad = rows_inner(hidden, block_rows)
    hidden_grad, down_grad = (hidden_grad, down_grad)
    gate_grad_float, value_grad_float = gated_back(hidden_grad)
    gate_grad = gate_grad_float.astype(jnp.bfloat16)
    value_grad = value_grad_float.astype(jnp.bfloat16)
    normed_mid_grad = lax.psum_scatter(
        rows_times_cols(gate_grad, dense_gate) + rows_times_cols(value_grad, dense_value),
        "mp",
        scatter_dimension=0,
        tiled=True,
    )
    dense_gate_grad = rows_inner(normed_mid_all, gate_grad)
    dense_value_grad = rows_inner(normed_mid_all, value_grad)
    middle_norm_grad, dense_gain_grad = norm_back_mid(normed_mid_grad)
    middle_grad = cotangent.astype(jnp.float32) + middle_norm_grad
    middle_low = middle_grad.astype(jnp.bfloat16)
    block_rows = lax.all_gather(middle_low, "mp", axis=0, tiled=True)
    mixed_grad = rows_times_cols(block_rows, mixer_out)
    out_grad = rows_inner(mixed_act, block_rows)
    mixed_grad, mixer_out_grad = (mixed_grad, out_grad)
    (
        value_pre_grad,
        gate_pre_grad,
        taps_grad,
        shift_grad,
        rate_weight_grad,
        rate_bias_grad,
        inlet_weight_grad,
        inlet_bias_grad,
        decay_grad,
    ) = mixer_back(mixed_grad)
    value_low = value_pre_grad.astype(jnp.bfloat16)
    gate_low = gate_pre_grad.astype(jnp.bfloat16)
    normed_in_grad = lax.psum_scatter(
        rows_times_cols(value_low, value_proj) + rows_times_cols(gate_low, gate_proj),
        "mp",
        scatter_dimension=0,
        tiled=True,
    )
    value_proj_grad = rows_inner(normed_all, value_low)
    gate_proj_grad = rows_inner(normed_all, gate_low)
    input_norm_grad, mixer_gain_grad = norm_back_in(normed_in_grad)
    input_grad = (middle_grad + input_norm_grad).astype(jnp.bfloat16)
    (
        value_proj_sum,
        gate_proj_sum,
        mixer_out_sum,
        dense_gate_sum,
        dense_value_sum,
        dense_down_sum,
    ) = (
        lax.psum_scatter(value_proj_grad, "dp", scatter_dimension=0, tiled=True),
        lax.psum_scatter(gate_proj_grad, "dp", scatter_dimension=0, tiled=True),
        lax.psum_scatter(mixer_out_grad, "dp", scatter_dimension=1, tiled=True),
        lax.psum_scatter(dense_gate_grad, "dp", scatter_dimension=0, tiled=True),
        lax.psum_scatter(dense_value_grad, "dp", scatter_dimension=0, tiled=True),
        lax.psum_scatter(down_grad, "dp", scatter_dimension=1, tiled=True),
    )
    (
        taps_sum,
        shift_sum,
        rate_weight_sum,
        rate_bias_sum,
        inlet_weight_sum,
        inlet_bias_sum,
        decay_sum,
    ) = lax.psum(
        (
            taps_grad,
            shift_grad,
            rate_weight_grad,
            rate_bias_grad,
            inlet_weight_grad,
            inlet_bias_grad,
            decay_grad,
        ),
        "dp",
    )
    mixer_gain_sum, dense_gain_sum = lax.psum((mixer_gain_grad, dense_gain_grad), ("dp", "mp"))
    branch_rms = jnp.sqrt(stat_pair[0] / (stat_pair[1] * columns))
    return (
        layer_out,
        input_grad,
        mixer_gain_sum,
        value_proj_sum,
        gate_proj_sum,
        taps_sum,
        shift_sum,
        rate_weight_sum,
        rate_bias_sum,
        inlet_weight_sum,
        inlet_bias_sum,
        decay_sum,
        mixer_out_sum,
        dense_gain_sum,
        dense_gate_sum,
        dense_value_sum,
        dense_down_sum,
        branch_rms,
    )


def solution(mesh):
    return jax.shard_map(
        local,
        mesh=mesh,
        in_specs=(
            P(("dp", "mp"), None),
            P(("dp", "mp"), None),
            P("dp", None),
            P(("dp", "mp")),
            P(),
            P(None, "mp"),
            P(None, "mp"),
            P(None, "mp"),
            P("mp"),
            P("mp", None, None),
            P("mp"),
            P("mp", None, None),
            P("mp"),
            P("mp"),
            P("mp", None),
            P(),
            P(None, "mp"),
            P(None, "mp"),
            P("mp", None),
        ),
        out_specs=(
            P(("dp", "mp"), None),
            P(("dp", "mp"), None),
            P(),
            P("dp", "mp"),
            P("dp", "mp"),
            P(None, "mp"),
            P("mp"),
            P("mp", None, None),
            P("mp"),
            P("mp", None, None),
            P("mp"),
            P("mp"),
            P("mp", "dp"),
            P(),
            P("dp", "mp"),
            P("dp", "mp"),
            P("mp", "dp"),
            P(),
        ),
        check_vma=False,
    )
```

profile of v0, /device:TPU:0, one launch (start us, length us, event | category | flops | bytes accessed | tf_op | source)
XLA Modules:
  0.0 2181.2 jit_solution(17264674080696305526)
XLA Ops:
  13.1 83.1 %all-gather.5.cloned.1.call-done = bf16[1024,2048]{1,0:T(8,128)(2,1)} async-done(((bf16[256,2048]{1,0:T(8,128)(2,1)}), bf16[1024,2048]{1,0:T(8,128)(2,1)}) %all-gather.5.cloned.1.call-update) | async-done | bytes 4194320 | tf_op jit(solution)/shard_map/all_gather | solution.py:124
  384.5 10.0 multiply_convert_fusion.2
  401.4 143.1 %reduce-scatter.11.cloned.1.call-done = f32[256,2048]{1,0:T(8,128)} async-done(((f32[1024,2048]{1,0:T(8,128)}), f32[256,2048]{1,0:T(8,128)}) %reduce-scatter.11.cloned.1.call-update) | async-done | bytes 2097168 | tf_op jit(solution)/shard_map/reduce_scatter | solution.py:167
  550.6 81.0 %all-gather.7.cloned.1.call-done = bf16[1024,2048]{1,0:T(8,128)(2,1)} async-done(((bf16[256,2048]{1,0:T(8,128)(2,1)}), bf16[1024,2048]{1,0:T(8,128)(2,1)}) %all-gather.7.cloned.1.call-update) | async-done | bytes 4194320 | tf_op jit(solution)/shard_map/all_gather | solution.py:173
  631.6 12.7 fusion.106
  644.3 10.5 fusion.107
  654.7 57.6 %all-gather.9.cloned.1.call-done = bf16[1024,2048]{1,0:T(8,128)(2,1)} async-done(((bf16[256,2048]{1,0:T(8,128)(2,1)}), bf16[1024,2048]{1,0:T(8,128)(2,1)}) %all-gather.9.cloned.1.call-update) | async-done | bytes 4194320 | tf_op jit(solution)/shard_map/all_gather | solution.py:192
  712.3 18.0 multiply_convert_fusion
  730.4 11.1 fusion.109
  741.4 11.4 convolution_add_fusion.1
  753.0 143.1 %reduce-scatter.15.cloned.1.call-done = f32[256,2048]{1,0:T(8,128)} async-done(((f32[1024,2048]{1,0:T(8,128)}), f32[256,2048]{1,0:T(8,128)}) %reduce-scatter.15.cloned.1.call-update) | async-done | bytes 2097168 | tf_op jit(solution)/shard_map/reduce_scatter | solution.py:199
  907.7 77.8 %all-gather.11.cloned.1.call-done = bf16[1024,2048]{1,0:T(8,128)(2,1)} async-done(((bf16[256,2048]{1,0:T(8,128)(2,1)}), bf16[1024,2048]{1,0:T(8,128)(2,1)}) %all-gather.11.cloned.1.call-update) | async-done | bytes 4194320 | tf_op jit(solution)/shard_map/all_gather | solution.py:210
  985.5 10.5 fusion.13
  1255.6 9.3 pad.508
  1264.9 9.3 pad.416
  1283.4 10.6 multiply_reduce_fusion
  1321.3 11.1 fusion.65
  1345.5 11.8 fusion.108
  1357.3 12.7 fusion.117
  1370.1 12.7 fusion.118
  1382.9 12.4 fusion.119
  1430.5 26.2 %all-reduce.106 = (f32[4,640]{1,0:T(4,128)}, f32[640]{0:T(1024)}, f32[640]{0:T(1024)}, f32[640]{0:T(1024)}, f32[640]{0:T(1024)}) all-reduce(f32[4,640]{1,0:T(4,128)S(1)} %pad_add_fusion.8, f32[640]{0:T(1024)S(1)} %get-tuple-element.22, f32[640]{0:T(1024)S(1)} %get-tuple-element.51, ...), channel_id=1, replica_groups=mesh['dp'=8,'mp'=4] {'dp'}, use_global_device_ids=true, to_apply=%region_18.19 | all-reduce | flops 5120 | bytes 40960 | tf_op jit(solution)/shard_map/psum | solution.py:260
  1456.7 31.9 %reduce-scatter.17.cloned.1.call-done = f32[256,2048]{1,0:T(8,128)} async-done(((f32[1024,2048]{1,0:T(8,128)}), f32[256,2048]{1,0:T(8,128)}) %reduce-scatter.17.cloned.1.call-update) | async-done | bytes 2097168 | tf_op jit(solution)/shard_map/reduce_scatter | solution.py:227
  1491.2 145.0 %reduce-scatter.13.cloned.1.call-done = f32[256,2048]{1,0:T(8,128)} async-done(((f32[1024,2048]{1,0:T(8,128)}), f32[256,2048]{1,0:T(8,128)}) %reduce-scatter.13.cloned.1.call-update) | async-done | bytes 2097168 | tf_op jit(solution)/shard_map/reduce_scatter | solution.py:178
  1644.5 41.6 %all-reduce.105 = (f32[2048]{0:T(1024)}, f32[2048]{0:T(1024)}, f32[3]{0:T(128)S(1)}, f32[]{:T(128)}) all-reduce(f32[2048]{0:T(1024)S(1)} %get-tuple-element.20, f32[2048]{0:T(1024)S(1)} %copy-done.50, f32[3]{0:T(128)S(1)} %pad_maximum_fusion.9, f32[]{:T(128)} %get-tuple-element.31), channel_id=1, replica_groups=mesh['dp'=8,'mp'=4] {'dp','mp'}, use_global_device_ids=true, to_apply=%region_11.12 | all-reduce | flops 4100 | bytes 32800 | tf_op jit(solution)/shard_map/psum | solution.py:272
  1687.3 46.7 %reduce-scatter.25.cloned.1.call-done = f32[256,1536]{1,0:T(8,128)} async-done(((f32[2048,1536]{1,0:T(8,128)}), f32[256,1536]{1,0:T(8,128)}) %reduce-scatter.25.cloned.1.call-update) | async-done | bytes 1572880 | tf_op jit(solution)/shard_map/reduce_scatter | solution.py:248
  1734.0 96.4 %reduce-scatter.27.cloned.1.call-done = f32[256,1536]{1,0:T(8,128)} async-done(((f32[2048,1536]{1,0:T(8,128)}), f32[256,1536]{1,0:T(8,128)}) %reduce-scatter.27.cloned.1.call-update) | async-done | bytes 1572880 | tf_op jit(solution)/shard_map/reduce_scatter | solution.py:249
  1830.4 96.5 %reduce-scatter.29.cloned.1.call-done = f32[1536,256]{1,0:T(8,128)} async-done(((f32[1536,2048]{1,0:T(8,128)}), f32[1536,256]{1,0:T(8,128)}) %reduce-scatter.29.cloned.1.call-update) | async-done | bytes 1572880 | tf_op jit(solution)/shard_map/reduce_scatter | solution.py:250
  1926.9 62.1 %all-reduce.110.cloned.1.call-done = (f32[4,160,160]{2,1,0:T(8,128)}, f32[4,160,160]{2,1,0:T(8,128)}) async-done(((f32[4,160,160]{2,1,0:T(8,128)}, f32[4,160,160]{2,1,0:T(8,128)}), (f32[4,160,160]{2,1,0:T(8,128)}, f32[4,160,160]{2,1,0:T(8,128)})) %all-reduce.110.cloned.1.call-update) | async-done | bytes 819216 | tf_op jit(solution)/shard_map/psum | solution.py:260
  1989.0 60.1 %reduce-scatter.19.cloned.1.call-done = f32[256,640]{1,0:T(8,128)} async-done(((f32[2048,640]{1,0:T(8,128)}), f32[256,640]{1,0:T(8,128)}) %reduce-scatter.19.cloned.1.call-update) | async-done | bytes 655376 | tf_op jit(solution)/shard_map/reduce_scatter | solution.py:245
  2049.1 60.4 %reduce-scatter.23.cloned.1.call-done = f32[640,256]{1,0:T(8,128)} async-done(((f32[640,2048]{1,0:T(8,128)}), f32[640,256]{1,0:T(8,128)}) %reduce-scatter.23.cloned.1.call-update) | async-done | bytes 655376 | tf_op jit(solution)/shard_map/reduce_scatter | solution.py:247
  2109.5 60.8 %reduce-scatter.21.cloned.1.call-done = f32[256,640]{1,0:T(8,128)} async-done(((f32[2048,640]{1,0:T(8,128)}), f32[256,640]{1,0:T(8,128)}) %reduce-scatter.21.cloned.1.call-update) | async-done | bytes 655376 | tf_op jit(solution)/shard_map/reduce_scatter | solution.py:246
  (518 shorter events, 677.8 us)
Async XLA Ops:
  7.2 377.3 %copy-start = (bf16[2048,640]{1,0:T(8,128)(2,1)S(1)}, bf16[2048,640]{1,0:T(8,128)(2,1)}, u32[]{:S(2)}) copy-start(bf16[2048,640]{1,0:T(8,128)(2,1)} %param.25) | copy-start | bytes 7864324
  7.2 89.0 %all-gather.5.cloned.1.call-start = ((), (), s32[]{:S(2)}) async-start(), calls=%async_computation.10 | async-start | bytes 5242880 | tf_op jit(solution)/shard_map/all_gather | solution.py:124
  12.6 531.9 %reduce-scatter.11.cloned.1.call-start = ((), (), s32[]{:S(2)}) async-start(), calls=%async_computation.11 | async-start | bytes 10485760 | tf_op jit(solution)/shard_map/reduce_scatter | solution.py:167
  12.9 89.3 %copy-start.42 = (f32[640]{0:T(1024)}, f32[640]{0:T(1024)S(1)}, u32[]{:S(2)}) copy-start(f32[640]{0:T(1024)S(1)} %get-tuple-element.27) | copy-start | bytes 7684
  12.9 89.3 %copy-start.44 = (f32[640]{0:T(1024)}, f32[640]{0:T(1024)S(1)}, u32[]{:S(2)}) copy-start(f32[640]{0:T(1024)S(1)} %get-tuple-element.28) | copy-start | bytes 7684
  12.9 89.3 %copy-start.46 = (f32[640]{0:T(1024)}, f32[640]{0:T(1024)S(1)}, u32[]{:S(2)}) copy-start(f32[640]{0:T(1024)S(1)} %get-tuple-element.29) | copy-start | bytes 7684
  12.9 89.3 %copy-start.48 = (f32[640]{0:T(1024)}, f32[640]{0:T(1024)S(1)}, u32[]{:S(2)}) copy-start(f32[640]{0:T(1024)S(1)} %get-tuple-element.30) | copy-start | bytes 7684
  13.0 115.7 %copy-start.31 = (f32[640]{0:T(1024)}, f32[640]{0:T(1024)S(1)}, u32[]{:S(2)}) copy-start(f32[640]{0:T(1024)S(1)} %broadcast_multiply_fusion) | copy-start | bytes 7684
  13.1 89.2 %copy-start.56 = (pred[1024]{0:T(1024)(128)(4,1)}, pred[1024]{0:T(1024)(128)(4,1)S(1)}, u32[]{:S(2)}) copy-start(pred[1024]{0:T(1024)(128)(4,1)S(1)} %get-tuple-element.174) | copy-start | bytes 3076
  13.1 115.6 %copy-start.75 = (pred[1024]{0:T(1024)(128)(4,1)}, pred[1024]{0:T(1024)(128)(4,1)S(1)}, u32[]{:S(2)}) copy-start(pred[1024]{0:T(1024)(128)(4,1)S(1)} %get-tuple-element.170) | copy-start | bytes 3076
  13.1 90.6 %copy-start.80 = (f32[640]{0:T(1024)S(1)}, f32[640]{0:T(1024)}, u32[]{:S(2)}) copy-start(f32[640]{0:T(1024)} %param.27) | copy-start | bytes 7684
  401.3 147.4 %copy-start.29 = (f32[2048]{0:T(1024)S(1)}, f32[2048]{0:T(1024)}, u32[]{:S(2)}) copy-start(f32[2048]{0:T(1024)} %param.34) | copy-start | bytes 24580
  401.3 230.2 %all-gather.7.cloned.1.call-start = ((), (), s32[]{:S(2)}) async-start(), calls=%async_computation.12 | async-start | bytes 5242880 | tf_op jit(solution)/shard_map/all_gather | solution.py:173
  547.9 352.4 %copy-start.52 = (f32[256]{0:T(256)}, f32[256]{0:T(256)S(1)}, u32[]{:S(2)}) copy-start(f32[256]{0:T(256)S(1)} %fusion.54) | copy-start | bytes 3076
  549.9 162.4 %all-gather.9.cloned.1.call-start = ((), (), s32[]{:S(2)}) async-start(), calls=%async_computation.14 | async-start | bytes 5242880 | tf_op jit(solution)/shard_map/all_gather | solution.py:192
  550.5 345.6 %reduce-scatter.15.cloned.1.call-start = ((), (), s32[]{:S(2)}) async-start(), calls=%async_computation.15 | async-start | bytes 10485760 | tf_op jit(solution)/shard_map/reduce_scatter | solution.py:199
  752.9 232.6 %all-gather.11.cloned.1.call-start = ((), (), s32[]{:S(2)}) async-start(), calls=%async_computation.16 | async-start | bytes 5242880 | tf_op jit(solution)/shard_map/all_gather | solution.py:210
  903.9 584.7 %reduce-scatter.17.cloned.1.call-start = ((), (), s32[]{:S(2)}) async-start(), calls=%async_computation.17 | async-start | bytes 10485760 | tf_op jit(solution)/shard_map/reduce_scatter | solution.py:227
  1345.4 290.8 %reduce-scatter.13.cloned.1.call-start = ((), (), s32[]{:S(2)}) async-start(), calls=%async_computation.13 | async-start | bytes 10485760 | tf_op jit(solution)/shard_map/reduce_scatter | solution.py:178
  1357.3 376.8 %reduce-scatter.25.cloned.1.call-start = ((), (), s32[]{:S(2)}) async-start(), calls=%async_computation.21 | async-start | bytes 14155776 | tf_op jit(solution)/shard_map/reduce_scatter | solution.py:248
  1370.1 460.3 %reduce-scatter.27.cloned.1.call-start = ((), (), s32[]{:S(2)}) async-start(), calls=%async_computation.22 | async-start | bytes 14155776 | tf_op jit(solution)/shard_map/reduce_scatter | solution.py:249
  1382.8 544.1 %reduce-scatter.29.cloned.1.call-start = ((), (), s32[]{:S(2)}) async-start(), calls=%async_computation.23 | async-start | bytes 14155776 | tf_op jit(solution)/shard_map/reduce_scatter | solution.py:250
  1395.3 593.7 %all-reduce.110.cloned.1.call-start = ((), (), s32[]{:S(2)}) async-start(), calls=%async_computation.24 | async-start | bytes 2621440 | tf_op jit(solution)/shard_map/psum | solution.py:260
  1405.1 644.0 %reduce-scatter.19.cloned.1.call-start = ((), (), s32[]{:S(2)}) async-start(), calls=%async_computation.18 | async-start | bytes 5898240 | tf_op jit(solution)/shard_map/reduce_scatter | solution.py:245
  1413.5 696.0 %reduce-scatter.23.cloned.1.call-start = ((), (), s32[]{:S(2)}) async-start(), calls=%async_computation.20 | async-start | bytes 5898240 | tf_op jit(solution)/shard_map/reduce_scatter | solution.py:247
  1421.7 748.6 %reduce-scatter.21.cloned.1.call-start = ((), (), s32[]{:S(2)}) async-start(), calls=%async_computation.19 | async-start | bytes 5898240 | tf_op jit(solution)/shard_map/reduce_scatter | solution.py:246
  1430.4 205.8 %copy-start.30 = (f32[2048]{0:T(1024)S(1)}, f32[2048]{0:T(1024)}, u32[]{:S(2)}) copy-start(f32[2048]{0:T(1024)} %param.34) | copy-start | bytes 24580
  1430.4 205.8 %copy-start.53 = (f32[256]{0:T(256)S(1)}, f32[256]{0:T(256)}, u32[]{:S(2)}) copy-start(f32[256]{0:T(256)} %copy-done.52) | copy-start | bytes 3076
  1430.4 205.8 %copy-start.78 = (f32[256]{0:T(256)S(1)}, f32[256]{0:T(256)}, u32[]{:S(2)}) copy-start(f32[256]{0:T(256)} %copy-done.77) | copy-start | bytes 3076
  1491.2 150.8 %copy-start.84 = (f32[256]{0:T(256)S(1)}, f32[256]{0:T(256)}, u32[]{:S(2)}) copy-start(f32[256]{0:T(256)} %get-tuple-element.91) | copy-start | bytes 3076
  1491.2 150.8 %copy-start.85 = (s32[256]{0:T(256)S(1)}, s32[256]{0:T(256)}, u32[]{:S(2)}) copy-start(s32[256]{0:T(256)} %param.22) | copy-start | bytes 3076
  1491.2 153.3 %copy-start.50 = (f32[2048]{0:T(1024)S(1)}, f32[2048]{0:T(1024)}, u32[]{:S(2)}) copy-start(f32[2048]{0:T(1024)} %get-tuple-element.18) | copy-start | bytes 24580
  (83 other events, 1102.6 us)
Sparse Core Ops, SparseCore 0:
  12.7 83.4 all-gather.4
  401.5 142.9 reduce-scatter.10
  550.1 81.4 all-gather.6
  633.0 79.2 all-gather.8
  753.0 143.0 reduce-scatter.14
  904.0 81.4 all-gather.10
  1345.5 143.0 reduce-scatter.16
  1491.0 145.1 reduce-scatter.12
  1640.3 93.7 reduce-scatter.24
  1738.0 92.3 reduce-scatter.26
  1834.5 92.3 reduce-scatter.28
  1931.1 57.8 all-reduce.109
  1993.3 55.7 reduce-scatter.18
  2052.9 56.5 reduce-scatter.22
  2113.7 56.5 reduce-scatter.20
where the time goes:
time: 2200 us; the launch traced here: 2180 us
  waiting for transfers between devices  1250 us (57%)
  local copies, waits for them, and re-layouts  455 us (21%)
  matrix products  212 us (10%)
  other arithmetic  182 us (8%)
  blocking collectives  67.8 us (3%)
    pad x79, local copies, waits for them, and re-layouts, recurrent(): lax.associative_scan(combine, (carried, normalizer * input_gate * convolv...  232 us
    slice x78, local copies, waits for them, and re-layouts, recurrent(): lax.associative_scan(combine, (carried, normalizer * input_gate * convolv...  182 us
    reduce_scatter x1, waiting for transfers between devices, local(): lax.psum_scatter(dense_product(hidden, dense_down), 'mp', scatter_dimensi...  145 us
    reduce_scatter x1, waiting for transfers between devices, local(): lax.psum_scatter(rows_times_cols(gate_grad, dense_gate) + rows_times_cols...  143 us
    reduce_scatter x1, waiting for transfers between devices, local(): lax.psum_scatter(dense_product(mixed_act, mixer_out), 'mp', scatter_dimen...  143 us
    reduce_scatter x1, waiting for transfers between devices, local(): lax.psum_scatter(down_grad, 'dp', scatter_dimension=1, tiled=True)  96.5 us
    reduce_scatter x1, waiting for transfers between devices, local(): lax.psum_scatter(dense_value_grad, 'dp', scatter_dimension=0, tiled=True)  96.4 us
    all_gather x1, waiting for transfers between devices, local(): normed_all = lax.all_gather(normed_in, 'mp', axis=0, tiled=True)  83.1 us
  transfers between devices with their start and end apart: 15, of which 15 were waited for; matrix products, arithmetic and copies ran while one was open for 6% of the time, Pallas kernels for 0%

commit v1 on v0

v1 whole, which is shorter than its diff:
```python
import functools

import jax
import jax.numpy as jnp
from jax import lax
from jax.experimental import pallas as pl
from jax.experimental.pallas import tpu as pltpu
from jax.sharding import PartitionSpec as P

EPS = 1e-06
BF = jnp.bfloat16
F32 = jnp.float32
GELU_C = 0.7978845608028654
GELU_A = 0.044715
CHUNK = 16
VMEM_LIMIT = 60 * 1024 * 1024


def doc_offsets(lengths_row, rows_total):
    doc_ends = jnp.cumsum(lengths_row)
    positions = jnp.arange(rows_total, dtype=jnp.int32)
    before = (doc_ends[None, :] <= positions[:, None]).astype(jnp.int32)
    starts = jnp.sum(before * lengths_row[None, :], axis=1)
    return positions - starts


def scaled_norm(values, gain_vec):
    return (
        values
        * lax.rsqrt(jnp.mean(values * values, axis=1, keepdims=True) + EPS)
        * gain_vec[None, :]
    )


def dot_nn(left, right):
    return jnp.dot(left, right, preferred_element_type=F32)


def dot_nt(left, right):
    return lax.dot_general(left, right, (((1,), (1,)), ((), ())), preferred_element_type=F32)


def dot_tn(left, right):
    return lax.dot_general(left, right, (((0,), (0,)), ((), ())), preferred_element_type=F32)


def gelu(x):
    return 0.5 * x * (1.0 + jnp.tanh(GELU_C * (x + GELU_A * x * x * x)))


def gelu_both(x):
    square = x * x
    tanh_in = jnp.tanh(GELU_C * x * (1.0 + GELU_A * square))
    half = 0.5 * (1.0 + tanh_in)
    slope = half + 0.5 * x * (1.0 - tanh_in * tanh_in) * (GELU_C * (1.0 + 3.0 * GELU_A * square))
    return half * x, slope


def sigmoid(x):
    return 1.0 / (1.0 + jnp.exp(-x))


def one_minus_square(log_decay, carried):
    y = 2.0 * log_decay
    series = 1.0 + y * (1.0 / 7.0)
    for k in (6.0, 5.0, 4.0, 3.0, 2.0):
        series = 1.0 + y * (1.0 / k) * series
    return jnp.where(y > -0.5, -y * series, 1.0 - carried * carried)


def row_in_tile(shape):
    return lax.broadcasted_iota(jnp.int32, shape, 0) % 8


def scan_tile_down(mult, add):
    row = row_in_tile(mult.shape)
    for step in (1, 2, 4):
        keep = row >= step
        add_up = jnp.where(keep, pltpu.roll(add, step, 0), 0.0)
        mult_up = jnp.where(keep, pltpu.roll(mult, step, 0), 1.0)
        add = add + mult * add_up
        mult = mult * mult_up
    return mult, add


def scan_tile_up(mult, add):
    row = row_in_tile(mult.shape)
    for step in (1, 2, 4):
        keep = row < 8 - step
        add_dn = jnp.where(keep, pltpu.roll(add, 8 - step, 0), 0.0)
        mult_dn = jnp.where(keep, pltpu.roll(mult, 8 - step, 0), 1.0)
        add = add + mult * add_dn
        mult = mult * mult_dn
    return mult, add


V_BIAS, V_RATE, V_INLET, V_DECAY = 4, 5, 6, 7


def rec_forward(rows, vp_ref, gp_ref, mask_ref, vec_ref, rate_ref, inlet_ref,
                mixed_ref, state_ref, conv_ref, forget_ref, input_ref, low_ref):
    bias = vec_ref[V_BIAS:V_BIAS + 1, :]

    def conv_step(index, unused):
        base = pl.multiple_of(index * CHUNK, CHUNK)
        ext = vp_ref[pl.ds(base, CHUNK + 8), :]
        masks = mask_ref[pl.ds(base, CHUNK), :]
        total = bias + vec_ref[0:1, :] * ext[8:8 + CHUNK, :]
        for tap in (1, 2, 3):
            total = total + (masks[:, tap:tap + 1] * ext[8 - tap:8 - tap + CHUNK, :]) * vec_ref[tap:tap + 1, :]
        conv_ref[pl.ds(base, CHUNK), :] = total
        low_ref[pl.ds(base, CHUNK), :] = total.astype(BF)
        return unused

    lax.fori_loop(0, rows // CHUNK, conv_step, 0)
    block = 256

    def gate_step(index, unused):
        base = pl.multiple_of(index * block, block)
        low = low_ref[pl.ds(base, block), :]
        forget_ref[pl.ds(base, block), :] = dot_nn(low, rate_ref[...])
        input_ref[pl.ds(base, block), :] = dot_nn(low, inlet_ref[...])
        return unused

    lax.fori_loop(0, rows // block, gate_step, 0)
    rate_bias = vec_ref[V_RATE:V_RATE + 1, :]
    inlet_bias = vec_ref[V_INLET:V_INLET + 1, :]
    decay = vec_ref[V_DECAY:V_DECAY + 1, :]

    def scan_step(index, carry):
        base = pl.multiple_of(index * CHUNK, CHUNK)
        window = pl.ds(base, CHUNK)
        forget = sigmoid(forget_ref[window, :] + rate_bias)
        inlet = sigmoid(input_ref[window, :] + inlet_bias)
        log_decay = decay * forget
        carried = jnp.exp(log_decay)
        normalizer = jnp.sqrt(one_minus_square(log_decay, carried))
        forget_ref[window, :] = forget
        input_ref[window, :] = inlet
        add = normalizer * inlet * conv_ref[window, :]
        mult = carried * mask_ref[window, 1:2]
        pieces = []
        for tile in range(CHUNK // 8):
            m, a = scan_tile_down(mult[8 * tile:8 * tile + 8], add[8 * tile:8 * tile + 8])
            states = a + m * carry
            carry = states[7:8, :]
            pieces.append(states)
        states = jnp.concatenate(pieces, axis=0)
        state_ref[window, :] = states
        mixed_ref[window, :] = (states * gelu(gp_ref[window, :])).astype(BF)
        return carry

    lax.fori_loop(0, rows // CHUNK, scan_step, jnp.zeros((1, conv_ref.shape[1]), F32))


def rec_backward(rows, dm_ref, vp_ref, gp_ref, mask_ref, vec_ref, rate_ref, inlet_ref,
                 state_ref, conv_ref, forget_ref, input_ref,
                 vlow_ref, glow_ref, dzf_ref, dzi_ref, dconv_ref, clow_ref, sums_ref):
    columns = conv_ref.shape[1]
    decay = vec_ref[V_DECAY:V_DECAY + 1, :]
    chunks = rows // CHUNK
    zero_row = jnp.zeros((1, columns), F32)

    def scan_step(step, carry):
        grad_next, mult_next, rate_sum, inlet_sum, decay_sum = carry
        base = pl.multiple_of((chunks - 1 - step) * CHUNK, CHUNK)
        window = pl.ds(base, CHUNK)
        mixed_grad = dm_ref[window, :]
        act, slope = gelu_both(gp_ref[window, :])
        ext = state_ref[pl.ds(base, CHUNK + 8), :]
        states = ext[8:, :]
        before = ext[7:7 + CHUNK, :]
        glow_ref[window, :] = (mixed_grad * states * slope).astype(BF)
        add = mixed_grad * act
        forget = forget_ref[window, :]
        inlet = input_ref[window, :]
        conv = conv_ref[window, :]
        clow_ref[window, :] = conv.astype(BF)
        log_decay = decay * forget
        carried = jnp.exp(log_decay)
        square = one_minus_square(log_decay, carried)
        inverse = lax.rsqrt(jnp.maximum(square, 1e-30))
        normalizer = square * inverse
        mult = carried * mask_ref[window, 1:2]
        pieces = []
        for tile in reversed(range(CHUNK // 8)):
            lo = 8 * tile
            after = mult[lo + 8:lo + 9, :] if lo + 8 < CHUNK else mult_next
            shifted = jnp.concatenate([mult[lo + 1:lo + 8, :], after], axis=0)
            m, a = scan_tile_up(shifted, add[lo:lo + 8])
            grads = a + m * grad_next
            grad_next = grads[0:1, :]
            pieces.append(grads)
        grads = jnp.concatenate(pieces[::-1], axis=0)
        gated = grads * inlet
        d_log = grads * before * mult - gated * conv * ((1.0 - square) * inverse)
        d_forget = d_log * decay
        dzf = d_forget * forget * (1.0 - forget)
        dzi = grads * normalizer * conv * inlet * (1.0 - inlet)
        dzf_ref[window, :] = dzf.astype(BF)
        dzi_ref[window, :] = dzi.astype(BF)
        dconv_ref[window, :] = gated * normalizer
        return (grad_next, mult[0:1, :],
                rate_sum + jnp.sum(dzf.reshape(CHUNK // 8, 8, columns), axis=0),
                inlet_sum + jnp.sum(dzi.reshape(CHUNK // 8, 8, columns), axis=0),
                decay_sum + jnp.sum((d_log * forget).reshape(CHUNK // 8, 8, columns), axis=0))

    zeros = jnp.zeros((8, columns), F32)
    unused, unused, rate_sum, inlet_sum, decay_sum = lax.fori_loop(
        0, chunks, scan_step, (zero_row, zero_row, zeros, zeros, zeros))
    sums_ref[V_RATE:V_RATE + 1, :] = jnp.sum(rate_sum, axis=0, keepdims=True)
    sums_ref[V_INLET:V_INLET + 1, :] = jnp.sum(inlet_sum, axis=0, keepdims=True)
    sums_ref[V_DECAY:V_DECAY + 1, :] = jnp.sum(decay_sum, axis=0, keepdims=True)
    block = 256

    def gate_step(index, unused):
        base = pl.multiple_of(index * block, block)
        window = pl.ds(base, block)
        dconv_ref[window, :] += (dot_nt(dzf_ref[window, :], rate_ref[...])
                                 + dot_nt(dzi_ref[window, :], inlet_ref[...]))
        return unused

    lax.fori_loop(0, rows // block, gate_step, 0)

    def conv_step(index, carry):
        base = pl.multiple_of(index * CHUNK, CHUNK)
        window = pl.ds(base, CHUNK)
        ext = dconv_ref[pl.ds(base, CHUNK + 8), :]
        masks = mask_ref[pl.ds(base, CHUNK + 8), :]
        values = vp_ref[pl.ds(base, CHUNK + 8), :]
        here = ext[:CHUNK, :]
        total = vec_ref[0:1, :] * here
        sums = [carry[0] + fold(here * values[8:, :], columns)]
        for tap in (1, 2, 3):
            gated = ext * masks[:, tap:tap + 1]
            total = total + vec_ref[tap:tap + 1, :] * gated[tap:tap + CHUNK, :]
            sums.append(carry[tap] + fold(gated[:CHUNK, :] * values[8 - tap:8 - tap + CHUNK, :], columns))
        sums.append(carry[4] + fold(here, columns))
        vlow_ref[window, :] = total.astype(BF)
        return tuple(sums)

    sums = lax.fori_loop(0, chunks, conv_step, (zeros,) * 5)
    for row in range(5):
        sums_ref[row:row + 1, :] = jnp.sum(sums[row], axis=0, keepdims=True)


def fold(values, columns):
    return jnp.sum(values.reshape(CHUNK // 8, 8, columns), axis=0)


def forward_kernel(vp_in, gp_ref, mask_ref, vec_ref, rate_ref, inlet_ref,
                   mixed_ref, state_ref, conv_ref, forget_ref, input_ref, vp_ref, low_ref):
    rows, columns = vp_in.shape
    vp_ref[0:8, :] = jnp.zeros((8, columns), F32)
    vp_ref[8:, :] = vp_in[...]
    rec_forward(rows, vp_ref, gp_ref, mask_ref, vec_ref, rate_ref, inlet_ref,
                mixed_ref, state_ref, conv_ref, forget_ref, input_ref, low_ref)


def backward_kernel(dm_ref, vp_in, gp_ref, mask_ref, vec_ref, rate_ref, inlet_ref,
                    state_in, conv_ref, forget_ref, input_ref,
                    vlow_ref, glow_ref, rate_grad_ref, inlet_grad_ref, sums_ref,
                    vp_ref, state_ref, dzf_ref, dzi_ref, dconv_ref, clow_ref):
    rows, columns = vp_in.shape
    zeros = jnp.zeros((8, columns), F32)
    vp_ref[0:8, :] = zeros
    vp_ref[8:, :] = vp_in[...]
    state_ref[0:8, :] = zeros
    state_ref[8:, :] = state_in[...]
    dconv_ref[rows:rows + 8, :] = zeros
    rec_backward(rows, dm_ref, vp_ref, gp_ref, mask_ref, vec_ref, rate_ref, inlet_ref,
                 state_ref, conv_ref, forget_ref, input_ref,
                 vlow_ref, glow_ref, dzf_ref, dzi_ref, dconv_ref, clow_ref, sums_ref)
    rate_grad_ref[...] = dot_tn(clow_ref[...], dzf_ref[...])
    inlet_grad_ref[...] = dot_tn(clow_ref[...], dzi_ref[...])


def call_forward(vp, gp, masks, vec, rate, inlet):
    rows, columns = vp.shape
    wide = jax.ShapeDtypeStruct((rows, columns), F32)
    return pl.pallas_call(
        forward_kernel,
        out_shape=(jax.ShapeDtypeStruct((rows, columns), BF), wide, wide, wide, wide),
        scratch_shapes=[pltpu.VMEM((rows + 8, columns), F32), pltpu.VMEM((rows, columns), BF)],
        compiler_params=pltpu.CompilerParams(vmem_limit_bytes=VMEM_LIMIT),
        cost_estimate=pl.CostEstimate(flops=4 * rows * columns * columns,
                                      bytes_accessed=30 * rows * columns, transcendentals=6 * rows * columns),
    )(vp, gp, masks, vec, rate, inlet)


def call_backward(dm, vp, gp, masks, vec, rate, inlet, state, conv, forget, inp):
    rows, columns = vp.shape
    low = jax.ShapeDtypeStruct((rows, columns), BF)
    square = jax.ShapeDtypeStruct((columns, columns), F32)
    return pl.pallas_call(
        backward_kernel,
        out_shape=(low, low, square, square, jax.ShapeDtypeStruct((8, columns), F32)),
        scratch_shapes=[
            pltpu.VMEM((rows + 8, columns), F32),
            pltpu.VMEM((rows + 8, columns), F32),
            pltpu.VMEM((rows, columns), BF),
            pltpu.VMEM((rows, columns), BF),
            pltpu.VMEM((rows + 8, columns), F32),
            pltpu.VMEM((rows, columns), BF),
        ],
        compiler_params=pltpu.CompilerParams(vmem_limit_bytes=VMEM_LIMIT),
        cost_estimate=pl.CostEstimate(flops=8 * rows * columns * columns,
                                      bytes_accessed=40 * rows * columns, transcendentals=4 * rows * columns),
    )(dm, vp, gp, masks, vec, rate, inlet, state, conv, forget, inp)


def block_diagonal(heads):
    count, width, unused = heads.shape
    spread = heads[:, :, None, :] * jnp.eye(count, dtype=heads.dtype)[:, None, :, None]
    return spread.reshape(count * width, count * width)


def diagonal_blocks(square, count):
    width = square.shape[0] // count
    return jnp.stack([square[h * width:(h + 1) * width, h * width:(h + 1) * width] for h in range(count)])


def scatter_mp(values):
    return lax.psum_scatter(values.astype(BF), "mp", scatter_dimension=0, tiled=True).astype(F32)


def scatter_dp(values, dimension):
    return lax.psum_scatter(values.astype(BF), "dp", scatter_dimension=dimension, tiled=True).astype(F32)


def gated_unit(gate_linear, value_linear):
    return gelu(gate_linear) * value_linear


def local(tokens, cotangent, lengths, live_mask, mixer_gain, value_proj, gate_proj, conv_taps, conv_bias,
          rate_weight, rate_bias, inlet_weight, inlet_bias, decay_param, mixer_out, dense_gain,
          dense_gate, dense_value, dense_down):
    residual = tokens.astype(F32)
    columns = residual.shape[1]
    head_count = rate_weight.shape[0]
    normed_first, norm_back_in = jax.vjp(scaled_norm, residual, mixer_gain)
    normed_all = lax.all_gather(normed_first.astype(BF), "mp", axis=0, tiled=True)
    rows_total = normed_all.shape[0]
    offsets = doc_offsets(lengths[0], rows_total)
    taps_here = jnp.arange(8, dtype=jnp.int32)
    masks = (offsets[:, None] >= taps_here[None, :]).astype(F32)
    masks_ext = jnp.concatenate([masks, jnp.zeros((8, 8), F32)], axis=0)
    vec = jnp.concatenate([
        conv_taps,
        jnp.stack([conv_bias, rate_bias, inlet_bias, -8.0 * jax.nn.softplus(-decay_param)]),
    ], axis=0)
    rate_square = block_diagonal(rate_weight).astype(BF)
    inlet_square = block_diagonal(inlet_weight).astype(BF)
    value_pre = dot_nn(normed_all, value_proj)
    gate_pre = dot_nn(normed_all, gate_proj)
    mixed_act, states, convolved, forget_gate, input_gate = call_forward(
        value_pre, gate_pre, masks_ext, vec, rate_square, inlet_square)
    mixer_part = scatter_mp(dot_nn(mixed_act, mixer_out))
    middle = residual + mixer_part
    normed_float, norm_back_mid = jax.vjp(scaled_norm, middle, dense_gain)
    normed_mid_all = lax.all_gather(normed_float.astype(BF), "mp", axis=0, tiled=True)
    gate_linear = dot_nn(normed_mid_all, dense_gate)
    value_linear = dot_nn(normed_mid_all, dense_value)
    hidden_float, gated_back = jax.vjp(gated_unit, gate_linear, value_linear)
    hidden = hidden_float.astype(BF)
    dense_part = scatter_mp(dot_nn(hidden, dense_down))
    layer_out = (middle + dense_part).astype(BF)
    weights_live = live_mask.astype(F32)
    squares = jnp.stack([
        jnp.sum(weights_live * jnp.sum(residual * residual, axis=1)),
        jnp.sum(weights_live * jnp.sum(mixer_part * mixer_part, axis=1)),
        jnp.sum(weights_live * jnp.sum(dense_part * dense_part, axis=1)),
    ])
    live_count = jnp.sum(weights_live)
    block_rows = lax.all_gather(cotangent, "mp", axis=0, tiled=True)
    hidden_grad = dot_nt(block_rows, dense_down)
    down_grad = dot_tn(hidden, block_rows)
    gate_grad_float, value_grad_float = gated_back(hidden_grad)
    gate_grad = gate_grad_float.astype(BF)
    value_grad = value_grad_float.astype(BF)
    normed_mid_grad = scatter_mp(dot_nt(gate_grad, dense_gate) + dot_nt(value_grad, dense_value))
    dense_gate_grad = dot_tn(normed_mid_all, gate_grad)
    dense_value_grad = dot_tn(normed_mid_all, value_grad)
    middle_norm_grad, dense_gain_grad = norm_back_mid(normed_mid_grad)
    middle_grad = cotangent.astype(F32) + middle_norm_grad
    middle_low = middle_grad.astype(BF)
    middle_rows = lax.all_gather(middle_low, "mp", axis=0, tiled=True)
    mixed_grad = dot_nt(middle_rows, mixer_out)
    mixer_out_grad = dot_tn(mixed_act, middle_rows)
    value_low, gate_low, rate_sq, inlet_sq, vec_grad = call_backward(
        mixed_grad, value_pre, gate_pre, masks_ext, vec, rate_square, inlet_square,
        states, convolved, forget_gate, input_gate)
    normed_in_grad = scatter_mp(dot_nt(value_low, value_proj) + dot_nt(gate_low, gate_proj))
    value_proj_grad = dot_tn(normed_all, value_low)
    gate_proj_grad = dot_tn(normed_all, gate_low)
    input_norm_grad, mixer_gain_grad = norm_back_in(normed_in_grad)
    input_grad = (middle_grad + input_norm_grad).astype(BF)
    small = (vec_grad, diagonal_blocks(rate_sq, head_count), diagonal_blocks(inlet_sq, head_count))
    vec_sum, rate_sum, inlet_sum = lax.psum(small, "dp")
    decay_scale = 8.0 * jax.nn.sigmoid(-decay_param)
    mixer_gain_sum, dense_gain_sum, squares, live_count = lax.psum(
        (mixer_gain_grad, dense_gain_grad, squares, live_count), ("dp", "mp"))
    branch_rms = jnp.sqrt(squares / (live_count * columns))
    return (
        layer_out,
        input_grad,
        mixer_gain_sum,
        scatter_dp(value_proj_grad, 0),
        scatter_dp(gate_proj_grad, 0),
        vec_sum[0:4],
        vec_sum[4],
        rate_sum,
        vec_sum[V_RATE],
        inlet_sum,
        vec_sum[V_INLET],
        vec_sum[V_DECAY] * decay_scale,
        scatter_dp(mixer_out_grad, 1),
        dense_gain_sum,
        scatter_dp(dense_gate_grad, 0),
        scatter_dp(dense_value_grad, 0),
        scatter_dp(down_grad, 1),
        branch_rms,
    )


def solution(mesh):
    rows = P(("dp", "mp"), None)
    return jax.shard_map(
        local,
        mesh=mesh,
        in_specs=(
            rows, rows, P("dp", None), P(("dp", "mp")), P(),
            P(None, "mp"), P(None, "mp"), P(None, "mp"), P("mp"),
            P("mp", None, None), P("mp"), P("mp", None, None), P("mp"), P("mp"),
            P("mp", None), P(), P(None, "mp"), P(None, "mp"), P("mp", None),
        ),
        out_specs=(
            rows, rows, P(), P("dp", "mp"), P("dp", "mp"),
            P(None, "mp"), P("mp"), P("mp", None, None), P("mp"), P("mp", None, None), P("mp"), P("mp"),
            P("mp", "dp"), P(), P("dp", "mp"), P("dp", "mp"), P("mp", "dp"), P(),
        ),
        check_vma=False,
    )
```

time: 2200 us -> 1170 us (0.53)
  waiting for transfers between devices: 1250 us -> 786 us
  local copies, waits for them, and re-layouts: 455 us -> 14.4 us
  other arithmetic: 182 us -> 47.2 us
  Pallas kernels: 0 us -> 57.1 us
  matrix products: 212 us -> 170 us
    reduce_scatter x10, waiting for transfers between devices: 884 us -> 516 us  [the longest x4 305 us: scatter_mp(): lax.psum_scatter(values.astype(BF), 'mp', scatter_dimension=0, tiled=True)]
    pad x79 -> x0, local copies, waits for them, and re-layouts: 232 us -> none  [recurrent(): lax.associative_scan(combine, (carried, normalizer * input_gate * convolv...]
    slice x79 -> x2, local copies, waits for them, and re-layouts: 182 us -> 1.23 us  [the longest x1 0.62 us: local(): vec_sum[V_DECAY] * decay_scale]
    pallas_call x0 -> x2, Pallas kernels: none -> 57.1 us  [the longest x1 32.3 us: call_backward(): pl.pallas_call(backward_kernel, out_shape=(low, low, square, square, jax....]
    psum x1, waiting for transfers between devices: 62.1 us -> 12.2 us  [local(): vec_sum, rate_sum, inlet_sum = lax.psum(small, 'dp')]
    all_gather x3, waiting for transfers between devices: 242 us -> 199 us  [the longest x1 80.6 us: local(): lax.all_gather(normed_float.astype(BF), 'mp', axis=0, tiled=True)]
    dot_general x24 -> x18, matrix products: 212 us -> 170 us  [the longest x6 59.5 us: dot_nt(): lax.dot_general(left, right, (((1,), (1,)), ((), ())), preferred_element_...]
    reduce_sum x4 -> x0, other arithmetic: 32.4 us -> none  [the longest x1 11.1 us: recurrent(): convolved = jnp.zeros_like(value_pre) + conv_bias[None, :]]
  transfers between devices with their start and end apart: 15 -> 15, of which waited for: 15 -> 14; matrix products, arithmetic and copies ran while one was open for 6% -> 13% of each run, Pallas kernels for 0% -> 3%
where the time goes in v1:
time: 1170 us; the launch traced here: 1160 us
  waiting for transfers between devices  786 us (67%)
  matrix products  170 us (15%)
  blocking collectives  64.9 us (6%)
  Pallas kernels  57.1 us (5%)
  other arithmetic  47.2 us (4%)
  between operations  15.5 us (1%)
  local copies, waits for them, and re-layouts  14.4 us (1%)
    reduce_scatter x4, waiting for transfers between devices, scatter_mp(): lax.psum_scatter(values.astype(BF), 'mp', scatter_dimension=0, tiled=True)  305 us
    reduce_scatter x6, waiting for transfers between devices, scatter_dp(): lax.psum_scatter(values.astype(BF), 'dp', scatter_dimension=dimension, ti...  211 us
    all_gather x1, waiting for transfers between devices, local(): lax.all_gather(normed_float.astype(BF), 'mp', axis=0, tiled=True)  80.6 us
    all_gather x1, waiting for transfers between devices, local(): lax.all_gather(normed_first.astype(BF), 'mp', axis=0, tiled=True)  72.3 us
    dot_general x6, matrix products, dot_nt(): lax.dot_general(left, right, (((1,), (1,)), ((), ())), preferred_element_...  59.5 us
    all_gather x1, waiting for transfers between devices, local(): block_rows = lax.all_gather(cotangent, 'mp', axis=0, tiled=True)  57.9 us
    dot_general x6, matrix products, dot_tn(): lax.dot_general(left, right, (((0,), (0,)), ((), ())), preferred_element_...  56.7 us
    dot_general x6, matrix products, dot_nn(): return jnp.dot(left, right, preferred_element_type=F32)  54 us
  transfers between devices with their start and end apart: 15, of which 14 were waited for; matrix products, arithmetic and copies ran while one was open for 13% of the time, Pallas kernels for 3%

profile of v1, /device:TPU:0, one launch (start us, length us, event | category | flops | bytes accessed | tf_op | source)
XLA Modules:
  0.0 1156.5 jit_solution(12248276675417913577)
XLA Ops:
  24.0 72.3 %all-gather.5.cloned.1.call-done = bf16[1024,2048]{1,0:T(8,128)(2,1)} async-done(((bf16[256,2048]{1,0:T(8,128)(2,1)}), bf16[1024,2048]{1,0:T(8,128)(2,1)}) %all-gather.5.cloned.1.call-update) | async-done | bytes 4194320 | tf_op jit(solution)/shard_map/all_gather | solution.py:342
  96.3 8.1 fusion.28.gp_ref
  109.3 24.8 %shard_map.322 = (bf16[1024,640]{1,0:T(8,128)(2,1)}, f32[1024,640]{1,0:T(8,128)}, f32[1024,640]{1,0:T(8,128)}, f32[1024,640]{1,0:T(8,128)}, f32[1024,640]{1,0:T(8,128)}) custom-call(f32[1024,640]{1,0:T(8,128)} %fusion.27.vp_in, f32[1024,640]{1,0:T(8,128)} %fusion.28.gp_ref, f32[1032,8]{1,0:T(8,128)} %pad_convert_fusion.mask_ref, ...), custom_call_target="tpu_custom_call" | custom-call | flops 1677721600 | bytes 19660800 | tf_op jit(solution)/shard_map/pallas_call | solution.py:281
  140.4 75.4 %reduce-scatter.11.cloned.1.call-done = bf16[256,2048]{1,0:T(8,128)(2,1)} async-done(((bf16[1024,2048]{1,0:T(8,128)(2,1)}), bf16[256,2048]{1,0:T(8,128)(2,1)}) %reduce-scatter.11.cloned.1.call-update) | async-done | bytes 1048592 | tf_op jit(solution)/shard_map/reduce_scatter | solution.py:324
  221.5 80.6 %all-gather.7.cloned.1.call-done = bf16[1024,2048]{1,0:T(8,128)(2,1)} async-done(((bf16[256,2048]{1,0:T(8,128)(2,1)}), bf16[1024,2048]{1,0:T(8,128)(2,1)}) %all-gather.7.cloned.1.call-update) | async-done | bytes 4194320 | tf_op jit(solution)/shard_map/all_gather | solution.py:361
  302.1 12.4 %fusion.30 = f32[1024,1536]{1,0:T(8,128)} fusion(bf16[1024,2048]{1,0:T(8,128)(2,1)} %all-gather.7.cloned.1.call-done, bf16[2048,1536]{1,0:T(8,128)(2,1)} %param.36), kind=kOutput, calls=%fused_computation.97 | convolution fusion | flops 6442450944 | bytes 16777216 | tf_op jit(solution)/shard_map/dot_general | solution.py:36
  314.5 10.5 fusion.29
  325.0 57.9 %all-gather.9.cloned.1.call-done = bf16[1024,2048]{1,0:T(8,128)(2,1)} async-done(((bf16[256,2048]{1,0:T(8,128)(2,1)}), bf16[1024,2048]{1,0:T(8,128)(2,1)}) %all-gather.9.cloned.1.call-update) | async-done | bytes 4194320 | tf_op jit(solution)/shard_map/all_gather | solution.py:375
  382.9 19.2 %multiply_convert_fusion = (bf16[1024,1536]{1,0:T(8,128)(2,1)S(1)}, bf16[1024,1536]{1,0:T(8,128)(2,1)S(1)}, bf16[1024,1536]{1,0:T(8,128)(2,1)}) fusion(f32[1024,1536]{1,0:T(8,128)} %fusion.29, f32[1024,1536]{1,0:T(8,128)} %fusion.30, bf16[1024,2048]{1,0:T(8,128)(2,1)} %all-gather.9.cloned.1.call-done, bf16[1536,2048]{1,0:T(8,128)(2,1)} %param.37), kind=kOutput, calls=%fused_computation.15 | convolution fusion | flops 6489636864 | bytes 32505856 | tf_op jit(solution)/shard_map/dot_general | solution.py:40
  402.1 11.0 fusion.31
  413.2 11.1 add_convert_fusion.1
  424.4 75.4 %reduce-scatter.15.cloned.1.call-done = bf16[256,2048]{1,0:T(8,128)(2,1)} async-done(((bf16[1024,2048]{1,0:T(8,128)(2,1)}), bf16[256,2048]{1,0:T(8,128)(2,1)}) %reduce-scatter.15.cloned.1.call-update) | async-done | bytes 1048592 | tf_op jit(solution)/shard_map/reduce_scatter | solution.py:324
  506.3 11.4 convolution_convert_fusion
  517.8 11.6 %convolution_convert_fusion.1 = bf16[2048,1536]{1,0:T(8,128)(2,1)} fusion(bf16[1024,2048]{1,0:T(8,128)(2,1)} %all-gather.7.cloned.1.call-done, bf16[1024,1536]{1,0:T(8,128)(2,1)} %copy-done.26), kind=kOutput, calls=%fused_computation.7 | convolution fusion | flops 6445596672 | bytes 13631488 | tf_op jit(solution)/shard_map/dot_general | solution.py:44
  529.5 11.5 convolution_convert_fusion.2
  541.1 46.6 %all-gather.11.cloned.1.call-done = bf16[1024,2048]{1,0:T(8,128)(2,1)} async-done(((bf16[256,2048]{1,0:T(8,128)(2,1)}), bf16[1024,2048]{1,0:T(8,128)(2,1)}) %all-gather.11.cloned.1.call-update) | async-done | bytes 4194320 | tf_op jit(solution)/shard_map/all_gather | solution.py:387
  587.7 7.0 convolution_convert_fusion.5
  594.9 7.2 fusion.32.dm_ref
  602.2 32.3 %shard_map.323 = (bf16[1024,640]{1,0:T(8,128)(2,1)}, bf16[1024,640]{1,0:T(8,128)(2,1)}, f32[640,640]{1,0:T(8,128)}, f32[640,640]{1,0:T(8,128)}, f32[8,640]{1,0:T(8,128)}) custom-call(f32[1024,640]{1,0:T(8,128)} %fusion.32.dm_ref, f32[1024,640]{1,0:T(8,128)} %fusion.27.vp_in, f32[1024,640]{1,0:T(8,128)} %fusion.28.gp_ref, ...), custom_call_target="tpu_custom_call" | custom-call | flops 3355443200 | bytes 26214400 | tf_op jit(solution)/shard_map/pallas_call | solution.py:295
  634.5 7.6 convolution_convert_fusion.7
  642.4 7.6 convolution_convert_fusion.6
  661.1 11.8 %convolution_convert_fusion.3 = bf16[1024,2048]{1,0:T(8,128)(2,1)} fusion(bf16[1024,1536]{1,0:T(8,128)(2,1)} %get-tuple-element.59, bf16[1536,2048]{1,0:T(8,128)(2,1)} %param.37), kind=kOutput, calls=%fused_computation.23 | convolution fusion | flops 6444548096 | bytes 13631488 | tf_op jit(solution)/shard_map/dot_general | solution.py:36
  675.4 41.5 %reduce-scatter.27.cloned.1.call-done = bf16[256,1536]{1,0:T(8,128)(2,1)} async-done(((bf16[2048,1536]{1,0:T(8,128)(2,1)}), bf16[256,1536]{1,0:T(8,128)(2,1)}) %reduce-scatter.27.cloned.1.call-update) | async-done | bytes 786448 | tf_op jit(solution)/shard_map/reduce_scatter | solution.py:328
  719.3 62.7 %reduce-scatter.25.cloned.1.call-done = bf16[256,1536]{1,0:T(8,128)(2,1)} async-done(((bf16[2048,1536]{1,0:T(8,128)(2,1)}), bf16[256,1536]{1,0:T(8,128)(2,1)}) %reduce-scatter.25.cloned.1.call-update) | async-done | bytes 786448 | tf_op jit(solution)/shard_map/reduce_scatter | solution.py:328
  784.5 23.7 %psum.50 = f32[8,640]{1,0:T(8,128)S(1)} all-reduce(f32[8,640]{1,0:T(8,128)S(1)} %copy-done.7), channel_id=1, replica_groups=mesh['dp'=8,'mp'=4] {'dp'}, use_global_device_ids=true, to_apply=%region_14.15 | all-reduce | flops 5120 | bytes 40960 | tf_op jit(solution)/shard_map/psum | solution.py:399
  813.6 15.6 %reduce-scatter.23.cloned.1.call-done = bf16[640,256]{1,0:T(8,128)(2,1)} async-done(((bf16[640,2048]{1,0:T(8,128)(2,1)}), bf16[640,256]{1,0:T(8,128)(2,1)}) %reduce-scatter.23.cloned.1.call-update) | async-done | bytes 327696 | tf_op jit(solution)/shard_map/reduce_scatter | solution.py:328
  831.1 45.5 %reduce-scatter.19.cloned.1.call-done = bf16[256,640]{1,0:T(8,128)(2,1)} async-done(((bf16[2048,640]{1,0:T(8,128)(2,1)}), bf16[256,640]{1,0:T(8,128)(2,1)}) %reduce-scatter.19.cloned.1.call-update) | async-done | bytes 327696 | tf_op jit(solution)/shard_map/reduce_scatter | solution.py:328
  878.5 45.4 %reduce-scatter.21.cloned.1.call-done = bf16[256,640]{1,0:T(8,128)(2,1)} async-done(((bf16[2048,640]{1,0:T(8,128)(2,1)}), bf16[256,640]{1,0:T(8,128)(2,1)}) %reduce-scatter.21.cloned.1.call-update) | async-done | bytes 327696 | tf_op jit(solution)/shard_map/reduce_scatter | solution.py:328
  925.7 77.3 %reduce-scatter.17.cloned.1.call-done = bf16[256,2048]{1,0:T(8,128)(2,1)} async-done(((bf16[1024,2048]{1,0:T(8,128)(2,1)}), bf16[256,2048]{1,0:T(8,128)(2,1)}) %reduce-scatter.17.cloned.1.call-update) | async-done | bytes 1048592 | tf_op jit(solution)/shard_map/reduce_scatter | solution.py:324
  1005.7 76.8 %reduce-scatter.13.cloned.1.call-done = bf16[256,2048]{1,0:T(8,128)(2,1)} async-done(((bf16[1024,2048]{1,0:T(8,128)(2,1)}), bf16[256,2048]{1,0:T(8,128)(2,1)}) %reduce-scatter.13.cloned.1.call-update) | async-done | bytes 1048592 | tf_op jit(solution)/shard_map/reduce_scatter | solution.py:324
  1090.9 41.3 %all-reduce.1 = (f32[2048]{0:T(1024)}, f32[2048]{0:T(1024)}, f32[3]{0:T(128)S(1)}, f32[]{:T(128)}) all-reduce(f32[2048]{0:T(1024)S(1)} %get-tuple-element.40, f32[2048]{0:T(1024)S(1)} %get-tuple-element.38, f32[3]{0:T(128)S(1)} %pad_maximum_fusion.2, f32[]{:T(128)} %get-tuple-element.47), channel_id=1, replica_groups=mesh['dp'=8,'mp'=4] {'dp','mp'}, use_global_device_ids=true, to_apply=%region_11.12 | all-reduce | flops 4100 | bytes 32800 | tf_op jit(solution)/shard_map/psum | solution.py:401
  1133.4 12.2 %all-reduce.5.cloned.1.call-done = (f32[4,160,160]{2,1,0:T(8,128)}, f32[4,160,160]{2,1,0:T(8,128)}) async-done(((f32[4,160,160]{2,1,0:T(8,128)}, f32[4,160,160]{2,1,0:T(8,128)}), (f32[4,160,160]{2,1,0:T(8,128)}, f32[4,160,160]{2,1,0:T(8,128)})) %all-reduce.5.cloned.1.call-update) | async-done | bytes 819216 | tf_op jit(solution)/shard_map/psum | solution.py:399
  (133 shorter events, 85.7 us)
Async XLA Ops:
  7.2 126.8 %copy-start = (bf16[640,2048]{1,0:T(8,128)(2,1)S(1)}, bf16[640,2048]{1,0:T(8,128)(2,1)}, u32[]{:S(2)}) copy-start(bf16[640,2048]{1,0:T(8,128)(2,1)} %param.33) | copy-start | bytes 7864324
  7.3 89.0 %all-gather.5.cloned.1.call-start = ((), (), s32[]{:S(2)}) async-start(), calls=%async_computation.10 | async-start | bytes 5242880 | tf_op jit(solution)/shard_map/all_gather | solution.py:342
  12.6 203.1 %reduce-scatter.11.cloned.1.call-start = ((), (), s32[]{:S(2)}) async-start(), calls=%async_computation.11 | async-start | bytes 5242880 | tf_op jit(solution)/shard_map/reduce_scatter | solution.py:324
  12.8 9.2 copy-start.19
  12.8 9.3 copy-start.14
  96.2 8.1 copy-start.20
  96.2 8.1 copy-start.22
  140.3 77.4 %copy-start.5 = (f32[2048]{0:T(1024)S(1)}, f32[2048]{0:T(1024)}, u32[]{:S(2)}) copy-start(f32[2048]{0:T(1024)} %param.34) | copy-start | bytes 24580
  140.3 161.8 %all-gather.7.cloned.1.call-start = ((), (), s32[]{:S(2)}) async-start(), calls=%async_computation.12 | async-start | bytes 5242880 | tf_op jit(solution)/shard_map/all_gather | solution.py:361
  220.7 162.3 %all-gather.9.cloned.1.call-start = ((), (), s32[]{:S(2)}) async-start(), calls=%async_computation.14 | async-start | bytes 5242880 | tf_op jit(solution)/shard_map/all_gather | solution.py:375
  221.2 278.6 %reduce-scatter.15.cloned.1.call-start = ((), (), s32[]{:S(2)}) async-start(), calls=%async_computation.15 | async-start | bytes 5242880 | tf_op jit(solution)/shard_map/reduce_scatter | solution.py:324
  302.1 12.4 %copy-start.21 = (bf16[1024,2048]{1,0:T(8,128)(2,1)S(1)}, bf16[1024,2048]{1,0:T(8,128)(2,1)}, u32[]{:S(2)}) copy-start(bf16[1024,2048]{1,0:T(8,128)(2,1)} %all-gather.7.cloned.1.call-done) | copy-start | bytes 12582916
  402.1 11.1 copy-start.25
  402.1 11.1 copy-start.26
  424.3 163.3 %all-gather.11.cloned.1.call-start = ((), (), s32[]{:S(2)}) async-start(), calls=%async_computation.16 | async-start | bytes 5242880 | tf_op jit(solution)/shard_map/all_gather | solution.py:387
  506.3 166.7 %reduce-scatter.29.cloned.1.call-start = ((), (), s32[]{:S(2)}) async-start(), calls=%async_computation.23 | async-start | bytes 7077888 | tf_op jit(solution)/shard_map/reduce_scatter | solution.py:328
  517.7 199.2 %reduce-scatter.27.cloned.1.call-start = ((), (), s32[]{:S(2)}) async-start(), calls=%async_computation.22 | async-start | bytes 7077888 | tf_op jit(solution)/shard_map/reduce_scatter | solution.py:328
  529.4 252.6 %reduce-scatter.25.cloned.1.call-start = ((), (), s32[]{:S(2)}) async-start(), calls=%async_computation.21 | async-start | bytes 7077888 | tf_op jit(solution)/shard_map/reduce_scatter | solution.py:328
  541.1 288.2 %reduce-scatter.23.cloned.1.call-start = ((), (), s32[]{:S(2)}) async-start(), calls=%async_computation.20 | async-start | bytes 2949120 | tf_op jit(solution)/shard_map/reduce_scatter | solution.py:328
  594.7 282.0 %reduce-scatter.19.cloned.1.call-start = ((), (), s32[]{:S(2)}) async-start(), calls=%async_computation.18 | async-start | bytes 2949120 | tf_op jit(solution)/shard_map/reduce_scatter | solution.py:328
  642.1 281.8 %reduce-scatter.21.cloned.1.call-start = ((), (), s32[]{:S(2)}) async-start(), calls=%async_computation.19 | async-start | bytes 2949120 | tf_op jit(solution)/shard_map/reduce_scatter | solution.py:328
  650.0 353.0 %reduce-scatter.17.cloned.1.call-start = ((), (), s32[]{:S(2)}) async-start(), calls=%async_computation.17 | async-start | bytes 5242880 | tf_op jit(solution)/shard_map/reduce_scatter | solution.py:324
  650.1 5.8 copy-start.23
  650.1 5.8 copy-start.24
  661.0 421.4 %reduce-scatter.13.cloned.1.call-start = ((), (), s32[]{:S(2)}) async-start(), calls=%async_computation.13 | async-start | bytes 5242880 | tf_op jit(solution)/shard_map/reduce_scatter | solution.py:324
  672.9 111.6 %copy-start.7 = (f32[8,640]{1,0:T(8,128)S(1)}, f32[8,640]{1,0:T(8,128)}, u32[]{:S(2)}) copy-start(f32[8,640]{1,0:T(8,128)} %get-tuple-element.35) | copy-start | bytes 61444
  672.9 472.6 %all-reduce.5.cloned.1.call-start = ((), (), s32[]{:S(2)}) async-start(), calls=%async_computation.24 | async-start | bytes 2621440 | tf_op jit(solution)/shard_map/psum | solution.py:399
  784.5 28.5 %copy-start.13 = (f32[640]{0:T(1024)S(1)}, f32[640]{0:T(1024)}, u32[]{:S(2)}) copy-start(f32[640]{0:T(1024)} %param.32) | copy-start | bytes 7684
  811.2 191.9 %copy-start.6 = (f32[2048]{0:T(1024)S(1)}, f32[2048]{0:T(1024)}, u32[]{:S(2)}) copy-start(f32[2048]{0:T(1024)} %param.23) | copy-start | bytes 24580
  811.2 191.9 %copy-start.9 = (f32[256]{0:T(256)S(1)}, f32[256]{0:T(256)}, u32[]{:S(2)}) copy-start(f32[256]{0:T(256)} %copy-done.8) | copy-start | bytes 3076
  813.6 192.0 %copy-start.11 = (f32[256]{0:T(256)S(1)}, f32[256]{0:T(256)}, u32[]{:S(2)}) copy-start(f32[256]{0:T(256)} %copy-done.10) | copy-start | bytes 3076
  1005.7 82.5 %copy-start.18 = (s32[256]{0:T(256)S(1)}, s32[256]{0:T(256)}, u32[]{:S(2)}) copy-start(s32[256]{0:T(256)} %param.22) | copy-start | bytes 3076
  (10 other events, 38.2 us)
Sparse Core Ops, SparseCore 0:
  12.7 83.4 all-gather.4
  140.4 75.2 reduce-scatter.10
  220.8 81.2 all-gather.6
  303.6 79.2 all-gather.8
  424.5 75.2 reduce-scatter.14
  506.4 81.2 all-gather.10
  591.0 60.2 reduce-scatter.28
  655.1 61.7 reduce-scatter.26
  720.3 61.7 reduce-scatter.24
  785.6 43.6 reduce-scatter.22
  832.9 43.6 reduce-scatter.18
  880.2 43.6 reduce-scatter.20
  926.3 76.7 reduce-scatter.16
  1005.2 77.2 reduce-scatter.12
  1087.0 58.4 all-reduce.4

commit v2 on v1

--- a/solution.py
+++ b/solution.py
@@ -309,6 +309,346 @@
     )(dm, vp, gp, masks, vec, rate, inlet, state, conv, forget, inp)
 
 
+MESH = pl.DeviceIdType.MESH
+PARTS = 4
+
+
+def greet(axis, count):
+    me = lax.axis_index(axis)
+    barrier = pltpu.get_barrier_semaphore()
+
+    @pl.when(me > 0)
+    def _():
+        pl.semaphore_signal(barrier, inc=1, device_id={axis: me - 1}, device_id_type=MESH)
+
+    @pl.when(me < count - 1)
+    def _():
+        pl.semaphore_signal(barrier, inc=1, device_id={axis: me + 1}, device_id_type=MESH)
+
+    inner = (me > 0) & (me < count - 1)
+
+    @pl.when(inner)
+    def _():
+        pl.semaphore_wait(barrier, 2)
+
+    @pl.when(jnp.logical_not(inner))
+    def _():
+        pl.semaphore_wait(barrier, 1)
+
+
+class Gather:
+    def __init__(self, count, buf, send, recv):
+        self.count, self.buf, self.send, self.recv = count, buf, send, recv
+        self.me = lax.axis_index("mp")
+
+    def copy(self, block, way):
+        return pltpu.make_async_remote_copy(
+            src_ref=self.buf.at[block],
+            dst_ref=self.buf.at[block],
+            send_sem=self.send.at[0 if way < 0 else 1, block],
+            recv_sem=self.recv.at[block],
+            device_id={"mp": self.me + way},
+            device_id_type=MESH,
+        )
+
+    def hand_on(self, block, way):
+        pl.when(self.me < self.count - 1 if way > 0 else self.me > 0)(self.copy(block, way).start)
+
+    def start(self):
+        self.hand_on(self.me, 1)
+        self.hand_on(self.me, -1)
+
+    def take(self, distance):
+        low, high = self.me - distance, self.me + distance
+
+        @pl.when(low >= 0)
+        def _():
+            self.copy(low, -1).wait_recv()
+            self.hand_on(low, 1)
+
+        @pl.when(high < self.count)
+        def _():
+            self.copy(high, 1).wait_recv()
+            self.hand_on(high, -1)
+
+    def drain(self):
+        def step(block, unused):
+            pl.when((block <= self.me) & (self.me < self.count - 1))(self.copy(block, 1).wait_send)
+            pl.when((block >= self.me) & (self.me > 0))(self.copy(block, -1).wait_send)
+            return unused
+
+        lax.fori_loop(0, self.count, step, 0)
+
+
+class Scatter:
+    def __init__(self, count, held, slots, send, recv):
+        self.count, self.held, self.slots, self.send, self.recv = count, held, slots, send, recv
+        self.me = lax.axis_index("mp")
+
+    def copy(self, block, part, way):
+        slot = block + 1 if way > 0 else block
+        return pltpu.make_async_remote_copy(
+            src_ref=self.held.at[block, part],
+            dst_ref=self.slots.at[slot, part],
+            send_sem=self.send.at[block, part],
+            recv_sem=self.recv.at[slot, part],
+            device_id={"mp": self.me + way},
+            device_id_type=MESH,
+        )
+
+    def first(self, block, part):
+        pl.when((self.me == 0) & (block > 0))(self.copy(block, part, 1).start)
+        pl.when((self.me == self.count - 1) & (block < self.count - 1))(self.copy(block, part, -1).start)
+
+    def pass_part(self, block, part, way):
+        self.arrived(block, part, way)
+        slot = block + 1 if way > 0 else block
+        self.held[block, part] = (
+            self.held[block, part].astype(F32) + self.slots[slot, part].astype(F32)).astype(BF)
+        self.copy(block, part, way).start()
+
+    def arrived(self, block, part, way):
+        slot = block + 1 if way > 0 else block
+        pltpu.make_async_remote_copy(
+            src_ref=self.held.at[block, part],
+            dst_ref=self.slots.at[slot, part],
+            send_sem=self.send.at[block, part],
+            recv_sem=self.recv.at[slot, part],
+            device_id={"mp": self.me - way},
+            device_id_type=MESH,
+        ).wait_recv()
+
+    def pass_on(self, time):
+        last = self.count - 1
+        up = time + 1 - self.me
+        down = last - 1 + last - self.me - time
+        up_here = (self.me > 0) & (up > self.me) & (up <= last)
+        down_here = (self.me < last) & (down < self.me) & (down >= 0)
+
+        def step(part, unused):
+            pl.when(up_here)(lambda: self.pass_part(up, part, 1))
+            pl.when(down_here)(lambda: self.pass_part(down, part, -1))
+            return unused
+
+        lax.fori_loop(0, PARTS, step, 0)
+
+    def total(self, part):
+        pl.when(self.me > 0)(lambda: self.arrived(self.me, part, 1))
+        pl.when(self.me < self.count - 1)(lambda: self.arrived(self.me, part, -1))
+        below = jnp.where(self.me > 0, self.slots[self.me + 1, part].astype(F32), 0.0)
+        above = jnp.where(self.me < self.count - 1, self.slots[self.me, part].astype(F32), 0.0)
+        return self.held[self.me, part].astype(F32) + below + above
+
+    def drain(self):
+        def step(block, unused):
+            for part in range(PARTS):
+                pl.when(block > self.me)(self.copy(block, part, 1).wait_send)
+                pl.when(block < self.me)(self.copy(block, part, -1).wait_send)
+            return unused
+
+        lax.fori_loop(0, self.count, step, 0)
+
+
+def spans(total):
+    size = 512 if total % 512 == 0 else 256
+    return [slice(at, at + size) for at in range(0, total, size)]
+
+
+def dense_kernel(count, groups, middle_ref, gain_ref, cot_hbm, gate_hbm, value_hbm, down_hbm,
+                 middle_grad_ref, gain_grad_ref, dense_part_hbm, gate_out, value_out, down_out,
+                 normed, cot, gate_w, value_w, down_w, hidden, gate_g, value_g, dense_part, held, slots, stage,
+                 load_sem, cot_sem, part_sem, stage_sem, ag_send, ag_recv, rs_send, rs_recv):
+    me = lax.axis_index("mp")
+    rows, columns = middle_ref.shape
+    units = gate_w.shape[1]
+    width = columns // PARTS
+    loads = [pltpu.make_async_copy(gate_hbm, gate_w, load_sem.at[0]),
+             pltpu.make_async_copy(value_hbm, value_w, load_sem.at[1]),
+             pltpu.make_async_copy(down_hbm, down_w, load_sem.at[2])]
+    for load in loads:
+        load.start()
+
+    def cot_copy(block):
+        return pltpu.make_async_copy(cot_hbm.at[pl.ds(pl.multiple_of(block * rows, rows), rows)],
+                                     cot.at[block], cot_sem.at[block])
+
+    for block in range(count):
+        cot_copy(block).start()
+    greet("mp", count)
+    gather = Gather(count, normed, ag_send, ag_recv)
+    scatter = Scatter(count, held, slots, rs_send, rs_recv)
+    step_rows = 64
+
+    def norm_step(index, unused):
+        window = pl.ds(pl.multiple_of(index * step_rows, step_rows), step_rows)
+        middle = middle_ref[window, :]
+        scale = lax.rsqrt(jnp.mean(middle * middle, axis=1, keepdims=True) + EPS)
+        normed[me, window, :] = (middle * scale * gain_ref[...]).astype(BF)
+        return unused
+
+    lax.fori_loop(0, rows // step_rows, norm_step, 0)
+    gather.start()
+    for load in loads:
+        load.wait()
+    pieces = 3
+    piece = units // pieces
+
+    def part_copy(block, slot):
+        return pltpu.make_async_copy(dense_part.at[slot], dense_part_hbm.at[block], part_sem.at[slot])
+
+    def compute(block, slot, reuse):
+        cot_copy(block).wait()
+        rows_in = normed[block]
+        rows_cot = cot[block]
+        for index in range(pieces):
+            span = slice(index * piece, (index + 1) * piece)
+            gate_linear = dot_nn(rows_in, gate_w[:, span])
+            value_linear = dot_nn(rows_in, value_w[:, span])
+            hidden_grad = dot_nt(rows_cot, down_w[span, :])
+            act, slope = gelu_both(gate_linear)
+            hidden[block, :, span] = (act * value_linear).astype(BF)
+            gate_g[block, :, span] = (hidden_grad * value_linear * slope).astype(BF)
+            value_g[block, :, span] = (hidden_grad * act).astype(BF)
+        for part in range(PARTS):
+            span = slice(part * width, (part + 1) * width)
+            held[block, part] = (dot_nt(gate_g[block], gate_w[span, :])
+                                 + dot_nt(value_g[block], value_w[span, :])).astype(BF)
+            scatter.first(block, part)
+        pl.when(reuse)(lambda: part_copy(block, slot).wait())
+        for part in range(PARTS):
+            span = slice(part * width, (part + 1) * width)
+            dense_part[slot, part] = dot_nn(hidden[block], down_w[:, span]).astype(BF)
+        part_copy(block, slot).start()
+
+    def arrive(distance, unused):
+        pl.when(distance > 0)(lambda: gather.take(distance))
+
+        def side(which, inner):
+            block = me - distance + 2 * distance * which
+            pl.when((block >= 0) & (block < count) & ((distance > 0) | (which == 0)))(
+                lambda: compute(block, which, (distance > 1) | ((distance == 1) & (which == 0))))
+            return inner
+
+        return lax.fori_loop(0, 2, side, unused)
+
+    lax.fori_loop(0, count, arrive, 0)
+
+    total_rows = count * rows
+    left_rows = columns // 4
+    unit_rows = units // 4
+    group_width = columns // groups
+
+    def stage_copy(kind, index, slot):
+        if kind == 2:
+            half = columns // 2
+            return pltpu.make_async_copy(
+                stage.at[slot, pl.ds(0, unit_rows), pl.ds(0, half)],
+                down_out.at[pl.ds(index // 2 * unit_rows, unit_rows), pl.ds(index % 2 * half, half)],
+                stage_sem.at[slot])
+        target = gate_out if kind == 0 else value_out
+        return pltpu.make_async_copy(
+            stage.at[slot, pl.ds(0, left_rows), pl.ds(0, units)],
+            target.at[pl.ds(index * left_rows, left_rows)], stage_sem.at[slot])
+
+    def grads(kind, index, slot):
+        if kind == 2:
+            low = index // 2 * unit_rows
+            left = hidden[:, :, low:low + unit_rows].reshape(total_rows, unit_rows)
+            for span in spans(columns // 2):
+                at = index % 2 * (columns // 2) + span.start
+                size = span.stop - span.start
+                right = cot[:, :, at:at + size].reshape(total_rows, size)
+                stage[slot, 0:unit_rows, span] = dot_tn(left, right).astype(BF)
+        else:
+            left = normed[:, :, index * left_rows:(index + 1) * left_rows].reshape(total_rows, left_rows)
+            source = gate_g if kind == 0 else value_g
+            for span in spans(units):
+                right = source[:, :, span].reshape(total_rows, span.stop - span.start)
+                stage[slot, 0:left_rows, span] = dot_tn(left, right).astype(BF)
+
+    work = [(kind, index) for kind in (0, 1, 2) for index in range((4, 4, 8)[kind])]
+    started = []
+    times = max(2 * count - 5, 0)
+    per_step = -(-len(work) // (times + 1))
+    for step in range(times + 1):
+        if step > 0:
+            scatter.pass_on(step + 1)
+        for kind, index in work[step * per_step:(step + 1) * per_step]:
+            slot = len(started) % 2
+            if len(started) >= 2:
+                stage_copy(*started[-2], slot).wait()
+            grads(kind, index, slot)
+            stage_copy(kind, index, slot).start()
+            started.append((kind, index))
+    for back in (2, 1):
+        stage_copy(*started[-back], (len(started) - back) % 2).wait()
+
+    dot_sum = jnp.zeros((rows, 1), F32)
+    square_sum = jnp.zeros((rows, 1), F32)
+    for part in range(PARTS):
+        span = slice(part * width, (part + 1) * width)
+        grad = scatter.total(part)
+        middle = middle_ref[:, span]
+        middle_grad_ref[:, span] = grad
+        dot_sum = dot_sum + jnp.sum(grad * gain_ref[:, span] * middle, axis=1, keepdims=True)
+        square_sum = square_sum + jnp.sum(middle * middle, axis=1, keepdims=True)
+    scale = lax.rsqrt(square_sum * (1.0 / columns) + EPS)
+    pull = scale * scale * scale * (dot_sum * (1.0 / columns))
+    for part in range(PARTS):
+        span = slice(part * width, (part + 1) * width)
+        grad = middle_grad_ref[:, span]
+        middle = middle_ref[:, span]
+        gain_grad_ref[:, span] = jnp.sum(grad * middle * scale, axis=0, keepdims=True)
+        result = cot[me, :, span].astype(F32) + scale * (grad * gain_ref[:, span]) - middle * pull
+        middle_grad_ref[:, span] = result
+    part_copy(0, 0).wait()
+    pl.when(me < count - 1)(part_copy(0, 1).wait)
+    gather.drain()
+    scatter.drain()
+
+
+def call_dense(count, groups, middle, gain, cot_all, dense_gate, dense_value, dense_down):
+    rows, columns = middle.shape
+    units = dense_gate.shape[1]
+    width = columns // PARTS
+    any_spec = pl.BlockSpec(memory_space=pl.ANY)
+    vmem = pl.BlockSpec(memory_space=pltpu.VMEM)
+    dma = pltpu.SemaphoreType.DMA
+    return pl.pallas_call(
+        functools.partial(dense_kernel, count, groups),
+        out_shape=(
+            jax.ShapeDtypeStruct((rows, columns), F32),
+            jax.ShapeDtypeStruct((1, columns), F32),
+            jax.ShapeDtypeStruct((count, PARTS, rows, width), BF),
+            jax.ShapeDtypeStruct((columns, units), BF),
+            jax.ShapeDtypeStruct((columns, units), BF),
+            jax.ShapeDtypeStruct((units, columns), BF),
+        ),
+        in_specs=[vmem, vmem, any_spec, any_spec, any_spec, any_spec],
+        out_specs=(vmem, vmem, any_spec, any_spec, any_spec, any_spec),
+        scratch_shapes=[
+            pltpu.VMEM((count, rows, columns), BF),
+            pltpu.VMEM((count, rows, columns), BF),
+            pltpu.VMEM((columns, units), BF),
+            pltpu.VMEM((columns, units), BF),
+            pltpu.VMEM((units, columns), BF),
+            pltpu.VMEM((count, rows, units), BF),
+            pltpu.VMEM((count, rows, units), BF),
+            pltpu.VMEM((count, rows, units), BF),
+            pltpu.VMEM((2, PARTS, rows, width), BF),
+            pltpu.VMEM((count, PARTS, rows, width), BF),
+            pltpu.VMEM((count + 1, PARTS, rows, width), BF),
+            pltpu.VMEM((2, columns // 4, max(units, columns // 2)), BF),
+            dma((3,)), dma((count,)), dma((2,)), dma((2,)),
+            dma((2, count)), dma((count,)), dma((count, PARTS)), dma((count + 1, PARTS)),
+        ],
+        compiler_params=pltpu.CompilerParams(
+            vmem_limit_bytes=VMEM_LIMIT, collective_id=0, has_side_effects=True),
+        cost_estimate=pl.CostEstimate(flops=18 * count * rows * columns * units,
+                                      bytes_accessed=12 * columns * units, transcendentals=count * rows * units),
+    )(middle, gain, cot_all, dense_gate, dense_value, dense_down)
+
+
 def block_diagonal(heads):
     count, width, unused = heads.shape
     spread = heads[:, :, None, :] * jnp.eye(count, dtype=heads.dtype)[:, None, :, None]
@@ -328,11 +668,7 @@
     return lax.psum_scatter(values.astype(BF), "dp", scatter_dimension=dimension, tiled=True).astype(F32)
 
 
-def gated_unit(gate_linear, value_linear):
-    return gelu(gate_linear) * value_linear
-
-
-def local(tokens, cotangent, lengths, live_mask, mixer_gain, value_proj, gate_proj, conv_taps, conv_bias,
+def local(groups, tokens, cotangent, lengths, live_mask, mixer_gain, value_proj, gate_proj, conv_taps, conv_bias,
           rate_weight, rate_bias, inlet_weight, inlet_bias, decay_param, mixer_out, dense_gain,
           dense_gate, dense_value, dense_down):
     residual = tokens.astype(F32)
@@ -357,13 +693,14 @@
         value_pre, gate_pre, masks_ext, vec, rate_square, inlet_square)
     mixer_part = scatter_mp(dot_nn(mixed_act, mixer_out))
     middle = residual + mixer_part
-    normed_float, norm_back_mid = jax.vjp(scaled_norm, middle, dense_gain)
-    normed_mid_all = lax.all_gather(normed_float.astype(BF), "mp", axis=0, tiled=True)
-    gate_linear = dot_nn(normed_mid_all, dense_gate)
-    value_linear = dot_nn(normed_mid_all, dense_value)
-    hidden_float, gated_back = jax.vjp(gated_unit, gate_linear, value_linear)
-    hidden = hidden_float.astype(BF)
-    dense_part = scatter_mp(dot_nn(hidden, dense_down))
+    block_rows = lax.all_gather(cotangent, "mp", axis=0, tiled=True)
+    count = rows_total // tokens.shape[0]
+    middle_grad, dense_gain_grad, dense_terms, dense_gate_grad, dense_value_grad, down_grad = call_dense(
+        count, groups, middle, dense_gain[None, :], block_rows, dense_gate, dense_value, dense_down)
+    dense_gain_grad = dense_gain_grad[0]
+    middle_low = middle_grad.astype(BF)
+    dense_part = lax.psum_scatter(dense_terms, "mp", scatter_dimension=0, tiled=True)[0].astype(F32)
+    dense_part = dense_part.transpose(1, 0, 2).reshape(tokens.shape)
     layer_out = (middle + dense_part).astype(BF)
     weights_live = live_mask.astype(F32)
     squares = jnp.stack([
@@ -372,18 +709,6 @@
         jnp.sum(weights_live * jnp.sum(dense_part * dense_part, axis=1)),
     ])
     live_count = jnp.sum(weights_live)
-    block_rows = lax.all_gather(cotangent, "mp", axis=0, tiled=True)
-    hidden_grad = dot_nt(block_rows, dense_down)
-    down_grad = dot_tn(hidden, block_rows)
-    gate_grad_float, value_grad_float = gated_back(hidden_grad)
-    gate_grad = gate_grad_float.astype(BF)
-    value_grad = value_grad_float.astype(BF)
-    normed_mid_grad = scatter_mp(dot_nt(gate_grad, dense_gate) + dot_nt(value_grad, dense_value))
-    dense_gate_grad = dot_tn(normed_mid_all, gate_grad)
-    dense_value_grad = dot_tn(normed_mid_all, value_grad)
-    middle_norm_grad, dense_gain_grad = norm_back_mid(normed_mid_grad)
-    middle_grad = cotangent.astype(F32) + middle_norm_grad
-    middle_low = middle_grad.astype(BF)
     middle_rows = lax.all_gather(middle_low, "mp", axis=0, tiled=True)
     mixed_grad = dot_nt(middle_rows, mixer_out)
     mixer_out_grad = dot_tn(mixed_act, middle_rows)
@@ -426,7 +751,7 @@
 def solution(mesh):
     rows = P(("dp", "mp"), None)
     return jax.shard_map(
-        local,
+        functools.partial(local, mesh.shape["dp"]),
         mesh=mesh,
         in_specs=(
             rows, rows, P("dp", None), P(("dp", "mp")), P(),

time: 1170 us -> 1090 us (0.932)
  Pallas kernels: 57.1 us -> 188 us
  matrix products: 170 us -> 59.8 us
  waiting for transfers between devices: 786 us -> 693 us
    reduce_scatter x4 -> x2, waiting for transfers between devices: 305 us -> 152 us  [scatter_mp(): lax.psum_scatter(values.astype(BF), 'mp', scatter_dimension=0, tiled=True)]
    pallas_call x0 -> x1, Pallas kernels: none -> 131 us  [call_dense(): pl.pallas_call(functools.partial(dense_kernel, count, groups), out_shape=...]
    reduce_scatter x6, waiting for transfers between devices: 211 us -> 298 us  [scatter_dp(): lax.psum_scatter(values.astype(BF), 'dp', scatter_dimension=dimension, ti...]
    all_gather x1 -> x0, waiting for transfers between devices: 80.6 us -> none  [local(): lax.all_gather(normed_float.astype(BF), 'mp', axis=0, tiled=True)]
    dot_general x6 -> x3, matrix products: 59.5 us -> 18.3 us  [dot_nt(): lax.dot_general(left, right, (((1,), (1,)), ((), ())), preferred_element_...]
    dot_general x6 -> x3, matrix products: 54 us -> 19.3 us  [dot_nn(): return jnp.dot(left, right, preferred_element_type=F32)]
    dot_general x6 -> x3, matrix products: 56.7 us -> 22.2 us  [dot_tn(): lax.dot_general(left, right, (((0,), (0,)), ((), ())), preferred_element_...]
    all_gather x1, waiting for transfers between devices: 46.6 us -> 77.8 us  [local(): middle_rows = lax.all_gather(middle_low, 'mp', axis=0, tiled=True)]
  transfers between devices with their start and end apart: 15 -> 13, of which waited for: 14 -> 12; matrix products, arithmetic and copies ran while one was open for 13% -> 8% of each run, Pallas kernels for 3% -> 3%
where the time goes in v2:
time: 1090 us; the launch traced here: 1080 us
  waiting for transfers between devices  693 us (64%)
  Pallas kernels  188 us (17%)
  blocking collectives  65.5 us (6%)
  matrix products  59.8 us (5%)
  other arithmetic  43 us (4%)
  local copies, waits for them, and re-layouts  15.8 us (1%)
  between operations  15.3 us (1%)
    reduce_scatter x6, waiting for transfers between devices, scatter_dp(): lax.psum_scatter(values.astype(BF), 'dp', scatter_dimension=dimension, ti...  298 us
    reduce_scatter x2, waiting for transfers between devices, scatter_mp(): lax.psum_scatter(values.astype(BF), 'mp', scatter_dimension=0, tiled=True)  152 us
    pallas_call x1, Pallas kernels, call_dense(): pl.pallas_call(functools.partial(dense_kernel, count, groups), out_shape=...  131 us
    all_gather x1, waiting for transfers between devices, local(): block_rows = lax.all_gather(cotangent, 'mp', axis=0, tiled=True)  79.7 us
    all_gather x1, waiting for transfers between devices, local(): middle_rows = lax.all_gather(middle_low, 'mp', axis=0, tiled=True)  77.8 us
    all_gather x1, waiting for transfers between devices, local(): lax.all_gather(normed_first.astype(BF), 'mp', axis=0, tiled=True)  72.3 us
    psum x1, blocking collectives, local(): lax.psum((mixer_gain_grad, dense_gain_grad, squares, live_count), ('dp',...  41.2 us
    pallas_call x1, Pallas kernels, call_backward(): pl.pallas_call(backward_kernel, out_shape=(low, low, square, square, jax....  32 us
  transfers between devices with their start and end apart: 13, of which 12 were waited for; matrix products, arithmetic and copies ran while one was open for 8% of the time, Pallas kernels for 3%

profile of v2, /device:TPU:0, one launch (start us, length us, event | category | flops | bytes accessed | tf_op | source)
XLA Modules:
  0.0 1080.7 jit_solution(17924544214776008453)
XLA Ops:
  11.7 3.6 multiply_convert_fusion
  15.3 2.8 convert_element_type.89.inlet_ref
  18.1 2.8 convert_element_type.87.rate_ref
  22.8 72.3 %all-gather.4.cloned.1.call-done = bf16[1024,2048]{1,0:T(8,128)(2,1)} async-done(((bf16[256,2048]{1,0:T(8,128)(2,1)}), bf16[1024,2048]{1,0:T(8,128)(2,1)}) %all-gather.4.cloned.1.call-update) | async-done | bytes 4194320 | tf_op jit(solution)/shard_map/all_gather | solution.py:678
  95.1 8.0 fusion.15.gp_ref
  103.2 4.9 fusion.14.vp_in
  108.0 24.8 %shard_map.322 = (bf16[1024,640]{1,0:T(8,128)(2,1)}, f32[1024,640]{1,0:T(8,128)}, f32[1024,640]{1,0:T(8,128)}, f32[1024,640]{1,0:T(8,128)}, f32[1024,640]{1,0:T(8,128)}) custom-call(f32[1024,640]{1,0:T(8,128)} %fusion.14.vp_in, f32[1024,640]{1,0:T(8,128)} %fusion.15.gp_ref, f32[1032,8]{1,0:T(8,128)} %pad_convert_fusion.mask_ref, ...), custom_call_target="tpu_custom_call" | custom-call | flops 1677721600 | bytes 19660800 | tf_op jit(solution)/shard_map/pallas_call | solution.py:281
  132.8 6.3 convolution_convert_fusion
  140.0 74.7 %reduce-scatter.10.cloned.1.call-done = bf16[256,2048]{1,0:T(8,128)(2,1)} async-done(((bf16[1024,2048]{1,0:T(8,128)(2,1)}), bf16[256,2048]{1,0:T(8,128)(2,1)}) %reduce-scatter.10.cloned.1.call-update) | async-done | bytes 1048592 | tf_op jit(solution)/shard_map/reduce_scatter | solution.py:664
  214.6 3.2 convert_add_fusion.middle_ref
  217.8 79.7 %all-gather.6.cloned.1.call-done.cot_hbm = bf16[1024,2048]{1,0:T(8,128)(2,1)} async-done(((bf16[256,2048]{1,0:T(8,128)(2,1)}), bf16[1024,2048]{1,0:T(8,128)(2,1)}) %all-gather.6.cloned.1.call-update) | async-done | bytes 4194320 | tf_op jit(solution)/shard_map/all_gather | solution.py:696
  297.6 131.1 %shard_map.323 = (f32[256,2048]{1,0:T(8,128)}, f32[1,2048]{1,0:T(1,128)}, bf16[4,4,256,512]{3,2,1,0:T(8,128)(2,1)}, bf16[2048,1536]{1,0:T(8,128)(2,1)}, bf16[204...) custom-call(f32[256,2048]{1,0:T(8,128)} %convert_add_fusion.middle_ref, f32[1,2048]{1,0:T(1,128)} %bitcast.60, ...), custom_call_target="tpu_custom_call" | custom-call | flops 57982058496 | bytes 37748736 | tf_op jit(solution)/shard_map/pallas_call | solution.py:617
  434.2 77.8 %all-gather.8.cloned.1.call-done = bf16[1024,2048]{1,0:T(8,128)(2,1)} async-done(((bf16[256,2048]{1,0:T(8,128)(2,1)}), bf16[1024,2048]{1,0:T(8,128)(2,1)}) %all-gather.8.cloned.1.call-update) | async-done | bytes 4194320 | tf_op jit(solution)/shard_map/all_gather | solution.py:712
  512.0 7.0 convolution_convert_fusion.1
  519.1 7.2 fusion.16.dm_ref
  526.3 32.0 %shard_map.324 = (bf16[1024,640]{1,0:T(8,128)(2,1)}, bf16[1024,640]{1,0:T(8,128)(2,1)}, f32[640,640]{1,0:T(8,128)}, f32[640,640]{1,0:T(8,128)}, f32[8,640]{1,0:T(8,128)}) custom-call(f32[1024,640]{1,0:T(8,128)} %fusion.16.dm_ref, f32[1024,640]{1,0:T(8,128)} %fusion.14.vp_in, f32[1024,640]{1,0:T(8,128)} %fusion.15.gp_ref, ...), custom_call_target="tpu_custom_call" | custom-call | flops 3355443200 | bytes 26214400 | tf_op jit(solution)/shard_map/pallas_call | solution.py:295
  558.3 7.7 convolution_convert_fusion.3
  566.1 7.6 convolution_convert_fusion.2
  573.7 5.7 fusion.17
  579.5 5.4 add_convert_fusion
  585.5 24.3 %psum.50 = f32[8,640]{1,0:T(8,128)S(1)} all-reduce(f32[8,640]{1,0:T(8,128)S(1)} %copy-done.6), channel_id=1, replica_groups=mesh['dp'=8,'mp'=4] {'dp'}, use_global_device_ids=true, to_apply=%region_11.12 | all-reduce | flops 5120 | bytes 40960 | tf_op jit(solution)/shard_map/psum | solution.py:724
  619.0 36.1 %reduce-scatter.26.cloned.1.call-done = bf16[1536,256]{1,0:T(8,128)(2,1)} async-done(((bf16[1536,2048]{1,0:T(8,128)(2,1)}), bf16[1536,256]{1,0:T(8,128)(2,1)}) %reduce-scatter.26.cloned.1.call-update) | async-done | bytes 786448 | tf_op jit(solution)/shard_map/reduce_scatter | solution.py:668
  657.5 63.1 %reduce-scatter.24.cloned.1.call-done = bf16[256,1536]{1,0:T(8,128)(2,1)} async-done(((bf16[2048,1536]{1,0:T(8,128)(2,1)}), bf16[256,1536]{1,0:T(8,128)(2,1)}) %reduce-scatter.24.cloned.1.call-update) | async-done | bytes 786448 | tf_op jit(solution)/shard_map/reduce_scatter | solution.py:668
  723.1 62.7 %reduce-scatter.22.cloned.1.call-done = bf16[256,1536]{1,0:T(8,128)(2,1)} async-done(((bf16[2048,1536]{1,0:T(8,128)(2,1)}), bf16[256,1536]{1,0:T(8,128)(2,1)}) %reduce-scatter.22.cloned.1.call-update) | async-done | bytes 786448 | tf_op jit(solution)/shard_map/reduce_scatter | solution.py:668
  788.2 44.9 %reduce-scatter.20.cloned.1.call-done = bf16[640,256]{1,0:T(8,128)(2,1)} async-done(((bf16[640,2048]{1,0:T(8,128)(2,1)}), bf16[640,256]{1,0:T(8,128)(2,1)}) %reduce-scatter.20.cloned.1.call-update) | async-done | bytes 327696 | tf_op jit(solution)/shard_map/reduce_scatter | solution.py:668
  835.0 45.4 %reduce-scatter.16.cloned.1.call-done = bf16[256,640]{1,0:T(8,128)(2,1)} async-done(((bf16[2048,640]{1,0:T(8,128)(2,1)}), bf16[256,640]{1,0:T(8,128)(2,1)}) %reduce-scatter.16.cloned.1.call-update) | async-done | bytes 327696 | tf_op jit(solution)/shard_map/reduce_scatter | solution.py:668
  882.2 45.5 %reduce-scatter.18.cloned.1.call-done = bf16[256,640]{1,0:T(8,128)(2,1)} async-done(((bf16[2048,640]{1,0:T(8,128)(2,1)}), bf16[256,640]{1,0:T(8,128)(2,1)}) %reduce-scatter.18.cloned.1.call-update) | async-done | bytes 327696 | tf_op jit(solution)/shard_map/reduce_scatter | solution.py:668
  929.6 77.2 %reduce-scatter.14.cloned.1.call-done = bf16[256,2048]{1,0:T(8,128)(2,1)} async-done(((bf16[1024,2048]{1,0:T(8,128)(2,1)}), bf16[256,2048]{1,0:T(8,128)(2,1)}) %reduce-scatter.14.cloned.1.call-update) | async-done | bytes 1048592 | tf_op jit(solution)/shard_map/reduce_scatter | solution.py:664
  1006.8 2.7 fusion.4
  1009.5 4.9 fusion.3
  1017.2 41.2 %all-reduce.1 = (f32[2048]{0:T(1024)}, f32[2048]{0:T(1024)}, f32[3]{0:T(128)S(1)}, f32[]{:T(128)}) all-reduce(f32[2048]{0:T(1024)S(1)} %get-tuple-element.50, f32[2048]{0:T(1024)S(1)} %bitcast.56, f32[3]{0:T(128)S(1)} %pad_maximum_fusion.2, f32[]{:T(128)} %get-tuple-element.56), channel_id=1, replica_groups=mesh['dp'=8,'mp'=4] {'dp','mp'}, use_global_device_ids=true, to_apply=%region_8.9 | all-reduce | flops 4100 | bytes 32800 | tf_op jit(solution)/shard_map/psum | solution.py:726
  1059.5 10.2 all-reduce.5.cloned.1.call-done
  (102 shorter events, 42.6 us)
Async XLA Ops:
  7.2 125.6 %copy-start = (bf16[640,2048]{1,0:T(8,128)(2,1)S(1)}, bf16[640,2048]{1,0:T(8,128)(2,1)}, u32[]{:S(2)}) copy-start(bf16[640,2048]{1,0:T(8,128)(2,1)} %param.33) | copy-start | bytes 7864324
  7.2 4.4 copy-start.10
  7.2 4.4 copy-start.11
  7.2 4.4 copy-start.12
  7.2 4.4 copy-start.7
  7.2 4.4 copy-start.4
  7.3 87.9 %all-gather.4.cloned.1.call-start = ((), (), s32[]{:S(2)}) async-start(), calls=%async_computation.9 | async-start | bytes 5242880 | tf_op jit(solution)/shard_map/all_gather | solution.py:678
  11.5 203.1 %reduce-scatter.10.cloned.1.call-start = ((), (), s32[]{:S(2)}) async-start(), calls=%async_computation.10 | async-start | bytes 5242880 | tf_op jit(solution)/shard_map/reduce_scatter | solution.py:664
  15.3 5.6 copy-start.14
  15.3 5.8 copy-start.8
  95.1 8.0 copy-start.15
  95.1 8.0 copy-start.16
  139.2 158.4 %all-gather.6.cloned.1.call-start = ((), (), s32[]{:S(2)}) async-start(), calls=%async_computation.11 | async-start | bytes 5242880 | tf_op jit(solution)/shard_map/all_gather | solution.py:696
  139.9 372.1 %all-gather.8.cloned.1.call-start = ((), (), s32[]{:S(2)}) async-start(), calls=%async_computation.13 | async-start | bytes 5242880 | tf_op jit(solution)/shard_map/all_gather | solution.py:712
  431.5 183.9 %reduce-scatter.12.cloned.1.call-start = ((), (), s32[]{:S(2)}) async-start(), calls=%async_computation.12 | async-start | bytes 5242880 | tf_op jit(solution)/shard_map/reduce_scatter | solution.py:702
  432.1 223.1 %reduce-scatter.26.cloned.1.call-start = ((), (), s32[]{:S(2)}) async-start(), calls=%async_computation.20 | async-start | bytes 7077888 | tf_op jit(solution)/shard_map/reduce_scatter | solution.py:668
  432.6 288.0 %reduce-scatter.24.cloned.1.call-start = ((), (), s32[]{:S(2)}) async-start(), calls=%async_computation.19 | async-start | bytes 7077888 | tf_op jit(solution)/shard_map/reduce_scatter | solution.py:668
  433.4 352.4 %reduce-scatter.22.cloned.1.call-start = ((), (), s32[]{:S(2)}) async-start(), calls=%async_computation.18 | async-start | bytes 7077888 | tf_op jit(solution)/shard_map/reduce_scatter | solution.py:668
  434.1 399.0 %reduce-scatter.20.cloned.1.call-start = ((), (), s32[]{:S(2)}) async-start(), calls=%async_computation.17 | async-start | bytes 2949120 | tf_op jit(solution)/shard_map/reduce_scatter | solution.py:668
  519.1 361.3 %reduce-scatter.16.cloned.1.call-start = ((), (), s32[]{:S(2)}) async-start(), calls=%async_computation.15 | async-start | bytes 2949120 | tf_op jit(solution)/shard_map/reduce_scatter | solution.py:668
  566.0 361.7 %reduce-scatter.18.cloned.1.call-start = ((), (), s32[]{:S(2)}) async-start(), calls=%async_computation.16 | async-start | bytes 2949120 | tf_op jit(solution)/shard_map/reduce_scatter | solution.py:668
  573.6 433.1 %reduce-scatter.14.cloned.1.call-start = ((), (), s32[]{:S(2)}) async-start(), calls=%async_computation.14 | async-start | bytes 5242880 | tf_op jit(solution)/shard_map/reduce_scatter | solution.py:664
  573.7 5.8 copy-start.17
  573.7 5.8 copy-start.18
  584.8 0.7 copy-start.6
  584.8 484.9 %all-reduce.5.cloned.1.call-start = ((), (), s32[]{:S(2)}) async-start(), calls=%async_computation.21 | async-start | bytes 2621440 | tf_op jit(solution)/shard_map/psum | solution.py:724
  616.9 1.9 copy-start.3
  723.1 283.7 %copy-start.5 = (f32[2048]{0:T(1024)S(1)}, f32[2048]{0:T(1024)}, u32[]{:S(2)}) copy-start(f32[2048]{0:T(1024)} %param.23) | copy-start | bytes 24580
  1006.8 2.7 copy-start.1
  1006.8 2.7 copy-start.2
  1009.5 4.9 copy-start.13
  1009.5 7.6 copy-start.9
Sparse Core Ops, SparseCore 0:
  11.6 83.4 all-gather.3
  139.3 75.2 reduce-scatter.9
  216.3 81.2 all-gather.5
  431.6 80.3 all-gather.7
  514.3 75.2 reduce-scatter.11
  592.8 62.2 reduce-scatter.25
  658.9 61.7 reduce-scatter.23
  724.0 61.7 reduce-scatter.21
  789.4 43.6 reduce-scatter.19
  836.7 43.6 reduce-scatter.15
  884.1 43.6 reduce-scatter.17
  930.0 76.7 reduce-scatter.13
  1011.1 58.5 all-reduce.4

commit v3 on v2

--- a/solution.py
+++ b/solution.py
@@ -22,14 +22,6 @@
     before = (doc_ends[None, :] <= positions[:, None]).astype(jnp.int32)
     starts = jnp.sum(before * lengths_row[None, :], axis=1)
     return positions - starts
-
-
-def scaled_norm(values, gain_vec):
-    return (
-        values
-        * lax.rsqrt(jnp.mean(values * values, axis=1, keepdims=True) + EPS)
-        * gain_vec[None, :]
-    )
 
 
 def dot_nn(left, right):
@@ -97,39 +89,36 @@
 V_BIAS, V_RATE, V_INLET, V_DECAY = 4, 5, 6, 7
 
 
-def rec_forward(rows, vp_ref, gp_ref, mask_ref, vec_ref, rate_ref, inlet_ref,
-                mixed_ref, state_ref, conv_ref, forget_ref, input_ref, low_ref):
+def fold(values, columns):
+    return jnp.sum(values.reshape(values.shape[0] // 8, 8, columns), axis=0)
+
+
+def rec_forward(base, rows, vp_ref, gp_ref, mask_ref, vec_ref, rate_ref, inlet_ref,
+                mixed_ref, state_ref, conv_ref, forget_ref, input_ref, low_ref, carry_ref):
     bias = vec_ref[V_BIAS:V_BIAS + 1, :]
 
     def conv_step(index, unused):
-        base = pl.multiple_of(index * CHUNK, CHUNK)
-        ext = vp_ref[pl.ds(base, CHUNK + 8), :]
-        masks = mask_ref[pl.ds(base, CHUNK), :]
+        at = pl.multiple_of(base + index * CHUNK, CHUNK)
+        ext = vp_ref[pl.ds(at, CHUNK + 8), :]
+        masks = mask_ref[pl.ds(at, CHUNK), :]
         total = bias + vec_ref[0:1, :] * ext[8:8 + CHUNK, :]
         for tap in (1, 2, 3):
             total = total + (masks[:, tap:tap + 1] * ext[8 - tap:8 - tap + CHUNK, :]) * vec_ref[tap:tap + 1, :]
-        conv_ref[pl.ds(base, CHUNK), :] = total
-        low_ref[pl.ds(base, CHUNK), :] = total.astype(BF)
+        conv_ref[pl.ds(at, CHUNK), :] = total
+        low_ref[pl.ds(pl.multiple_of(index * CHUNK, CHUNK), CHUNK), :] = total.astype(BF)
         return unused
 
     lax.fori_loop(0, rows // CHUNK, conv_step, 0)
-    block = 256
-
-    def gate_step(index, unused):
-        base = pl.multiple_of(index * block, block)
-        low = low_ref[pl.ds(base, block), :]
-        forget_ref[pl.ds(base, block), :] = dot_nn(low, rate_ref[...])
-        input_ref[pl.ds(base, block), :] = dot_nn(low, inlet_ref[...])
-        return unused
-
-    lax.fori_loop(0, rows // block, gate_step, 0)
+    block = pl.ds(pl.multiple_of(base, rows), rows)
+    forget_ref[block, :] = dot_nn(low_ref[...], rate_ref[...])
+    input_ref[block, :] = dot_nn(low_ref[...], inlet_ref[...])
     rate_bias = vec_ref[V_RATE:V_RATE + 1, :]
     inlet_bias = vec_ref[V_INLET:V_INLET + 1, :]
     decay = vec_ref[V_DECAY:V_DECAY + 1, :]
 
     def scan_step(index, carry):
-        base = pl.multiple_of(index * CHUNK, CHUNK)
-        window = pl.ds(base, CHUNK)
+        at = pl.multiple_of(base + index * CHUNK, CHUNK)
+        window = pl.ds(at, CHUNK)
         forget = sigmoid(forget_ref[window, :] + rate_bias)
         inlet = sigmoid(input_ref[window, :] + inlet_bias)
         log_decay = decay * forget
@@ -146,35 +135,35 @@
             carry = states[7:8, :]
             pieces.append(states)
         states = jnp.concatenate(pieces, axis=0)
-        state_ref[window, :] = states
+        state_ref[pl.ds(at + 8, CHUNK), :] = states
         mixed_ref[window, :] = (states * gelu(gp_ref[window, :])).astype(BF)
         return carry
 
-    lax.fori_loop(0, rows // CHUNK, scan_step, jnp.zeros((1, conv_ref.shape[1]), F32))
-
-
-def rec_backward(rows, dm_ref, vp_ref, gp_ref, mask_ref, vec_ref, rate_ref, inlet_ref,
+    carry_ref[0:1, :] = lax.fori_loop(0, rows // CHUNK, scan_step, carry_ref[0:1, :])
+
+
+def rec_backward(base, rows, dm_ref, vp_ref, gp_ref, mask_ref, vec_ref, rate_ref, inlet_ref,
                  state_ref, conv_ref, forget_ref, input_ref,
-                 vlow_ref, glow_ref, dzf_ref, dzi_ref, dconv_ref, clow_ref, sums_ref):
+                 vlow_ref, glow_ref, dzf_ref, dzi_ref, dconv_ref, clow_ref, sums_ref, carry_ref):
     columns = conv_ref.shape[1]
     decay = vec_ref[V_DECAY:V_DECAY + 1, :]
     chunks = rows // CHUNK
-    zero_row = jnp.zeros((1, columns), F32)
 
     def scan_step(step, carry):
         grad_next, mult_next, rate_sum, inlet_sum, decay_sum = carry
-        base = pl.multiple_of((chunks - 1 - step) * CHUNK, CHUNK)
-        window = pl.ds(base, CHUNK)
-        mixed_grad = dm_ref[window, :]
-        act, slope = gelu_both(gp_ref[window, :])
-        ext = state_ref[pl.ds(base, CHUNK + 8), :]
+        low = pl.multiple_of((chunks - 1 - step) * CHUNK, CHUNK)
+        here = pl.ds(low, CHUNK)
+        window = pl.ds(pl.multiple_of(base + low, CHUNK), CHUNK)
+        mixed_grad = dm_ref[here, :]
+        act, slope = gelu_both(gp_ref[here, :])
+        ext = state_ref[pl.ds(low, CHUNK + 8), :]
         states = ext[8:, :]
         before = ext[7:7 + CHUNK, :]
         glow_ref[window, :] = (mixed_grad * states * slope).astype(BF)
         add = mixed_grad * act
-        forget = forget_ref[window, :]
-        inlet = input_ref[window, :]
-        conv = conv_ref[window, :]
+        forget = forget_ref[here, :]
+        inlet = input_ref[here, :]
+        conv = conv_ref[here, :]
         clow_ref[window, :] = conv.astype(BF)
         log_decay = decay * forget
         carried = jnp.exp(log_decay)
@@ -194,40 +183,31 @@
         grads = jnp.concatenate(pieces[::-1], axis=0)
         gated = grads * inlet
         d_log = grads * before * mult - gated * conv * ((1.0 - square) * inverse)
-        d_forget = d_log * decay
-        dzf = d_forget * forget * (1.0 - forget)
+        dzf = d_log * decay * forget * (1.0 - forget)
         dzi = grads * normalizer * conv * inlet * (1.0 - inlet)
         dzf_ref[window, :] = dzf.astype(BF)
         dzi_ref[window, :] = dzi.astype(BF)
-        dconv_ref[window, :] = gated * normalizer
-        return (grad_next, mult[0:1, :],
-                rate_sum + jnp.sum(dzf.reshape(CHUNK // 8, 8, columns), axis=0),
-                inlet_sum + jnp.sum(dzi.reshape(CHUNK // 8, 8, columns), axis=0),
-                decay_sum + jnp.sum((d_log * forget).reshape(CHUNK // 8, 8, columns), axis=0))
-
-    zeros = jnp.zeros((8, columns), F32)
-    unused, unused, rate_sum, inlet_sum, decay_sum = lax.fori_loop(
-        0, chunks, scan_step, (zero_row, zero_row, zeros, zeros, zeros))
-    sums_ref[V_RATE:V_RATE + 1, :] = jnp.sum(rate_sum, axis=0, keepdims=True)
-    sums_ref[V_INLET:V_INLET + 1, :] = jnp.sum(inlet_sum, axis=0, keepdims=True)
-    sums_ref[V_DECAY:V_DECAY + 1, :] = jnp.sum(decay_sum, axis=0, keepdims=True)
-    block = 256
-
-    def gate_step(index, unused):
-        base = pl.multiple_of(index * block, block)
-        window = pl.ds(base, block)
-        dconv_ref[window, :] += (dot_nt(dzf_ref[window, :], rate_ref[...])
-                                 + dot_nt(dzi_ref[window, :], inlet_ref[...]))
-        return unused
-
-    lax.fori_loop(0, rows // block, gate_step, 0)
+        dconv_ref[here, :] = gated * normalizer
+        return (grad_next, mult[0:1, :], rate_sum + fold(dzf, columns), inlet_sum + fold(dzi, columns),
+                decay_sum + fold(d_log * forget, columns))
+
+    grad_next, mult_next, rate_sum, inlet_sum, decay_sum = lax.fori_loop(
+        0, chunks, scan_step,
+        (carry_ref[0:1, :], carry_ref[1:2, :], sums_ref[V_RATE], sums_ref[V_INLET], sums_ref[V_DECAY]))
+    carry_ref[0:1, :] = grad_next
+    carry_ref[1:2, :] = mult_next
+    sums_ref[V_RATE] = rate_sum
+    sums_ref[V_INLET] = inlet_sum
+    sums_ref[V_DECAY] = decay_sum
+    block = pl.ds(pl.multiple_of(base, rows), rows)
+    dconv_ref[0:rows, :] += dot_nt(dzf_ref[block, :], rate_ref[...]) + dot_nt(dzi_ref[block, :], inlet_ref[...])
 
     def conv_step(index, carry):
-        base = pl.multiple_of(index * CHUNK, CHUNK)
-        window = pl.ds(base, CHUNK)
-        ext = dconv_ref[pl.ds(base, CHUNK + 8), :]
-        masks = mask_ref[pl.ds(base, CHUNK + 8), :]
-        values = vp_ref[pl.ds(base, CHUNK + 8), :]
+        low = pl.multiple_of(index * CHUNK, CHUNK)
+        at = pl.multiple_of(base + low, CHUNK)
+        ext = dconv_ref[pl.ds(low, CHUNK + 8), :]
+        masks = mask_ref[pl.ds(at, CHUNK + 8), :]
+        values = vp_ref[pl.ds(low, CHUNK + 8), :]
         here = ext[:CHUNK, :]
         total = vec_ref[0:1, :] * here
         sums = [carry[0] + fold(here * values[8:, :], columns)]
@@ -236,104 +216,135 @@
             total = total + vec_ref[tap:tap + 1, :] * gated[tap:tap + CHUNK, :]
             sums.append(carry[tap] + fold(gated[:CHUNK, :] * values[8 - tap:8 - tap + CHUNK, :], columns))
         sums.append(carry[4] + fold(here, columns))
-        vlow_ref[window, :] = total.astype(BF)
+        vlow_ref[pl.ds(at, CHUNK), :] = total.astype(BF)
         return tuple(sums)
 
-    sums = lax.fori_loop(0, chunks, conv_step, (zeros,) * 5)
+    sums = lax.fori_loop(0, chunks, conv_step, tuple(sums_ref[row] for row in range(5)))
     for row in range(5):
-        sums_ref[row:row + 1, :] = jnp.sum(sums[row], axis=0, keepdims=True)
-
-
-def fold(values, columns):
-    return jnp.sum(values.reshape(CHUNK // 8, 8, columns), axis=0)
-
-
-def forward_kernel(vp_in, gp_ref, mask_ref, vec_ref, rate_ref, inlet_ref,
-                   mixed_ref, state_ref, conv_ref, forget_ref, input_ref, vp_ref, low_ref):
-    rows, columns = vp_in.shape
-    vp_ref[0:8, :] = jnp.zeros((8, columns), F32)
-    vp_ref[8:, :] = vp_in[...]
-    rec_forward(rows, vp_ref, gp_ref, mask_ref, vec_ref, rate_ref, inlet_ref,
-                mixed_ref, state_ref, conv_ref, forget_ref, input_ref, low_ref)
-
-
-def backward_kernel(dm_ref, vp_in, gp_ref, mask_ref, vec_ref, rate_ref, inlet_ref,
-                    state_in, conv_ref, forget_ref, input_ref,
-                    vlow_ref, glow_ref, rate_grad_ref, inlet_grad_ref, sums_ref,
-                    vp_ref, state_ref, dzf_ref, dzi_ref, dconv_ref, clow_ref):
-    rows, columns = vp_in.shape
-    zeros = jnp.zeros((8, columns), F32)
-    vp_ref[0:8, :] = zeros
-    vp_ref[8:, :] = vp_in[...]
-    state_ref[0:8, :] = zeros
-    state_ref[8:, :] = state_in[...]
-    dconv_ref[rows:rows + 8, :] = zeros
-    rec_backward(rows, dm_ref, vp_ref, gp_ref, mask_ref, vec_ref, rate_ref, inlet_ref,
-                 state_ref, conv_ref, forget_ref, input_ref,
-                 vlow_ref, glow_ref, dzf_ref, dzi_ref, dconv_ref, clow_ref, sums_ref)
-    rate_grad_ref[...] = dot_tn(clow_ref[...], dzf_ref[...])
-    inlet_grad_ref[...] = dot_tn(clow_ref[...], dzi_ref[...])
-
-
-def call_forward(vp, gp, masks, vec, rate, inlet):
-    rows, columns = vp.shape
-    wide = jax.ShapeDtypeStruct((rows, columns), F32)
-    return pl.pallas_call(
-        forward_kernel,
-        out_shape=(jax.ShapeDtypeStruct((rows, columns), BF), wide, wide, wide, wide),
-        scratch_shapes=[pltpu.VMEM((rows + 8, columns), F32), pltpu.VMEM((rows, columns), BF)],
-        compiler_params=pltpu.CompilerParams(vmem_limit_bytes=VMEM_LIMIT),
-        cost_estimate=pl.CostEstimate(flops=4 * rows * columns * columns,
-                                      bytes_accessed=30 * rows * columns, transcendentals=6 * rows * columns),
-    )(vp, gp, masks, vec, rate, inlet)
-
-
-def call_backward(dm, vp, gp, masks, vec, rate, inlet, state, conv, forget, inp):
-    rows, columns = vp.shape
-    low = jax.ShapeDtypeStruct((rows, columns), BF)
-    square = jax.ShapeDtypeStruct((columns, columns), F32)
-    return pl.pallas_call(
-        backward_kernel,
-        out_shape=(low, low, square, square, jax.ShapeDtypeStruct((8, columns), F32)),
-        scratch_shapes=[
-            pltpu.VMEM((rows + 8, columns), F32),
-            pltpu.VMEM((rows + 8, columns), F32),
-            pltpu.VMEM((rows, columns), BF),
-            pltpu.VMEM((rows, columns), BF),
-            pltpu.VMEM((rows + 8, columns), F32),
-            pltpu.VMEM((rows, columns), BF),
-        ],
-        compiler_params=pltpu.CompilerParams(vmem_limit_bytes=VMEM_LIMIT),
-        cost_estimate=pl.CostEstimate(flops=8 * rows * columns * columns,
-                                      bytes_accessed=40 * rows * columns, transcendentals=4 * rows * columns),
-    )(dm, vp, gp, masks, vec, rate, inlet, state, conv, forget, inp)
+        sums_ref[row] = sums[row]
+    dconv_ref[rows:rows + 8, :] = dconv_ref[0:8, :]
 
 
 MESH = pl.DeviceIdType.MESH
 PARTS = 4
 
 
-def greet(axis, count):
-    me = lax.axis_index(axis)
+IN_VMEM = pl.BlockSpec(memory_space=pltpu.VMEM)
+ANYWHERE = pl.BlockSpec(memory_space=pl.ANY)
+DMA = pltpu.SemaphoreType.DMA
+
+
+def greet(count, groups=1):
+    me = lax.axis_index("mp")
     barrier = pltpu.get_barrier_semaphore()
 
     @pl.when(me > 0)
     def _():
-        pl.semaphore_signal(barrier, inc=1, device_id={axis: me - 1}, device_id_type=MESH)
+        pl.semaphore_signal(barrier, inc=1, device_id={"mp": me - 1}, device_id_type=MESH)
 
     @pl.when(me < count - 1)
     def _():
-        pl.semaphore_signal(barrier, inc=1, device_id={axis: me + 1}, device_id_type=MESH)
-
+        pl.semaphore_signal(barrier, inc=1, device_id={"mp": me + 1}, device_id_type=MESH)
+
+    levels = groups.bit_length() - 1
+    for bit in range(levels):
+        pl.semaphore_signal(barrier, inc=1, device_id={"dp": partner_of(bit)}, device_id_type=MESH)
     inner = (me > 0) & (me < count - 1)
 
     @pl.when(inner)
     def _():
-        pl.semaphore_wait(barrier, 2)
+        pl.semaphore_wait(barrier, 2 + levels)
 
     @pl.when(jnp.logical_not(inner))
     def _():
-        pl.semaphore_wait(barrier, 1)
+        pl.semaphore_wait(barrier, 1 + levels)
+
+
+def bit_of(value, bit):
+    return (value // (1 << bit)) % 2
+
+
+def partner_of(bit):
+    me = lax.axis_index("dp")
+    return me + (1 << bit) * (1 - 2 * bit_of(me, bit))
+
+
+class Cube:
+    def __init__(self, count, order, held, slots, send, recv):
+        self.count, self.order, self.held, self.slots, self.send, self.recv = count, order, held, slots, send, recv
+        self.me = lax.axis_index("dp")
+
+    def places(self, level):
+        total = self.count >> (level + 1)
+        start = self.count - (self.count >> level)
+        return [(index, start + index) for index in range(total)]
+
+    def chunk(self, level, index, mine):
+        at = 0
+        for rank, bit in enumerate(self.order):
+            own = bit_of(self.me, bit)
+            if rank < level:
+                at = at + own * (1 << bit)
+            elif rank == level:
+                at = at + (own if mine else 1 - own) * (1 << bit)
+            else:
+                at = at + ((index >> (rank - level - 1)) & 1) * (1 << bit)
+        return at
+
+    def copy(self, level, index, slot):
+        return pltpu.make_async_remote_copy(
+            src_ref=self.held.at[self.chunk(level, index, False)],
+            dst_ref=self.slots.at[slot],
+            send_sem=self.send.at[slot],
+            recv_sem=self.recv.at[slot],
+            device_id={"dp": partner_of(self.order[level])},
+            device_id_type=MESH,
+        )
+
+    def start(self, level):
+        for index, slot in self.places(level):
+            self.copy(level, index, slot).start()
+
+    def finish(self, level):
+        for index, slot in self.places(level):
+            self.copy(level, index, slot).wait()
+            chunk = self.chunk(level, index, True)
+            if level < len(self.order) - 1:
+                self.held[chunk] = (
+                    self.held[chunk].astype(F32) + self.slots[slot].astype(F32)).astype(self.held.dtype)
+
+    def result(self):
+        return self.held[self.me].astype(F32) + self.slots[self.count - 2].astype(F32)
+
+
+class Spread:
+    def __init__(self, cube, full, send, recv):
+        self.cube, self.full, self.send, self.recv = cube, full, send, recv
+
+    def copy(self, level, index, slot, mine=True):
+        chunk = self.cube.chunk(level, index, mine)
+        return pltpu.make_async_remote_copy(
+            src_ref=self.full.at[chunk],
+            dst_ref=self.full.at[chunk],
+            send_sem=self.send.at[slot],
+            recv_sem=self.recv.at[slot],
+            device_id={"dp": partner_of(self.cube.order[level])},
+            device_id_type=MESH,
+        )
+
+    def start(self, level):
+        for index, slot in self.cube.places(level):
+            self.copy(level, index, slot).start()
+
+    def finish(self, level):
+        for index, slot in self.cube.places(level):
+            self.copy(level, index, slot).wait_send()
+            self.copy(level, index, slot, False).wait_recv()
+
+
+def orders(groups):
+    bits = list(range(groups.bit_length() - 1))
+    return bits, bits[:1] + bits[:0:-1]
 
 
 class Gather:
@@ -396,6 +407,9 @@
             device_id_type=MESH,
         )
 
+    def times(self):
+        return range(1, 2 * self.count - 3)
+
     def first(self, block, part):
         pl.when((self.me == 0) & (block > 0))(self.copy(block, part, 1).start)
         pl.when((self.me == self.count - 1) & (block < self.count - 1))(self.copy(block, part, -1).start)
@@ -418,10 +432,10 @@
             device_id_type=MESH,
         ).wait_recv()
 
-    def pass_on(self, time):
+    def pass_on(self, time, up_near, down_near):
         last = self.count - 1
-        up = time + 1 - self.me
-        down = last - 1 + last - self.me - time
+        up = time + 1 - self.me if up_near else last + self.me - time
+        down = 2 * last - 1 - self.me - time if down_near else time - last + self.me
         up_here = (self.me > 0) & (up > self.me) & (up <= last)
         down_here = (self.me < last) & (down < self.me) & (down >= 0)
 
@@ -432,9 +446,11 @@
 
         lax.fori_loop(0, PARTS, step, 0)
 
-    def total(self, part):
+    def wait_total(self, part):
         pl.when(self.me > 0)(lambda: self.arrived(self.me, part, 1))
         pl.when(self.me < self.count - 1)(lambda: self.arrived(self.me, part, -1))
+
+    def total(self, part):
         below = jnp.where(self.me > 0, self.slots[self.me + 1, part].astype(F32), 0.0)
         above = jnp.where(self.me < self.count - 1, self.slots[self.me, part].astype(F32), 0.0)
         return self.held[self.me, part].astype(F32) + below + above
@@ -447,6 +463,496 @@
             return unused
 
         lax.fori_loop(0, self.count, step, 0)
+
+
+def norm_rows(source_ref, gain_ref, target_ref):
+    step_rows = 64
+
+    def step(index, unused):
+        window = pl.ds(pl.multiple_of(index * step_rows, step_rows), step_rows)
+        values = source_ref[window, :].astype(F32)
+        scale = lax.rsqrt(jnp.mean(values * values, axis=1, keepdims=True) + EPS)
+        target_ref[window, :] = (values * scale * gain_ref[...]).astype(BF)
+        return unused
+
+    lax.fori_loop(0, source_ref.shape[0] // step_rows, step, 0)
+
+
+def norm_back(values_ref, gain_ref, scatter, gain_grad_ref, write):
+    rows, columns = values_ref.shape
+    width = columns // PARTS
+    dot_sum = jnp.zeros((rows, 1), F32)
+    square_sum = jnp.zeros((rows, 1), F32)
+    for part in range(PARTS):
+        span = slice(part * width, (part + 1) * width)
+        scatter.wait_total(part)
+        grad = scatter.total(part)
+        values = values_ref[:, span].astype(F32)
+        dot_sum = dot_sum + jnp.sum(grad * gain_ref[:, span] * values, axis=1, keepdims=True)
+        square_sum = square_sum + jnp.sum(values * values, axis=1, keepdims=True)
+    scale = lax.rsqrt(square_sum * (1.0 / columns) + EPS)
+    pull = scale * scale * scale * (dot_sum * (1.0 / columns))
+    for part in range(PARTS):
+        span = slice(part * width, (part + 1) * width)
+        grad = scatter.total(part)
+        values = values_ref[:, span].astype(F32)
+        gain_grad_ref[:, span] = jnp.sum(grad * values * scale, axis=0, keepdims=True)
+        write(span, scale * (grad * gain_ref[:, span]) - values * pull)
+
+
+def live_squares(live_ref, row_sums, stat_ref):
+    stat_ref[...] = jnp.zeros(stat_ref.shape, F32) + jnp.sum(live_ref[...] * row_sums, axis=0, keepdims=True)
+
+
+def mixer_kernel(count, tokens_ref, gain_ref, live_ref, mask_ref, vec_ref, rate_ref, inlet_ref,
+                 cot_hbm, value_hbm, gate_hbm, out_hbm,
+                 middle_ref, stat_ref, normed_all, cot_all, mixed_out, vp_out, gp_out, state_out, conv_out,
+                 forget_out, input_out,
+                 normed, value_w, gate_w, out_w, vp, gp, mixed, state, conv, forget, inlet_gate, low, carry, held,
+                 slots, load_sem, own_sem, out_sem, block_sem, ag_send, ag_recv, cot_send, cot_recv, rs_send, rs_recv):
+    me = lax.axis_index("mp")
+    rows, columns = tokens_ref.shape
+    channels = value_w.shape[1]
+    width = columns // PARTS
+    own_copy = pltpu.make_async_copy(cot_hbm, cot_all.at[me], own_sem)
+    own_copy.start()
+    loads = [pltpu.make_async_copy(source, target, load_sem.at[index]) for index, (source, target) in enumerate(
+        ((value_hbm, value_w), (gate_hbm, gate_w), (out_hbm, out_w)))]
+    for load in loads:
+        load.start()
+    norm_rows(tokens_ref, gain_ref, normed.at[me])
+    greet(count)
+    gather = Gather(count, normed, ag_send, ag_recv)
+    cots = Gather(count, cot_all, cot_send, cot_recv)
+    scatter = Scatter(count, held, slots, rs_send, rs_recv)
+    gather.start()
+    zeros = jnp.zeros((8, channels), F32)
+    vp[0:8, :] = zeros
+    state[0:8, :] = zeros
+    carry[...] = zeros
+    own_copy.wait()
+    for load in loads:
+        load.wait()
+
+    def block_copy(block):
+        return pltpu.make_async_copy(normed.at[block], normed_all.at[block], block_sem.at[block])
+
+    def project(block):
+        block_copy(block).start()
+        rows_in = normed[block]
+        vp[pl.ds(pl.multiple_of(block * rows + 8, 8), rows), :] = dot_nn(rows_in, value_w[...])
+        gp[pl.ds(pl.multiple_of(block * rows, rows), rows), :] = dot_nn(rows_in, gate_w[...])
+
+    def arrive(distance, unused):
+        pl.when(distance > 0)(lambda: gather.take(distance))
+
+        def side(which, inner):
+            block = me - distance + 2 * distance * which
+            pl.when((block >= 0) & (block < count) & ((distance > 0) | (which == 0)))(lambda: project(block))
+            return inner
+
+        return lax.fori_loop(0, 2, side, unused)
+
+    lax.fori_loop(0, count, arrive, 0)
+    cots.start()
+
+    def mix(block, unused):
+        base = block * rows
+        rec_forward(base, rows, vp, gp, mask_ref, vec_ref, rate_ref, inlet_ref,
+                    mixed, state, conv, forget, inlet_gate, low, carry)
+        rows_in = mixed[pl.ds(pl.multiple_of(base, rows), rows), :]
+        for part in range(PARTS):
+            held[block, part] = dot_nn(rows_in, out_w[:, part * width:(part + 1) * width]).astype(BF)
+            scatter.first(block, part)
+        return unused
+
+    lax.fori_loop(0, count, mix, 0)
+    saves = [pltpu.make_async_copy(source, target, out_sem.at[index]) for index, (source, target) in enumerate(
+        ((mixed, mixed_out), (vp, vp_out), (gp, gp_out), (state, state_out), (conv, conv_out),
+         (forget, forget_out), (inlet_gate, input_out)))]
+    for save in saves:
+        save.start()
+    taken = 1
+    for time in scatter.times():
+        if taken < count and time >= 2 * taken - 1:
+            cots.take(taken)
+            taken += 1
+        scatter.pass_on(time, True, False)
+    for distance in range(taken, count):
+        cots.take(distance)
+    row_sums = jnp.zeros((rows, 1), F32)
+    for part in range(PARTS):
+        span = slice(part * width, (part + 1) * width)
+        scatter.wait_total(part)
+        total = scatter.total(part)
+        row_sums = row_sums + jnp.sum(total * total, axis=1, keepdims=True)
+        middle_ref[:, span] = tokens_ref[:, span].astype(F32) + total
+    live_squares(live_ref, row_sums, stat_ref)
+    for save in saves:
+        save.wait()
+    for block in range(count):
+        block_copy(block).wait()
+    gather.drain()
+    cots.drain()
+    scatter.drain()
+
+
+def call_mixer(count, tokens, gain, live, masks, vec, rate, inlet, cotangent, value_proj, gate_proj, mixer_out):
+    rows, columns = tokens.shape
+    channels = value_proj.shape[1]
+    total = count * rows
+    wide = jax.ShapeDtypeStruct((total, channels), F32)
+    ahead = jax.ShapeDtypeStruct((total + 8, channels), F32)
+    blocks = jax.ShapeDtypeStruct((count, rows, columns), BF)
+    return pl.pallas_call(
+        functools.partial(mixer_kernel, count),
+        out_shape=(
+            jax.ShapeDtypeStruct((rows, columns), F32), jax.ShapeDtypeStruct((8, 128), F32),
+            blocks, blocks, jax.ShapeDtypeStruct((total, channels), BF), ahead, wide, ahead, wide, wide, wide,
+        ),
+        in_specs=[IN_VMEM] * 7 + [ANYWHERE] * 4,
+        out_specs=(IN_VMEM,) * 2 + (ANYWHERE,) * 9,
+        scratch_shapes=[
+            pltpu.VMEM((count, rows, columns), BF),
+            pltpu.VMEM((columns, channels), BF),
+            pltpu.VMEM((columns, channels), BF),
+            pltpu.VMEM((channels, columns), BF),
+            pltpu.VMEM((total + 8, channels), F32),
+            pltpu.VMEM((total, channels), F32),
+            pltpu.VMEM((total, channels), BF),
+            pltpu.VMEM((total + 8, channels), F32),
+            pltpu.VMEM((total, channels), F32),
+            pltpu.VMEM((total, channels), F32),
+            pltpu.VMEM((total, channels), F32),
+            pltpu.VMEM((rows, channels), BF),
+            pltpu.VMEM((8, channels), F32),
+            pltpu.VMEM((count, PARTS, rows, columns // PARTS), BF),
+            pltpu.VMEM((count + 1, PARTS, rows, columns // PARTS), BF),
+            DMA((3,)), DMA, DMA((7,)), DMA((count,)),
+            DMA((2, count)), DMA((count,)), DMA((2, count)), DMA((count,)),
+            DMA((count, PARTS)), DMA((count + 1, PARTS)),
+        ],
+        compiler_params=pltpu.CompilerParams(vmem_limit_bytes=VMEM_LIMIT, collective_id=1, has_side_effects=True),
+        cost_estimate=pl.CostEstimate(flops=6 * total * columns * channels, bytes_accessed=40 * total * channels,
+                                      transcendentals=6 * total * channels),
+    )(tokens, gain, live, masks, vec, rate, inlet, cotangent, value_proj, gate_proj, mixer_out)
+
+
+def middle_kernel(count, groups, middle_grad_ref, middle_ref, live_ref, terms_hbm, out_hbm, mixed_hbm,
+                  layer_ref, stat_ref, out_grad_ref, dm_hbm,
+                  low, out_w, mixed, dm, held, slots, cube_a, slots_a, cube_b, slots_b,
+                  load_sem, dm_sem, ag_send, ag_recv, rs_send, rs_recv, a_send, a_recv, b_send, b_recv):
+    me = lax.axis_index("mp")
+    rows, columns = middle_ref.shape
+    channels = out_w.shape[0]
+    width = columns // PARTS
+    chunk = columns // groups
+    half = channels // 2
+    loads = [pltpu.make_async_copy(source, target, load_sem.at[index]) for index, (source, target) in enumerate(
+        ((out_hbm, out_w), (mixed_hbm, mixed), (terms_hbm, held)))]
+    for load in loads:
+        load.start()
+    low[me] = middle_grad_ref[...].astype(BF)
+    greet(count, groups)
+    gather = Gather(count, low, ag_send, ag_recv)
+    scatter = Scatter(count, held, slots, rs_send, rs_recv)
+    order_a, order_b = orders(groups)
+    cubes = (Cube(groups, order_a, cube_a, slots_a, a_send, a_recv),
+             Cube(groups, order_b, cube_b, slots_b, b_send, b_recv))
+    gather.start()
+    for load in loads:
+        load.wait()
+
+    def dm_copy(block):
+        return pltpu.make_async_copy(dm.at[block], dm_hbm.at[pl.ds(pl.multiple_of(block * rows, rows), rows)],
+                                     dm_sem.at[block])
+
+    def back(block):
+        dm[block] = dot_nt(low[block], out_w[...])
+        dm_copy(block).start()
+
+    back(me)
+    for distance in range(1, count):
+        gather.take(distance)
+        if distance == 1:
+            for step in range(count - 1):
+                for part in range(PARTS):
+                    pl.when(me == 0)(scatter.copy(count - 1 - step, part, 1).start)
+                    pl.when(me == count - 1)(scatter.copy(step, part, -1).start)
+        pl.when(me - distance >= 0)(lambda: back(me - distance))
+        pl.when(me + distance < count)(lambda: back(me + distance))
+
+    def out_grad(index, unused):
+        right = low[:, :, pl.ds(pl.multiple_of(index * chunk, chunk), chunk)].reshape(count * rows, chunk)
+        both = dot_tn(mixed[...], right).astype(BF)
+        cube_a[index] = both[:half]
+        cube_b[index] = both[half:]
+        return unused
+
+    lax.fori_loop(0, groups, out_grad, 0)
+    levels = len(order_a)
+    for cube in cubes:
+        cube.start(0)
+    level = 0
+    for time in scatter.times():
+        scatter.pass_on(time, False, False)
+        if level < levels and time > 1:
+            for cube in cubes:
+                cube.finish(level)
+                if level + 1 < levels:
+                    cube.start(level + 1)
+            level += 1
+    for rest in range(level, levels):
+        for cube in cubes:
+            cube.finish(rest)
+            if rest + 1 < levels:
+                cube.start(rest + 1)
+    out_grad_ref[0:half, :] = cubes[0].result()
+    out_grad_ref[half:channels, :] = cubes[1].result()
+    row_sums = jnp.zeros((rows, 1), F32)
+    for part in range(PARTS):
+        span = slice(part * width, (part + 1) * width)
+        scatter.wait_total(part)
+        total = scatter.total(part)
+        row_sums = row_sums + jnp.sum(total * total, axis=1, keepdims=True)
+        layer_ref[:, span] = (middle_ref[:, span] + total).astype(BF)
+    live_squares(live_ref, row_sums, stat_ref)
+    for block in range(count):
+        dm_copy(block).wait()
+    gather.drain()
+    scatter.drain()
+
+
+def call_middle(count, groups, middle_grad, middle, live, terms, mixer_out, mixed):
+    rows, columns = middle.shape
+    channels = mixer_out.shape[0]
+    total = count * rows
+    chunk = columns // groups
+    return pl.pallas_call(
+        functools.partial(middle_kernel, count, groups),
+        out_shape=(
+            jax.ShapeDtypeStruct((rows, columns), BF), jax.ShapeDtypeStruct((8, 128), F32),
+            jax.ShapeDtypeStruct((channels, chunk), F32), jax.ShapeDtypeStruct((total, channels), F32),
+        ),
+        in_specs=[IN_VMEM] * 3 + [ANYWHERE] * 3,
+        out_specs=(IN_VMEM, IN_VMEM, IN_VMEM, ANYWHERE),
+        scratch_shapes=[
+            pltpu.VMEM((count, rows, columns), BF),
+            pltpu.VMEM((channels, columns), BF),
+            pltpu.VMEM((total, channels), BF),
+            pltpu.VMEM((count, rows, channels), F32),
+            pltpu.VMEM((count, PARTS, rows, columns // PARTS), BF),
+            pltpu.VMEM((count + 1, PARTS, rows, columns // PARTS), BF),
+            pltpu.VMEM((groups, channels // 2, chunk), BF),
+            pltpu.VMEM((groups - 1, channels // 2, chunk), BF),
+            pltpu.VMEM((groups, channels // 2, chunk), BF),
+            pltpu.VMEM((groups - 1, channels // 2, chunk), BF),
+            DMA((3,)), DMA((count,)), DMA((2, count)), DMA((count,)), DMA((count, PARTS)), DMA((count + 1, PARTS)),
+            DMA((groups - 1,)), DMA((groups - 1,)), DMA((groups - 1,)), DMA((groups - 1,)),
+        ],
+        compiler_params=pltpu.CompilerParams(vmem_limit_bytes=VMEM_LIMIT, collective_id=2, has_side_effects=True),
+        cost_estimate=pl.CostEstimate(flops=4 * total * columns * channels, bytes_accessed=40 * total * channels,
+                                      transcendentals=0),
+    )(middle_grad, middle, live, terms, mixer_out, mixed)
+
+
+def input_kernel(count, groups, heads, tokens_ref, gain_ref, middle_grad_ref, mask_ref, vec_ref, rate_ref, inlet_ref,
+                 value_hbm, gate_hbm, normed_hbm, dm_hbm, vp_hbm, gp_hbm, state_hbm, conv_hbm, forget_hbm, input_hbm,
+                 input_grad_ref, gain_grad_ref, value_grad_ref, gate_grad_ref, small_ref, vec_grad_ref,
+                 value_w, gate_w, dm, vp, gp, state, conv, forget, inlet_gate, normed, vlow, glow, dzf, dzi, dconv,
+                 clow, sums, carry, held, slots, cube_a, slots_a, cube_b, slots_b, cube_c, slots_c, full,
+                 vec_held, vec_slots,
+                 load_sem, block_sem, normed_sem, rs_send, rs_recv, a_send, a_recv, b_send, b_recv, c_send, c_recv,
+                 f_send, f_recv, v_send, v_recv):
+    me = lax.axis_index("mp")
+    rows, columns = tokens_ref.shape
+    channels = value_w.shape[1]
+    width = columns // PARTS
+    chunk = columns // groups
+    total_rows = count * rows
+    head = channels // heads
+    loads = [pltpu.make_async_copy(value_hbm, value_w, load_sem.at[0]),
+             pltpu.make_async_copy(gate_hbm, gate_w, load_sem.at[1])]
+    for load in loads:
+        load.start()
+
+    def block_loads(block, slot):
+        at = pl.multiple_of(block * rows, rows)
+        plain = pl.ds(at, rows)
+        ahead = pl.ds(at, rows + 8)
+        return [pltpu.make_async_copy(source.at[window], target.at[slot], block_sem.at[slot, index])
+                for index, (source, window, target) in enumerate((
+                    (dm_hbm, plain, dm), (vp_hbm, ahead, vp), (gp_hbm, plain, gp), (state_hbm, ahead, state),
+                    (conv_hbm, plain, conv), (forget_hbm, plain, forget), (input_hbm, plain, inlet_gate)))]
+
+    for load in block_loads(count - 1, 0):
+        load.start()
+    zeros = jnp.zeros((8, channels), F32)
+    dconv[rows:rows + 8, :] = zeros
+    carry[...] = zeros
+    for row in range(8):
+        sums[row] = zeros
+    greet(count, groups)
+    scatter = Scatter(count, held, slots, rs_send, rs_recv)
+    order_a, order_b = orders(groups)
+    cubes = (Cube(groups, order_a, cube_a, slots_a, a_send, a_recv),
+             Cube(groups, order_b, cube_b, slots_b, b_send, b_recv),
+             Cube(groups, order_b, cube_c, slots_c, c_send, c_recv))
+    spread = Spread(cubes[2], full, f_send, f_recv)
+    for load in loads:
+        load.wait()
+
+    def back(step, unused):
+        block = count - 1 - step
+        slot = step % 2
+        for load in block_loads(block, slot):
+            load.wait()
+
+        @pl.when(step + 1 < count)
+        def _():
+            for load in block_loads(block - 1, 1 - slot):
+                load.start()
+
+        base = block * rows
+        rec_backward(base, rows, dm.at[slot], vp.at[slot], gp.at[slot], mask_ref, vec_ref, rate_ref, inlet_ref,
+                     state.at[slot], conv.at[slot], forget.at[slot], inlet_gate.at[slot],
+                     vlow, glow, dzf, dzi, dconv, clow, sums, carry)
+        window = pl.ds(pl.multiple_of(base, rows), rows)
+        for part in range(PARTS):
+            span = slice(part * width, (part + 1) * width)
+            held[block, part] = (dot_nt(vlow[window, :], value_w[span, :])
+                                 + dot_nt(glow[window, :], gate_w[span, :])).astype(BF)
+            scatter.first(block, part)
+        return unused
+
+    def normed_copy(index, slot):
+        return pltpu.make_async_copy(
+            normed_hbm.at[:, :, pl.ds(pl.multiple_of(index * chunk, chunk), chunk)], normed.at[slot],
+            normed_sem.at[slot])
+
+    normed_copy(0, 0).start()
+    lax.fori_loop(0, count, back, 0)
+
+    def weights(index, unused):
+        slot = index % 2
+        normed_copy(index, slot).wait()
+        pl.when(index + 1 < groups)(lambda: normed_copy(index + 1, 1 - slot).start())
+        left = normed[slot].reshape(total_rows, chunk)
+        cube_a[index] = dot_tn(left, vlow[...]).astype(BF)
+        cube_b[index] = dot_tn(left, glow[...]).astype(BF)
+        return unused
+
+    lax.fori_loop(0, groups, weights, 0)
+    cubes[0].start(0)
+    cubes[1].start(0)
+    slab = 2 * channels // groups
+    for which, source in enumerate((dzf, dzi)):
+        for index in range(heads):
+            span = slice(index * head, (index + 1) * head)
+            at = which * channels + index * head
+            small_ref[at:at + head, :] = dot_tn(clow[:, span], source[:, span])
+    for index in range(groups):
+        cube_c[index] = small_ref[index * slab:(index + 1) * slab, :]
+    cubes[2].start(0)
+    for row in range(8):
+        vec_held[0, row:row + 1, :] = jnp.sum(sums[row], axis=0, keepdims=True)
+
+    def vec_copy(level):
+        return pltpu.make_async_remote_copy(
+            src_ref=vec_held.at[level], dst_ref=vec_slots.at[level], send_sem=v_send.at[level],
+            recv_sem=v_recv.at[level], device_id={"dp": partner_of(level)}, device_id_type=MESH)
+
+    levels = len(order_a)
+    vec_copy(0).start()
+
+    def advance(level):
+        if level < levels:
+            for cube in cubes:
+                cube.finish(level)
+                if level + 1 < levels:
+                    cube.start(level + 1)
+            vec_copy(level).wait()
+            if level + 1 < levels:
+                vec_held[level + 1] = vec_held[level] + vec_slots[level]
+                vec_copy(level + 1).start()
+            else:
+                vec_grad_ref[...] = vec_held[level] + vec_slots[level]
+                value_grad_ref[...] = cubes[0].result()
+                gate_grad_ref[...] = cubes[1].result()
+                full[lax.axis_index("dp")] = cubes[2].result()
+                spread.start(levels - 1)
+        elif level < 2 * levels:
+            back_level = 2 * levels - 1 - level
+            spread.finish(back_level)
+            if back_level > 0:
+                spread.start(back_level - 1)
+
+    level = 0
+    for time in scatter.times():
+        scatter.pass_on(time, False, True)
+        if time > 1:
+            advance(level)
+            level += 1
+    for rest in range(level, 2 * levels):
+        advance(rest)
+    for index in range(groups):
+        small_ref[index * slab:(index + 1) * slab, :] = full[index]
+
+    def write(span, change):
+        input_grad_ref[:, span] = (middle_grad_ref[:, span] + change).astype(BF)
+
+    norm_back(tokens_ref, gain_ref, scatter, gain_grad_ref, write)
+    scatter.drain()
+
+
+def call_input(count, groups, heads, tokens, gain, middle_grad, masks, vec, rate, inlet, value_proj, gate_proj,
+               normed_all, dm, vp, gp, state, conv, forget, inp):
+    rows, columns = tokens.shape
+    channels = value_proj.shape[1]
+    total = count * rows
+    chunk = columns // groups
+    head = channels // heads
+    slab = 2 * channels // groups
+    plain = pltpu.VMEM((2, rows, channels), F32)
+    ahead = pltpu.VMEM((2, rows + 8, channels), F32)
+    low = pltpu.VMEM((total, channels), BF)
+    levels = groups.bit_length() - 1
+    return pl.pallas_call(
+        functools.partial(input_kernel, count, groups, heads),
+        out_shape=(
+            jax.ShapeDtypeStruct((rows, columns), BF), jax.ShapeDtypeStruct((1, columns), F32),
+            jax.ShapeDtypeStruct((chunk, channels), F32), jax.ShapeDtypeStruct((chunk, channels), F32),
+            jax.ShapeDtypeStruct((2 * channels, head), F32), jax.ShapeDtypeStruct((8, channels), F32),
+        ),
+        in_specs=[IN_VMEM] * 7 + [ANYWHERE] * 10,
+        out_specs=(IN_VMEM,) * 6,
+        scratch_shapes=[
+            pltpu.VMEM((columns, channels), BF),
+            pltpu.VMEM((columns, channels), BF),
+            plain, ahead, plain, ahead, plain, plain, plain,
+            pltpu.VMEM((2, count, rows, chunk), BF),
+            low, low, low, low,
+            pltpu.VMEM((rows + 8, channels), F32),
+            low,
+            pltpu.VMEM((8, 8, channels), F32),
+            pltpu.VMEM((8, channels), F32),
+            pltpu.VMEM((count, PARTS, rows, columns // PARTS), BF),
+            pltpu.VMEM((count + 1, PARTS, rows, columns // PARTS), BF),
+            pltpu.VMEM((groups, chunk, channels), BF), pltpu.VMEM((groups - 1, chunk, channels), BF),
+            pltpu.VMEM((groups, chunk, channels), BF), pltpu.VMEM((groups - 1, chunk, channels), BF),
+            pltpu.VMEM((groups, slab, head), F32), pltpu.VMEM((groups - 1, slab, head), F32),
+            pltpu.VMEM((groups, slab, head), F32),
+            pltpu.VMEM((levels, 8, channels), F32), pltpu.VMEM((levels, 8, channels), F32),
+            DMA((2,)), DMA((2, 7)), DMA((2,)), DMA((count, PARTS)), DMA((count + 1, PARTS)),
+            DMA((groups - 1,)), DMA((groups - 1,)), DMA((groups - 1,)), DMA((groups - 1,)),
+            DMA((groups - 1,)), DMA((groups - 1,)), DMA((groups - 1,)), DMA((groups - 1,)),
+            DMA((levels,)), DMA((levels,)),
+        ],
+        compiler_params=pltpu.CompilerParams(vmem_limit_bytes=VMEM_LIMIT, collective_id=3, has_side_effects=True),
+        cost_estimate=pl.CostEstimate(flops=8 * total * columns * channels, bytes_accessed=60 * total * channels,
+                                      transcendentals=4 * total * channels),
+    )(tokens, gain, middle_grad, masks, vec, rate, inlet, value_proj, gate_proj, normed_all, dm, vp, gp, state, conv,
+      forget, inp)
 
 
 def spans(total):
@@ -469,24 +975,15 @@
         load.start()
 
     def cot_copy(block):
-        return pltpu.make_async_copy(cot_hbm.at[pl.ds(pl.multiple_of(block * rows, rows), rows)],
+        return pltpu.make_async_copy(cot_hbm.at[block],
                                      cot.at[block], cot_sem.at[block])
 
     for block in range(count):
         cot_copy(block).start()
-    greet("mp", count)
+    greet(count)
     gather = Gather(count, normed, ag_send, ag_recv)
     scatter = Scatter(count, held, slots, rs_send, rs_recv)
-    step_rows = 64
-
-    def norm_step(index, unused):
-        window = pl.ds(pl.multiple_of(index * step_rows, step_rows), step_rows)
-        middle = middle_ref[window, :]
-        scale = lax.rsqrt(jnp.mean(middle * middle, axis=1, keepdims=True) + EPS)
-        normed[me, window, :] = (middle * scale * gain_ref[...]).astype(BF)
-        return unused
-
-    lax.fori_loop(0, rows // step_rows, norm_step, 0)
+    norm_rows(middle_ref, gain_ref, normed.at[me])
     gather.start()
     for load in loads:
         load.wait()
@@ -568,11 +1065,11 @@
 
     work = [(kind, index) for kind in (0, 1, 2) for index in range((4, 4, 8)[kind])]
     started = []
-    times = max(2 * count - 5, 0)
-    per_step = -(-len(work) // (times + 1))
-    for step in range(times + 1):
+    times = scatter.times()
+    per_step = -(-len(work) // (len(times) + 1))
+    for step in range(len(times) + 1):
         if step > 0:
-            scatter.pass_on(step + 1)
+            scatter.pass_on(step, True, True)
         for kind, index in work[step * per_step:(step + 1) * per_step]:
             slot = len(started) % 2
             if len(started) >= 2:
@@ -583,24 +1080,10 @@
     for back in (2, 1):
         stage_copy(*started[-back], (len(started) - back) % 2).wait()
 
-    dot_sum = jnp.zeros((rows, 1), F32)
-    square_sum = jnp.zeros((rows, 1), F32)
-    for part in range(PARTS):
-        span = slice(part * width, (part + 1) * width)
-        grad = scatter.total(part)
-        middle = middle_ref[:, span]
-        middle_grad_ref[:, span] = grad
-        dot_sum = dot_sum + jnp.sum(grad * gain_ref[:, span] * middle, axis=1, keepdims=True)
-        square_sum = square_sum + jnp.sum(middle * middle, axis=1, keepdims=True)
-    scale = lax.rsqrt(square_sum * (1.0 / columns) + EPS)
-    pull = scale * scale * scale * (dot_sum * (1.0 / columns))
-    for part in range(PARTS):
-        span = slice(part * width, (part + 1) * width)
-        grad = middle_grad_ref[:, span]
-        middle = middle_ref[:, span]
-        gain_grad_ref[:, span] = jnp.sum(grad * middle * scale, axis=0, keepdims=True)
-        result = cot[me, :, span].astype(F32) + scale * (grad * gain_ref[:, span]) - middle * pull
-        middle_grad_ref[:, span] = result
+    def write(span, change):
+        middle_grad_ref[:, span] = cot[me, :, span].astype(F32) + change
+
+    norm_back(middle_ref, gain_ref, scatter, gain_grad_ref, write)
     part_copy(0, 0).wait()
     pl.when(me < count - 1)(part_copy(0, 1).wait)
     gather.drain()
@@ -655,95 +1138,65 @@
     return spread.reshape(count * width, count * width)
 
 
-def diagonal_blocks(square, count):
-    width = square.shape[0] // count
-    return jnp.stack([square[h * width:(h + 1) * width, h * width:(h + 1) * width] for h in range(count)])
-
-
-def scatter_mp(values):
-    return lax.psum_scatter(values.astype(BF), "mp", scatter_dimension=0, tiled=True).astype(F32)
-
-
 def scatter_dp(values, dimension):
-    return lax.psum_scatter(values.astype(BF), "dp", scatter_dimension=dimension, tiled=True).astype(F32)
+    return lax.psum_scatter(values, "dp", scatter_dimension=dimension, tiled=True).astype(F32)
 
 
 def local(groups, tokens, cotangent, lengths, live_mask, mixer_gain, value_proj, gate_proj, conv_taps, conv_bias,
           rate_weight, rate_bias, inlet_weight, inlet_bias, decay_param, mixer_out, dense_gain,
           dense_gate, dense_value, dense_down):
-    residual = tokens.astype(F32)
-    columns = residual.shape[1]
-    head_count = rate_weight.shape[0]
-    normed_first, norm_back_in = jax.vjp(scaled_norm, residual, mixer_gain)
-    normed_all = lax.all_gather(normed_first.astype(BF), "mp", axis=0, tiled=True)
-    rows_total = normed_all.shape[0]
+    columns = tokens.shape[1]
+    head_count, head_width = rate_weight.shape[:2]
+    channels = head_count * head_width
+    count = lax.axis_size("mp")
+    rows_total = count * tokens.shape[0]
     offsets = doc_offsets(lengths[0], rows_total)
     taps_here = jnp.arange(8, dtype=jnp.int32)
     masks = (offsets[:, None] >= taps_here[None, :]).astype(F32)
-    masks_ext = jnp.concatenate([masks, jnp.zeros((8, 8), F32)], axis=0)
+    masks = jnp.concatenate([masks, jnp.zeros((8, 8), F32)], axis=0)
     vec = jnp.concatenate([
         conv_taps,
         jnp.stack([conv_bias, rate_bias, inlet_bias, -8.0 * jax.nn.softplus(-decay_param)]),
     ], axis=0)
     rate_square = block_diagonal(rate_weight).astype(BF)
     inlet_square = block_diagonal(inlet_weight).astype(BF)
-    value_pre = dot_nn(normed_all, value_proj)
-    gate_pre = dot_nn(normed_all, gate_proj)
-    mixed_act, states, convolved, forget_gate, input_gate = call_forward(
-        value_pre, gate_pre, masks_ext, vec, rate_square, inlet_square)
-    mixer_part = scatter_mp(dot_nn(mixed_act, mixer_out))
-    middle = residual + mixer_part
-    block_rows = lax.all_gather(cotangent, "mp", axis=0, tiled=True)
-    count = rows_total // tokens.shape[0]
-    middle_grad, dense_gain_grad, dense_terms, dense_gate_grad, dense_value_grad, down_grad = call_dense(
-        count, groups, middle, dense_gain[None, :], block_rows, dense_gate, dense_value, dense_down)
-    dense_gain_grad = dense_gain_grad[0]
-    middle_low = middle_grad.astype(BF)
-    dense_part = lax.psum_scatter(dense_terms, "mp", scatter_dimension=0, tiled=True)[0].astype(F32)
-    dense_part = dense_part.transpose(1, 0, 2).reshape(tokens.shape)
-    layer_out = (middle + dense_part).astype(BF)
     weights_live = live_mask.astype(F32)
+    live_column = weights_live[:, None]
+    middle, mixer_stat, normed_all, cot_all, mixed, vp, gp, state, conv, forget, inp = call_mixer(
+        count, tokens, mixer_gain[None, :], live_column, masks, vec, rate_square, inlet_square,
+        cotangent, value_proj, gate_proj, mixer_out)
+    middle_grad, dense_gain_grad, dense_terms, gate_weights, value_weights, down_weights = call_dense(
+        count, groups, middle, dense_gain[None, :], cot_all, dense_gate, dense_value, dense_down)
+    layer_out, dense_stat, mixer_out_sum, dm = call_middle(
+        count, groups, middle_grad, middle, live_column, dense_terms, mixer_out, mixed)
+    input_grad, mixer_gain_grad, value_proj_sum, gate_proj_sum, small, vec_sum = call_input(
+        count, groups, head_count, tokens, mixer_gain[None, :], middle_grad, masks, vec, rate_square, inlet_square,
+        value_proj, gate_proj, normed_all, dm, vp, gp, state, conv, forget, inp)
+    residual = tokens.astype(F32)
     squares = jnp.stack([
-        jnp.sum(weights_live * jnp.sum(residual * residual, axis=1)),
-        jnp.sum(weights_live * jnp.sum(mixer_part * mixer_part, axis=1)),
-        jnp.sum(weights_live * jnp.sum(dense_part * dense_part, axis=1)),
-    ])
-    live_count = jnp.sum(weights_live)
-    middle_rows = lax.all_gather(middle_low, "mp", axis=0, tiled=True)
-    mixed_grad = dot_nt(middle_rows, mixer_out)
-    mixer_out_grad = dot_tn(mixed_act, middle_rows)
-    value_low, gate_low, rate_sq, inlet_sq, vec_grad = call_backward(
-        mixed_grad, value_pre, gate_pre, masks_ext, vec, rate_square, inlet_square,
-        states, convolved, forget_gate, input_gate)
-    normed_in_grad = scatter_mp(dot_nt(value_low, value_proj) + dot_nt(gate_low, gate_proj))
-    value_proj_grad = dot_tn(normed_all, value_low)
-    gate_proj_grad = dot_tn(normed_all, gate_low)
-    input_norm_grad, mixer_gain_grad = norm_back_in(normed_in_grad)
-    input_grad = (middle_grad + input_norm_grad).astype(BF)
-    small = (vec_grad, diagonal_blocks(rate_sq, head_count), diagonal_blocks(inlet_sq, head_count))
-    vec_sum, rate_sum, inlet_sum = lax.psum(small, "dp")
+        jnp.sum(weights_live * jnp.sum(residual * residual, axis=1)), mixer_stat[0, 0], dense_stat[0, 0]])
+    mixer_gain_sum, dense_gain_sum, squares, live_count = lax.psum(
+        (mixer_gain_grad[0], dense_gain_grad[0], squares, jnp.sum(weights_live)), ("dp", "mp"))
+    branch_rms = jnp.sqrt(squares / (live_count * columns))
     decay_scale = 8.0 * jax.nn.sigmoid(-decay_param)
-    mixer_gain_sum, dense_gain_sum, squares, live_count = lax.psum(
-        (mixer_gain_grad, dense_gain_grad, squares, live_count), ("dp", "mp"))
-    branch_rms = jnp.sqrt(squares / (live_count * columns))
     return (
         layer_out,
         input_grad,
         mixer_gain_sum,
-        scatter_dp(value_proj_grad, 0),
-        scatter_dp(gate_proj_grad, 0),
+        value_proj_sum,
+        gate_proj_sum,
         vec_sum[0:4],
         vec_sum[4],
-        rate_sum,
+        small[:channels].reshape(rate_weight.shape),
         vec_sum[V_RATE],
-        inlet_sum,
+        small[channels:].reshape(rate_weight.shape),
         vec_sum[V_INLET],
         vec_sum[V_DECAY] * decay_scale,
-        scatter_dp(mixer_out_grad, 1),
+        mixer_out_sum,
         dense_gain_sum,
-        scatter_dp(dense_gate_grad, 0),
-        scatter_dp(dense_value_grad, 0),
-        scatter_dp(down_grad, 1),
+        scatter_dp(gate_weights, 0),
+        scatter_dp(value_weights, 0),
+        scatter_dp(down_weights, 1),
         branch_rms,
     )
 

time: 1090 us -> 659 us (0.60)
  waiting for transfers between devices: 693 us -> 1.4 us
  Pallas kernels: 188 us -> 553 us
  matrix products: 59.8 us -> 0 us
  other arithmetic: 43 us -> 17.8 us
  blocking collectives: 65.5 us -> 46.8 us
    reduce_scatter x9 -> x3, waiting for transfers between devices: 450 us -> 0.01 us  [scatter_dp(): lax.psum_scatter(values, 'dp', scatter_dimension=dimension, tiled=True)]
    pallas_call x2 -> x3, Pallas kernels: 56.7 us -> 425 us  [the longest x1 191 us: call_mixer(): pl.pallas_call(functools.partial(mixer_kernel, count), out_shape=(jax.Sha...]
    all_gather x3 -> x0, waiting for transfers between devices: 230 us -> none  [the longest x1 79.7 us: local(): block_rows = lax.all_gather(cotangent, 'mp', axis=0, tiled=True)]
    dot_general x9 -> x0, matrix products: 59.8 us -> none  [the longest x3 22.2 us: dot_tn(): lax.dot_general(left, right, (((0,), (0,)), ((), ())), preferred_element_...]
    psum x2 -> x1, blocking collectives: 65.5 us -> 46.8 us  [local(): lax.psum((mixer_gain_grad[0], dense_gain_grad[0], squares, jnp.sum(weight...]
  transfers between devices with their start and end apart: 13 -> 3, of which waited for: 12 -> 0; matrix products, arithmetic and copies ran while one was open for 8% -> 3% of each run, Pallas kernels for 3% -> 36%
where the time goes in v3:
time: 659 us; the launch traced here: 653 us
  Pallas kernels  553 us (84%)
  blocking collectives  46.8 us (7%)
  local copies, waits for them, and re-layouts  18.7 us (3%)
  other arithmetic  17.8 us (3%)
  between operations  14.7 us (2%)
    pallas_call x1, Pallas kernels, call_mixer(): pl.pallas_call(functools.partial(mixer_kernel, count), out_shape=(jax.Sha...  191 us
    pallas_call x1, Pallas kernels, call_dense(): pl.pallas_call(functools.partial(dense_kernel, count, groups), out_shape=...  129 us
    pallas_call x1, Pallas kernels, call_input(): pl.pallas_call(functools.partial(input_kernel, count, groups, heads), out...  118 us
    pallas_call x1, Pallas kernels, call_middle(): pl.pallas_call(functools.partial(middle_kernel, count, groups), out_shape...  116 us
    psum x1, blocking collectives, local(): lax.psum((mixer_gain_grad[0], dense_gain_grad[0], squares, jnp.sum(weight...  46.8 us
  transfers between devices with their start and end apart: 3, of which 0 were waited for; matrix products, arithmetic and copies ran while one was open for 3% of the time, Pallas kernels for 36%

profile of v3, /device:TPU:0, one launch (start us, length us, event | category | flops | bytes accessed | tf_op | source)
XLA Modules:
  0.0 652.7 jit_solution(5795723690448649486)
XLA Ops:
  7.2 0.7 convert_element_type.37
  7.9 0.7 stack.18
  8.6 0.7 stack.19
  9.3 0.7 stack.20
  10.0 0.8 reduce-window.8
  10.8 0.7 select_reduce_fusion
  11.6 0.7 fusion
  12.5 0.8 copy.39.live_ref
  13.3 0.8 pad_convert_fusion.mask_ref
  14.2 2.3 multiply_convert_fusion
  16.5 1.6 convert_element_type.42.inlet_ref
  18.1 1.6 convert_element_type.40.rate_ref
  20.2 191.3 %shard_map.322 = (f32[256,2048]{1,0:T(8,128)}, f32[8,128]{1,0:T(8,128)}, bf16[4,256,2048]{2,1,0:T(8,128)(2,1)}, bf16[4,256,2048]{2,1,0:T(8,128)(2,1)}, bf16[1024...) custom-call(bf16[256,2048]{1,0:T(8,128)(2,1)} %tokens_ref.3, ...), custom_call_target="tpu_custom_call" | custom-call | flops 8053063680 | bytes 26214400 | tf_op jit(solution)/shard_map/pallas_call | solution.py:607
  211.6 128.6 %shard_map.323 = (f32[256,2048]{1,0:T(8,128)}, f32[1,2048]{1,0:T(1,128)}, bf16[4,4,256,512]{3,2,1,0:T(8,128)(2,1)}, bf16[2048,1536]{1,0:T(8,128)(2,1)}, bf16[204...) custom-call(f32[256,2048]{1,0:T(8,128)} %get-tuple-element.45.middle_ref, f32[1,2048]{1,0:T(1,128)} %bitcast.21, ...), custom_call_target="tpu_custom_call" | custom-call | flops 57982058496 | bytes 37748736 | tf_op jit(solution)/shard_map/pallas_call | solution.py:1100
  340.2 0.7 reduce-scatter.6.cloned.1.call-update
  341.6 1.2 slice.34
  342.8 115.6 %shard_map.324 = (bf16[256,2048]{1,0:T(8,128)(2,1)}, f32[8,128]{1,0:T(8,128)}, f32[640,256]{1,0:T(8,128)}, f32[1024,640]{1,0:T(8,128)}) custom-call(f32[256,2048]{1,0:T(8,128)} %get-tuple-element.47.middle_grad_ref, f32[256,2048]{1,0:T(8,128)} %get-tuple-element.45.middle_ref, f32[256,1]{1,0:T(8,128)} %copy.39.live_ref, ...), custom_call_target="tpu_custom_call" | custom-call | flops 5368709120 | bytes 26214400 | tf_op jit(solution)/shard_map/pallas_call | solution.py:731
  458.4 1.2 slice.35
  459.6 117.7 %shard_map.325 = (bf16[256,2048]{1,0:T(8,128)(2,1)}, f32[1,2048]{1,0:T(1,128)}, f32[256,640]{1,0:T(8,128)}, f32[256,640]{1,0:T(8,128)}, f32[1280,160]{1,0:T(8,128)}, /*index=5*/f32[8,640]{1,0:T(8,128)}) custom-call(bf16[256,2048]{1,0:T(8,128)(2,1)} %tokens_ref.3, f32[1,2048]{1,0:T(1,128)} %bitcast.23, f32[256,2048]{1,0:T(8,128)} %get-tuple-element.47.middle_grad_ref, ...), custom_call_target="tpu_custom_call" | custom-call | flops 10737418240 | bytes 39321600 | tf_op jit(solution)/shard_map/pallas_call | solution.py:920
  577.3 1.3 slice.27
  579.5 2.0 pad_maximum_fusion
  581.5 46.8 %all-reduce.1 = (f32[2048]{0:T(1024)}, f32[2048]{0:T(1024)}, f32[3]{0:T(128)S(1)}, f32[]{:T(128)}) all-reduce(f32[2048]{0:T(1024)} %bitcast.16, f32[2048]{0:T(1024)S(1)} %bitcast.15, f32[3]{0:T(128)S(1)} %pad_maximum_fusion, f32[]{:T(128)} %get-tuple-element.76), channel_id=1, replica_groups=mesh['dp'=8,'mp'=4] {'dp','mp'}, use_global_device_ids=true, to_apply=%region_2.3 | all-reduce | flops 4100 | bytes 32800 | tf_op jit(solution)/shard_map/psum | solution.py:1178
  629.0 1.5 slice_reduce_fusion
  631.6 2.4 fusion.2
  634.0 2.4 convert_element_type.45
  636.4 2.5 convert_element_type.44
  639.0 2.5 convert_element_type.43
  641.5 1.0 copy.46
  642.5 1.0 copy.47
  643.5 0.8 copy.48
  644.3 0.8 copy.49
  645.2 0.8 copy.50
  (37 shorter events, 3.7 us)
Async XLA Ops:
  7.2 626.8 %reduce-scatter.8.cloned.1.call-start = ((), (), s32[]{:S(2)}) async-start(), calls=%async_computation.5 | async-start | bytes 7077888 | tf_op jit(solution)/shard_map/reduce_scatter | solution.py:1142
  16.5 3.2 copy-start.7
  340.2 296.3 %reduce-scatter.6.cloned.1.call-start = ((), (), s32[]{:S(2)}) async-start(), calls=%async_computation.4 | async-start | bytes 7077888 | tf_op jit(solution)/shard_map/reduce_scatter | solution.py:1142
  340.9 298.1 %reduce-scatter.4.cloned.1.call-start = ((), (), s32[]{:S(2)}) async-start(), calls=%async_computation.3 | async-start | bytes 7077888 | tf_op jit(solution)/shard_map/reduce_scatter | solution.py:1142
  459.6 119.0 %copy-start = (bf16[256,2048]{1,0:T(8,128)(2,1)S(1)}, bf16[256,2048]{1,0:T(8,128)(2,1)}, u32[]{:S(2)}) copy-start(bf16[256,2048]{1,0:T(8,128)(2,1)} %tokens_ref.3) | copy-start | bytes 3145732
  459.6 119.3 %copy-start.9 = (s32[256]{0:T(256)S(1)}, s32[256]{0:T(256)}, u32[]{:S(2)}) copy-start(s32[256]{0:T(256)} %param.22) | copy-start | bytes 3076
  459.6 121.9 %copy-start.8 = (f32[1,2048]{1,0:T(1,128)S(1)}, f32[1,2048]{1,0:T(1,128)}, u32[]{:S(2)}) copy-start(f32[1,2048]{1,0:T(1,128)} %get-tuple-element.66) | copy-start | bytes 24580
  459.6 171.4 %copy-start.6 = (f32[640]{0:T(1024)S(1)}, f32[640]{0:T(1024)}, u32[]{:S(2)}) copy-start(f32[640]{0:T(1024)} %param.32) | copy-start | bytes 7684
  636.4 5.1 copy-start.1
  639.0 3.5 copy-start.2
  641.5 2.0 copy-start.5
  641.5 2.8 copy-start.4
  642.5 2.7 copy-start.3
Sparse Core Ops, SparseCore 0:
  340.3 63.8 reduce-scatter.7
  407.9 68.0 reduce-scatter.5
  479.4 81.2 reduce-scatter.3

commit v4 on v3

--- a/solution.py
+++ b/solution.py
@@ -14,14 +14,6 @@
 GELU_A = 0.044715
 CHUNK = 16
 VMEM_LIMIT = 60 * 1024 * 1024
-
-
-def doc_offsets(lengths_row, rows_total):
-    doc_ends = jnp.cumsum(lengths_row)
-    positions = jnp.arange(rows_total, dtype=jnp.int32)
-    before = (doc_ends[None, :] <= positions[:, None]).astype(jnp.int32)
-    starts = jnp.sum(before * lengths_row[None, :], axis=1)
-    return positions - starts
 
 
 def dot_nn(left, right):
@@ -234,7 +226,7 @@
 DMA = pltpu.SemaphoreType.DMA
 
 
-def greet(count, groups=1):
+def greet(count, groups=1, far=False):
     me = lax.axis_index("mp")
     barrier = pltpu.get_barrier_semaphore()
 
@@ -246,26 +238,28 @@
     def _():
         pl.semaphore_signal(barrier, inc=1, device_id={"mp": me + 1}, device_id_type=MESH)
 
-    levels = groups.bit_length() - 1
-    for bit in range(levels):
-        pl.semaphore_signal(barrier, inc=1, device_id={"dp": partner_of(bit)}, device_id_type=MESH)
+    peers = [("dp", bit) for bit in range(groups.bit_length() - 1)]
+    if far:
+        peers += [("mp", bit) for bit in range(1, count.bit_length() - 1)]
+    for axis, bit in peers:
+        pl.semaphore_signal(barrier, inc=1, device_id={axis: partner_of(bit, axis)}, device_id_type=MESH)
     inner = (me > 0) & (me < count - 1)
 
     @pl.when(inner)
     def _():
-        pl.semaphore_wait(barrier, 2 + levels)
+        pl.semaphore_wait(barrier, 2 + len(peers))
 
     @pl.when(jnp.logical_not(inner))
     def _():
-        pl.semaphore_wait(barrier, 1 + levels)
+        pl.semaphore_wait(barrier, 1 + len(peers))
 
 
 def bit_of(value, bit):
     return (value // (1 << bit)) % 2
 
 
-def partner_of(bit):
-    me = lax.axis_index("dp")
+def partner_of(bit, axis="dp"):
+    me = lax.axis_index(axis)
     return me + (1 << bit) * (1 - 2 * bit_of(me, bit))
 
 
@@ -308,13 +302,23 @@
     def finish(self, level):
         for index, slot in self.places(level):
             self.copy(level, index, slot).wait()
-            chunk = self.chunk(level, index, True)
             if level < len(self.order) - 1:
-                self.held[chunk] = (
-                    self.held[chunk].astype(F32) + self.slots[slot].astype(F32)).astype(self.held.dtype)
-
-    def result(self):
-        return self.held[self.me].astype(F32) + self.slots[self.count - 2].astype(F32)
+                self.add(self.chunk(level, index, True), slot, self.held.at[self.chunk(level, index, True)])
+
+    def add(self, chunk, slot, target):
+        size = self.held.shape[1]
+        rows = 64 if size % 64 == 0 else size
+
+        def step(index, unused):
+            window = pl.ds(index * rows, rows)
+            target[window, :] = (self.held[chunk, window, :].astype(F32)
+                                 + self.slots[slot, window, :].astype(F32)).astype(target.dtype)
+            return unused
+
+        lax.fori_loop(0, size // rows, step, 0)
+
+    def result(self, target):
+        self.add(self.me, self.count - 2, target)
 
 
 class Spread:
@@ -496,18 +500,41 @@
         span = slice(part * width, (part + 1) * width)
         grad = scatter.total(part)
         values = values_ref[:, span].astype(F32)
-        gain_grad_ref[:, span] = jnp.sum(grad * values * scale, axis=0, keepdims=True)
+        if gain_grad_ref is not None:
+            gain_grad_ref[:, span] = jnp.sum(grad * values * scale, axis=0, keepdims=True)
         write(span, scale * (grad * gain_ref[:, span]) - values * pull)
 
 
-def live_squares(live_ref, row_sums, stat_ref):
-    stat_ref[...] = jnp.zeros(stat_ref.shape, F32) + jnp.sum(live_ref[...] * row_sums, axis=0, keepdims=True)
-
-
-def mixer_kernel(count, tokens_ref, gain_ref, live_ref, mask_ref, vec_ref, rate_ref, inlet_ref,
+def live_total(live_ref, row_sums):
+    size = live_ref.shape[1]
+    same = lax.broadcasted_iota(jnp.int32, (size, size), 0) == lax.broadcasted_iota(jnp.int32, (size, size), 1)
+    column = jnp.sum(jnp.where(same, live_ref[...].astype(F32), 0.0), axis=1, keepdims=True)
+    return jnp.sum(column * row_sums, axis=0, keepdims=True)
+
+
+def fill_masks(lengths_ref, rows, mask_ref):
+    row = lax.broadcasted_iota(jnp.int32, mask_ref.shape, 0)
+    offset = row
+    end = 0
+    for index in range(lengths_ref.shape[1] - 1):
+        end = end + lengths_ref[0, index]
+        offset = jnp.where(row >= end, row - end, offset)
+    taps = lax.broadcasted_iota(jnp.int32, mask_ref.shape, 1)
+    mask_ref[...] = jnp.where((offset >= taps) & (row < rows), 1.0, 0.0)
+
+
+def fill_square(heads_ref, square_ref):
+    square_ref[...] = jnp.zeros(square_ref.shape, BF)
+    width = heads_ref.shape[1]
+    for head in range(heads_ref.shape[0]):
+        span = slice(head * width, (head + 1) * width)
+        square_ref[span, span] = heads_ref[head].astype(BF)
+
+
+def mixer_kernel(count, lengths_ref, tokens_ref, gain_ref, live_ref, taps_ref, small_ref, rate_heads_ref, inlet_heads_ref,
                  cot_hbm, value_hbm, gate_hbm, out_hbm,
-                 middle_ref, stat_ref, normed_all, cot_all, mixed_out, vp_out, gp_out, state_out, conv_out,
-                 forget_out, input_out,
+                 middle_ref, stat_ref, mask_ref, vec_ref, rate_ref, inlet_ref,
+                 normed_all, cot_all, mixed_out, vp_out, gp_out, state_out, conv_out, forget_out, input_out,
                  normed, value_w, gate_w, out_w, vp, gp, mixed, state, conv, forget, inlet_gate, low, carry, held,
                  slots, load_sem, own_sem, out_sem, block_sem, ag_send, ag_recv, cot_send, cot_recv, rs_send, rs_recv):
     me = lax.axis_index("mp")
@@ -530,6 +557,12 @@
     vp[0:8, :] = zeros
     state[0:8, :] = zeros
     carry[...] = zeros
+    fill_masks(lengths_ref, count * rows, mask_ref)
+    fill_square(rate_heads_ref, rate_ref)
+    fill_square(inlet_heads_ref, inlet_ref)
+    vec_ref[0:4, :] = taps_ref[...]
+    vec_ref[V_BIAS:V_DECAY, :] = small_ref[0:3, :]
+    vec_ref[V_DECAY:V_DECAY + 1, :] = -8.0 * jnp.log1p(jnp.exp(-small_ref[3:4, :]))
     own_copy.wait()
     for load in loads:
         load.wait()
@@ -543,20 +576,7 @@
         vp[pl.ds(pl.multiple_of(block * rows + 8, 8), rows), :] = dot_nn(rows_in, value_w[...])
         gp[pl.ds(pl.multiple_of(block * rows, rows), rows), :] = dot_nn(rows_in, gate_w[...])
 
-    def arrive(distance, unused):
-        pl.when(distance > 0)(lambda: gather.take(distance))
-
-        def side(which, inner):
-            block = me - distance + 2 * distance * which
-            pl.when((block >= 0) & (block < count) & ((distance > 0) | (which == 0)))(lambda: project(block))
-            return inner
-
-        return lax.fori_loop(0, 2, side, unused)
-
-    lax.fori_loop(0, count, arrive, 0)
-    cots.start()
-
-    def mix(block, unused):
+    def mix(block):
         base = block * rows
         rec_forward(base, rows, vp, gp, mask_ref, vec_ref, rate_ref, inlet_ref,
                     mixed, state, conv, forget, inlet_gate, low, carry)
@@ -564,9 +584,31 @@
         for part in range(PARTS):
             held[block, part] = dot_nn(rows_in, out_w[:, part * width:(part + 1) * width]).astype(BF)
             scatter.first(block, part)
-        return unused
-
-    lax.fori_loop(0, count, mix, 0)
+
+    def mixed_by(block, distance):
+        return (distance >= count - 1) | ((distance >= me) & (block <= me + distance)
+                                          & (block < 2 * (distance - me + 1)))
+
+    def arrive(distance, unused):
+        pl.when(distance > 0)(lambda: gather.take(distance))
+        pl.when((distance == me + 1) & (me < count - 1))(cots.copy(me, 1).start)
+        pl.when((distance == count - me) & (me > 0))(cots.copy(me, -1).start)
+
+        def side(which, inner):
+            block = me - distance + 2 * distance * which
+            pl.when((block >= 0) & (block < count) & ((distance > 0) | (which == 0)))(lambda: project(block))
+            return inner
+
+        lax.fori_loop(0, 2, side, unused)
+
+        def turn(block, inner):
+            before = (distance > 0) & mixed_by(block, distance - 1)
+            pl.when(mixed_by(block, distance) & jnp.logical_not(before))(lambda: mix(block))
+            return inner
+
+        return lax.fori_loop(0, count, turn, unused)
+
+    lax.fori_loop(0, count, arrive, 0)
     saves = [pltpu.make_async_copy(source, target, out_sem.at[index]) for index, (source, target) in enumerate(
         ((mixed, mixed_out), (vp, vp_out), (gp, gp_out), (state, state_out), (conv, conv_out),
          (forget, forget_out), (inlet_gate, input_out)))]
@@ -581,13 +623,19 @@
     for distance in range(taken, count):
         cots.take(distance)
     row_sums = jnp.zeros((rows, 1), F32)
+    token_sums = jnp.zeros((rows, 1), F32)
     for part in range(PARTS):
         span = slice(part * width, (part + 1) * width)
         scatter.wait_total(part)
         total = scatter.total(part)
+        tokens = tokens_ref[:, span].astype(F32)
         row_sums = row_sums + jnp.sum(total * total, axis=1, keepdims=True)
-        middle_ref[:, span] = tokens_ref[:, span].astype(F32) + total
-    live_squares(live_ref, row_sums, stat_ref)
+        token_sums = token_sums + jnp.sum(tokens * tokens, axis=1, keepdims=True)
+        middle_ref[:, span] = tokens + total
+    stat_ref[...] = jnp.zeros(stat_ref.shape, F32)
+    stat_ref[0:1, :] += live_total(live_ref, token_sums)
+    stat_ref[1:2, :] += live_total(live_ref, row_sums)
+    stat_ref[2:3, :] += live_total(live_ref, jnp.ones((rows, 1), F32))
     for save in saves:
         save.wait()
     for block in range(count):
@@ -597,21 +645,23 @@
     scatter.drain()
 
 
-def call_mixer(count, tokens, gain, live, masks, vec, rate, inlet, cotangent, value_proj, gate_proj, mixer_out):
+def call_mixer(count, lengths, tokens, gain, live, taps, small, rate_heads, inlet_heads, cotangent, value_proj, gate_proj, mixer_out):
     rows, columns = tokens.shape
     channels = value_proj.shape[1]
     total = count * rows
     wide = jax.ShapeDtypeStruct((total, channels), F32)
     ahead = jax.ShapeDtypeStruct((total + 8, channels), F32)
     blocks = jax.ShapeDtypeStruct((count, rows, columns), BF)
+    square = jax.ShapeDtypeStruct((channels, channels), BF)
     return pl.pallas_call(
         functools.partial(mixer_kernel, count),
         out_shape=(
             jax.ShapeDtypeStruct((rows, columns), F32), jax.ShapeDtypeStruct((8, 128), F32),
+            jax.ShapeDtypeStruct((total + 8, 8), F32), jax.ShapeDtypeStruct((8, channels), F32), square, square,
             blocks, blocks, jax.ShapeDtypeStruct((total, channels), BF), ahead, wide, ahead, wide, wide, wide,
         ),
-        in_specs=[IN_VMEM] * 7 + [ANYWHERE] * 4,
-        out_specs=(IN_VMEM,) * 2 + (ANYWHERE,) * 9,
+        in_specs=[pl.BlockSpec(memory_space=pltpu.SMEM)] + [IN_VMEM] * 7 + [ANYWHERE] * 4,
+        out_specs=(IN_VMEM,) * 6 + (ANYWHERE,) * 9,
         scratch_shapes=[
             pltpu.VMEM((count, rows, columns), BF),
             pltpu.VMEM((columns, channels), BF),
@@ -635,7 +685,8 @@
         compiler_params=pltpu.CompilerParams(vmem_limit_bytes=VMEM_LIMIT, collective_id=1, has_side_effects=True),
         cost_estimate=pl.CostEstimate(flops=6 * total * columns * channels, bytes_accessed=40 * total * channels,
                                       transcendentals=6 * total * channels),
-    )(tokens, gain, live, masks, vec, rate, inlet, cotangent, value_proj, gate_proj, mixer_out)
+    )(lengths, tokens, gain, live, taps, small, rate_heads, inlet_heads, cotangent,
+      value_proj, gate_proj, mixer_out)
 
 
 def middle_kernel(count, groups, middle_grad_ref, middle_ref, live_ref, terms_hbm, out_hbm, mixed_hbm,
@@ -707,8 +758,8 @@
             cube.finish(rest)
             if rest + 1 < levels:
                 cube.start(rest + 1)
-    out_grad_ref[0:half, :] = cubes[0].result()
-    out_grad_ref[half:channels, :] = cubes[1].result()
+    cubes[0].result(out_grad_ref.at[0:half])
+    cubes[1].result(out_grad_ref.at[half:channels])
     row_sums = jnp.zeros((rows, 1), F32)
     for part in range(PARTS):
         span = slice(part * width, (part + 1) * width)
@@ -716,7 +767,7 @@
         total = scatter.total(part)
         row_sums = row_sums + jnp.sum(total * total, axis=1, keepdims=True)
         layer_ref[:, span] = (middle_ref[:, span] + total).astype(BF)
-    live_squares(live_ref, row_sums, stat_ref)
+    stat_ref[...] = jnp.zeros(stat_ref.shape, F32) + live_total(live_ref, row_sums)
     for block in range(count):
         dm_copy(block).wait()
     gather.drain()
@@ -757,13 +808,13 @@
 
 
 def input_kernel(count, groups, heads, tokens_ref, gain_ref, middle_grad_ref, mask_ref, vec_ref, rate_ref, inlet_ref,
-                 value_hbm, gate_hbm, normed_hbm, dm_hbm, vp_hbm, gp_hbm, state_hbm, conv_hbm, forget_hbm, input_hbm,
-                 input_grad_ref, gain_grad_ref, value_grad_ref, gate_grad_ref, small_ref, vec_grad_ref,
+                 dense_gain_ref, stat_ref, dense_stat_ref, value_hbm, gate_hbm, normed_hbm, dm_hbm, vp_hbm, gp_hbm, state_hbm, conv_hbm, forget_hbm, input_hbm,
+                 input_grad_ref, flat_ref, value_grad_ref, gate_grad_ref, full, vec_grad_ref,
                  value_w, gate_w, dm, vp, gp, state, conv, forget, inlet_gate, normed, vlow, glow, dzf, dzi, dconv,
-                 clow, sums, carry, held, slots, cube_a, slots_a, cube_b, slots_b, cube_c, slots_c, full,
-                 vec_held, vec_slots,
+                 clow, sums, carry, held, slots, cube_a, slots_a, cube_b, slots_b, cube_c, slots_c,
+                 vec_held, vec_slots, flat_held, flat_slots,
                  load_sem, block_sem, normed_sem, rs_send, rs_recv, a_send, a_recv, b_send, b_recv, c_send, c_recv,
-                 f_send, f_recv, v_send, v_recv):
+                 f_send, f_recv, v_send, v_recv, flat_send, flat_recv):
     me = lax.axis_index("mp")
     rows, columns = tokens_ref.shape
     channels = value_w.shape[1]
@@ -792,7 +843,7 @@
     carry[...] = zeros
     for row in range(8):
         sums[row] = zeros
-    greet(count, groups)
+    greet(count, groups, True)
     scatter = Scatter(count, held, slots, rs_send, rs_recv)
     order_a, order_b = orders(groups)
     cubes = (Cube(groups, order_a, cube_a, slots_a, a_send, a_recv),
@@ -840,19 +891,41 @@
         left = normed[slot].reshape(total_rows, chunk)
         cube_a[index] = dot_tn(left, vlow[...]).astype(BF)
         cube_b[index] = dot_tn(left, glow[...]).astype(BF)
+        part = index * chunk // width
+        inside = pl.ds(pl.multiple_of(index * chunk % width, chunk), chunk)
+        gain_row = jnp.zeros((1, chunk), F32)
+        for block in range(count):
+            gain_row = gain_row + jnp.sum(
+                normed[slot, block].astype(F32) * held[block, part, :, inside].astype(F32), axis=0, keepdims=True)
+        flat_held[0:1, pl.ds(pl.multiple_of(index * chunk, chunk), chunk)] = gain_row
         return unused
 
+    flat_held[...] = jnp.zeros(flat_held.shape, F32)
     lax.fori_loop(0, groups, weights, 0)
+    flat_held[0:1, :] = flat_held[0:1, :] / gain_ref[...]
+    flat_held[1:2, :] = dense_gain_ref[...]
+    for index, value in enumerate((stat_ref[0:1], stat_ref[1:2], dense_stat_ref[0:1], stat_ref[2:3])):
+        flat_held[2:3, index * 128:(index + 1) * 128] = value
+    peers = [("dp", bit) for bit in range(groups.bit_length() - 1)]
+    peers += [("mp", bit) for bit in range(count.bit_length() - 1)]
+
+    def flat_copy(index):
+        axis, bit = peers[index]
+        return pltpu.make_async_remote_copy(
+            src_ref=flat_held, dst_ref=flat_slots.at[index], send_sem=flat_send.at[index],
+            recv_sem=flat_recv.at[index], device_id={axis: partner_of(bit, axis)}, device_id_type=MESH)
+
+    flat_copy(0).start()
     cubes[0].start(0)
     cubes[1].start(0)
     slab = 2 * channels // groups
     for which, source in enumerate((dzf, dzi)):
         for index in range(heads):
             span = slice(index * head, (index + 1) * head)
-            at = which * channels + index * head
-            small_ref[at:at + head, :] = dot_tn(clow[:, span], source[:, span])
-    for index in range(groups):
-        cube_c[index] = small_ref[index * slab:(index + 1) * slab, :]
+            square = dot_tn(clow[:, span], source[:, span])
+            first = (which * channels + index * head) // slab
+            for piece in range(head // slab):
+                cube_c[first + piece] = square[piece * slab:(piece + 1) * slab]
     cubes[2].start(0)
     for row in range(8):
         vec_held[0, row:row + 1, :] = jnp.sum(sums[row], axis=0, keepdims=True)
@@ -866,6 +939,11 @@
     vec_copy(0).start()
 
     def advance(level):
+        if level < len(peers):
+            flat_copy(level).wait()
+            flat_held[...] += flat_slots[level]
+            if level + 1 < len(peers):
+                flat_copy(level + 1).start()
         if level < levels:
             for cube in cubes:
                 cube.finish(level)
@@ -877,9 +955,9 @@
                 vec_copy(level + 1).start()
             else:
                 vec_grad_ref[...] = vec_held[level] + vec_slots[level]
-                value_grad_ref[...] = cubes[0].result()
-                gate_grad_ref[...] = cubes[1].result()
-                full[lax.axis_index("dp")] = cubes[2].result()
+                cubes[0].result(value_grad_ref)
+                cubes[1].result(gate_grad_ref)
+                cubes[2].result(full.at[lax.axis_index("dp")])
                 spread.start(levels - 1)
         elif level < 2 * levels:
             back_level = 2 * levels - 1 - level
@@ -893,20 +971,18 @@
         if time > 1:
             advance(level)
             level += 1
-    for rest in range(level, 2 * levels):
+    for rest in range(level, max(2 * levels, len(peers))):
         advance(rest)
-    for index in range(groups):
-        small_ref[index * slab:(index + 1) * slab, :] = full[index]
-
+    flat_ref[...] = flat_held[...]
     def write(span, change):
         input_grad_ref[:, span] = (middle_grad_ref[:, span] + change).astype(BF)
 
-    norm_back(tokens_ref, gain_ref, scatter, gain_grad_ref, write)
+    norm_back(tokens_ref, gain_ref, scatter, None, write)
     scatter.drain()
 
 
-def call_input(count, groups, heads, tokens, gain, middle_grad, masks, vec, rate, inlet, value_proj, gate_proj,
-               normed_all, dm, vp, gp, state, conv, forget, inp):
+def call_input(count, groups, heads, tokens, gain, middle_grad, masks, vec, rate, inlet, dense_gain_grad, stat,
+               dense_stat, value_proj, gate_proj, normed_all, dm, vp, gp, state, conv, forget, inp):
     rows, columns = tokens.shape
     channels = value_proj.shape[1]
     total = count * rows
@@ -917,14 +993,15 @@
     ahead = pltpu.VMEM((2, rows + 8, channels), F32)
     low = pltpu.VMEM((total, channels), BF)
     levels = groups.bit_length() - 1
+    flats = levels + count.bit_length() - 1
     return pl.pallas_call(
         functools.partial(input_kernel, count, groups, heads),
         out_shape=(
-            jax.ShapeDtypeStruct((rows, columns), BF), jax.ShapeDtypeStruct((1, columns), F32),
+            jax.ShapeDtypeStruct((rows, columns), BF), jax.ShapeDtypeStruct((8, columns), F32),
             jax.ShapeDtypeStruct((chunk, channels), F32), jax.ShapeDtypeStruct((chunk, channels), F32),
-            jax.ShapeDtypeStruct((2 * channels, head), F32), jax.ShapeDtypeStruct((8, channels), F32),
+            jax.ShapeDtypeStruct((groups, slab, head), F32), jax.ShapeDtypeStruct((8, channels), F32),
         ),
-        in_specs=[IN_VMEM] * 7 + [ANYWHERE] * 10,
+        in_specs=[IN_VMEM] * 10 + [ANYWHERE] * 10,
         out_specs=(IN_VMEM,) * 6,
         scratch_shapes=[
             pltpu.VMEM((columns, channels), BF),
@@ -941,18 +1018,18 @@
             pltpu.VMEM((groups, chunk, channels), BF), pltpu.VMEM((groups - 1, chunk, channels), BF),
             pltpu.VMEM((groups, chunk, channels), BF), pltpu.VMEM((groups - 1, chunk, channels), BF),
             pltpu.VMEM((groups, slab, head), F32), pltpu.VMEM((groups - 1, slab, head), F32),
-            pltpu.VMEM((groups, slab, head), F32),
             pltpu.VMEM((levels, 8, channels), F32), pltpu.VMEM((levels, 8, channels), F32),
+            pltpu.VMEM((8, columns), F32), pltpu.VMEM((flats, 8, columns), F32),
             DMA((2,)), DMA((2, 7)), DMA((2,)), DMA((count, PARTS)), DMA((count + 1, PARTS)),
             DMA((groups - 1,)), DMA((groups - 1,)), DMA((groups - 1,)), DMA((groups - 1,)),
             DMA((groups - 1,)), DMA((groups - 1,)), DMA((groups - 1,)), DMA((groups - 1,)),
-            DMA((levels,)), DMA((levels,)),
+            DMA((levels,)), DMA((levels,)), DMA((flats,)), DMA((flats,)),
         ],
         compiler_params=pltpu.CompilerParams(vmem_limit_bytes=VMEM_LIMIT, collective_id=3, has_side_effects=True),
         cost_estimate=pl.CostEstimate(flops=8 * total * columns * channels, bytes_accessed=60 * total * channels,
                                       transcendentals=4 * total * channels),
-    )(tokens, gain, middle_grad, masks, vec, rate, inlet, value_proj, gate_proj, normed_all, dm, vp, gp, state, conv,
-      forget, inp)
+    )(tokens, gain, middle_grad, masks, vec, rate, inlet, dense_gain_grad, stat, dense_stat, value_proj, gate_proj,
+      normed_all, dm, vp, gp, state, conv, forget, inp)
 
 
 def spans(total):
@@ -1132,12 +1209,6 @@
     )(middle, gain, cot_all, dense_gate, dense_value, dense_down)
 
 
-def block_diagonal(heads):
-    count, width, unused = heads.shape
-    spread = heads[:, :, None, :] * jnp.eye(count, dtype=heads.dtype)[:, None, :, None]
-    return spread.reshape(count * width, count * width)
-
-
 def scatter_dp(values, dimension):
     return lax.psum_scatter(values, "dp", scatter_dimension=dimension, tiled=True).astype(F32)
 
@@ -1149,51 +1220,35 @@
     head_count, head_width = rate_weight.shape[:2]
     channels = head_count * head_width
     count = lax.axis_size("mp")
-    rows_total = count * tokens.shape[0]
-    offsets = doc_offsets(lengths[0], rows_total)
-    taps_here = jnp.arange(8, dtype=jnp.int32)
-    masks = (offsets[:, None] >= taps_here[None, :]).astype(F32)
-    masks = jnp.concatenate([masks, jnp.zeros((8, 8), F32)], axis=0)
-    vec = jnp.concatenate([
-        conv_taps,
-        jnp.stack([conv_bias, rate_bias, inlet_bias, -8.0 * jax.nn.softplus(-decay_param)]),
-    ], axis=0)
-    rate_square = block_diagonal(rate_weight).astype(BF)
-    inlet_square = block_diagonal(inlet_weight).astype(BF)
-    weights_live = live_mask.astype(F32)
-    live_column = weights_live[:, None]
-    middle, mixer_stat, normed_all, cot_all, mixed, vp, gp, state, conv, forget, inp = call_mixer(
-        count, tokens, mixer_gain[None, :], live_column, masks, vec, rate_square, inlet_square,
-        cotangent, value_proj, gate_proj, mixer_out)
+    live = live_mask[None, :]
+    middle, stat, masks, vec, rate_square, inlet_square, normed_all, cot_all, mixed, *saved = call_mixer(
+        count, lengths, tokens, mixer_gain[None, :], live, conv_taps,
+        jnp.stack([conv_bias, rate_bias, inlet_bias, decay_param]), rate_weight, inlet_weight, cotangent,
+        value_proj, gate_proj, mixer_out)
     middle_grad, dense_gain_grad, dense_terms, gate_weights, value_weights, down_weights = call_dense(
         count, groups, middle, dense_gain[None, :], cot_all, dense_gate, dense_value, dense_down)
     layer_out, dense_stat, mixer_out_sum, dm = call_middle(
-        count, groups, middle_grad, middle, live_column, dense_terms, mixer_out, mixed)
-    input_grad, mixer_gain_grad, value_proj_sum, gate_proj_sum, small, vec_sum = call_input(
+        count, groups, middle_grad, middle, live, dense_terms, mixer_out, mixed)
+    input_grad, flat, value_proj_sum, gate_proj_sum, small, vec_sum = call_input(
         count, groups, head_count, tokens, mixer_gain[None, :], middle_grad, masks, vec, rate_square, inlet_square,
-        value_proj, gate_proj, normed_all, dm, vp, gp, state, conv, forget, inp)
-    residual = tokens.astype(F32)
-    squares = jnp.stack([
-        jnp.sum(weights_live * jnp.sum(residual * residual, axis=1)), mixer_stat[0, 0], dense_stat[0, 0]])
-    mixer_gain_sum, dense_gain_sum, squares, live_count = lax.psum(
-        (mixer_gain_grad[0], dense_gain_grad[0], squares, jnp.sum(weights_live)), ("dp", "mp"))
-    branch_rms = jnp.sqrt(squares / (live_count * columns))
+        dense_gain_grad, stat, dense_stat, value_proj, gate_proj, normed_all, dm, *saved)
+    branch_rms = jnp.sqrt(flat[2, 0:384:128] / (flat[2, 384] * columns))
     decay_scale = 8.0 * jax.nn.sigmoid(-decay_param)
     return (
         layer_out,
         input_grad,
-        mixer_gain_sum,
+        flat[0],
         value_proj_sum,
         gate_proj_sum,
         vec_sum[0:4],
         vec_sum[4],
-        small[:channels].reshape(rate_weight.shape),
+        small[:groups // 2].reshape(rate_weight.shape),
         vec_sum[V_RATE],
-        small[channels:].reshape(rate_weight.shape),
+        small[groups // 2:].reshape(rate_weight.shape),
         vec_sum[V_INLET],
         vec_sum[V_DECAY] * decay_scale,
         mixer_out_sum,
-        dense_gain_sum,
+        flat[1],
         scatter_dp(gate_weights, 0),
         scatter_dp(value_weights, 0),
         scatter_dp(down_weights, 1),

time: 659 us -> 599 us (0.909)
  blocking collectives: 46.8 us -> 0 us
  other arithmetic: 17.8 us -> 9.24 us
    psum x1 -> x0, blocking collectives: 46.8 us -> none  [local(): lax.psum((mixer_gain_grad[0], dense_gain_grad[0], squares, jnp.sum(weight...]
    pallas_call x1, Pallas kernels: 191 us -> 181 us  [call_mixer(): pl.pallas_call(functools.partial(mixer_kernel, count), out_shape=(jax.Sha...]
    pallas_call x1, Pallas kernels: 118 us -> 127 us  [call_input(): pl.pallas_call(functools.partial(input_kernel, count, groups, heads), out...]
  transfers between devices with their start and end apart: 3 -> 3, of which waited for: 0 -> 0; matrix products, arithmetic and copies ran while one was open for 3% -> 3% of each run, Pallas kernels for 36% -> 40%
where the time goes in v4:
time: 599 us; the launch traced here: 593 us
  Pallas kernels  551 us (92%)
  local copies, waits for them, and re-layouts  16 us (3%)
  between operations  14.7 us (2%)
  other arithmetic  9.24 us (2%)
    pallas_call x1, Pallas kernels, call_mixer(): pl.pallas_call(functools.partial(mixer_kernel, count), out_shape=(jax.Sha...  181 us
    pallas_call x1, Pallas kernels, call_dense(): pl.pallas_call(functools.partial(dense_kernel, count, groups), out_shape=...  132 us
    pallas_call x1, Pallas kernels, call_input(): pl.pallas_call(functools.partial(input_kernel, count, groups, heads), out...  127 us
    pallas_call x1, Pallas kernels, call_middle(): pl.pallas_call(functools.partial(middle_kernel, count, groups), out_shape...  112 us
  transfers between devices with their start and end apart: 3, of which 0 were waited for; matrix products, arithmetic and copies ran while one was open for 3% of the time, Pallas kernels for 40%

profile of v4, /device:TPU:0, one launch (start us, length us, event | category | flops | bytes accessed | tf_op | source)
XLA Modules:
  0.0 592.9 jit_solution(9372759023566834080)
XLA Ops:
  7.2 0.0 reduce-scatter.8.cloned.1.call-start
  7.2 0.7 stack.15
  7.9 0.7 stack.16
  8.6 0.7 stack.17
  9.3 0.7 stack.18
  10.0 0.6 pad_maximum_fusion.small_ref
  10.6 181.0 %shard_map.322 = (f32[256,2048]{1,0:T(8,128)}, f32[8,128]{1,0:T(8,128)}, f32[1032,8]{1,0:T(8,128)}, f32[8,640]{1,0:T(8,128)}, bf16[640,640]{1,0:T(8,128)(2,1)}, ...) custom-call(s32[1,4]{1,0:T(1,128)} %lengths_ref.1, ...), custom_call_target="tpu_custom_call" | custom-call | flops 8053063680 | bytes 26214400 | tf_op jit(solution)/shard_map/pallas_call | solution.py:656
  191.7 131.6 %shard_map.323 = (f32[256,2048]{1,0:T(8,128)}, f32[1,2048]{1,0:T(1,128)}, bf16[4,4,256,512]{3,2,1,0:T(8,128)(2,1)}, bf16[2048,1536]{1,0:T(8,128)(2,1)}, bf16[204...) custom-call(f32[256,2048]{1,0:T(8,128)} %get-tuple-element.49.middle_ref, f32[1,2048]{1,0:T(1,128)} %bitcast.10, ...), custom_call_target="tpu_custom_call" | custom-call | flops 57982058496 | bytes 37748736 | tf_op jit(solution)/shard_map/pallas_call | solution.py:1177
  323.3 0.0 reduce-scatter.8.cloned.1.call-update
  323.3 0.0 reduce-scatter.6.cloned.1.call-start
  323.4 0.7 reduce-scatter.6.cloned.1.call-update
  324.1 0.0 reduce-scatter.4.cloned.1.call-start
  324.1 0.7 reduce-scatter.4.cloned.1.call-update
  324.8 111.7 %shard_map.324 = (bf16[256,2048]{1,0:T(8,128)(2,1)}, f32[8,128]{1,0:T(8,128)}, f32[640,256]{1,0:T(8,128)}, f32[1024,640]{1,0:T(8,128)}) custom-call(f32[256,2048]{1,0:T(8,128)} %get-tuple-element.51.middle_grad_ref, f32[256,2048]{1,0:T(8,128)} %get-tuple-element.49.middle_ref, s32[1,256]{1,0:T(1,128)} %bitcast.14, ...), custom_call_target="tpu_custom_call" | custom-call | flops 5368709120 | bytes 26214400 | tf_op jit(solution)/shard_map/pallas_call | solution.py:782
  436.5 0.0 copy-start.5
  436.5 127.1 %shard_map.325 = (bf16[256,2048]{1,0:T(8,128)(2,1)}, f32[8,2048]{1,0:T(8,128)}, f32[256,640]{1,0:T(8,128)}, f32[256,640]{1,0:T(8,128)}, f32[8,160,160]{2,1,0:T(8,128)}, /*index=5*/f32[8,640]{1,0:T(8,128)}) custom-call(bf16[256,2048]{1,0:T(8,128)(2,1)} %tokens_ref.3, f32[1,2048]{1,0:T(1,128)} %bitcast.12, f32[256,2048]{1,0:T(8,128)} %get-tuple-element.51.middle_grad_ref, ...), custom_call_target="tpu_custom_call" | custom-call | flops 10737418240 | bytes 39321600 | tf_op jit(solution)/shard_map/pallas_call | solution.py:997
  563.6 1.2 slice.43
  564.8 0.8 slice.42
  565.6 1.3 slice.34
  567.6 1.5 slice_reduce_fusion
  569.1 0.5 sqrt_bitcast_fusion
  569.6 0.6 multiply_multiply_fusion
  570.2 2.4 fusion
  572.6 1.5 fusion.1
  574.2 2.4 convert_element_type.11
  576.6 2.5 convert_element_type.10
  579.1 2.5 convert_element_type.9
  581.7 1.0 copy.42
  582.6 1.0 copy.43
  583.6 0.8 copy.44
  584.5 0.8 copy.45
  585.3 0.8 copy.46
  (14 shorter events, 0.0 us)
Async XLA Ops:
  7.2 567.0 %reduce-scatter.8.cloned.1.call-start = ((), (), s32[]{:S(2)}) async-start(), calls=%async_computation.5 | async-start | bytes 7077888 | tf_op jit(solution)/shard_map/reduce_scatter | solution.py:1213
  323.3 253.2 %reduce-scatter.6.cloned.1.call-start = ((), (), s32[]{:S(2)}) async-start(), calls=%async_computation.4 | async-start | bytes 7077888 | tf_op jit(solution)/shard_map/reduce_scatter | solution.py:1213
  324.1 255.0 %reduce-scatter.4.cloned.1.call-start = ((), (), s32[]{:S(2)}) async-start(), calls=%async_computation.3 | async-start | bytes 7077888 | tf_op jit(solution)/shard_map/reduce_scatter | solution.py:1213
  436.5 133.1 %copy-start.5 = (f32[640]{0:T(1024)S(1)}, f32[640]{0:T(1024)}, u32[]{:S(2)}) copy-start(f32[640]{0:T(1024)} %param.32) | copy-start | bytes 7684
  576.6 5.1 copy-start
  579.1 3.5 copy-start.1
  581.7 2.0 copy-start.4
  581.7 2.8 copy-start.3
  582.6 2.7 copy-start.2
Sparse Core Ops, SparseCore 0:
  323.4 59.9 reduce-scatter.7
  387.2 69.7 reduce-scatter.5
  460.4 82.4 reduce-scatter.3

commit v5 on v4

--- a/solution.py
+++ b/solution.py
@@ -436,16 +436,22 @@
             device_id_type=MESH,
         ).wait_recv()
 
-    def pass_on(self, time, up_near, down_near):
+    def passing(self, time, up_near, down_near):
         last = self.count - 1
         up = time + 1 - self.me if up_near else last + self.me - time
         down = 2 * last - 1 - self.me - time if down_near else time - last + self.me
         up_here = (self.me > 0) & (up > self.me) & (up <= last)
         down_here = (self.me < last) & (down < self.me) & (down >= 0)
-
+        return up, up_here, down, down_here
+
+    def pass_one(self, time, part, up_near, down_near):
+        up, up_here, down, down_here = self.passing(time, up_near, down_near)
+        pl.when(up_here)(lambda: self.pass_part(up, part, 1))
+        pl.when(down_here)(lambda: self.pass_part(down, part, -1))
+
+    def pass_on(self, time, up_near, down_near):
         def step(part, unused):
-            pl.when(up_here)(lambda: self.pass_part(up, part, 1))
-            pl.when(down_here)(lambda: self.pass_part(down, part, -1))
+            self.pass_one(time, part, up_near, down_near)
             return unused
 
         lax.fori_loop(0, PARTS, step, 0)
@@ -531,7 +537,8 @@
         square_ref[span, span] = heads_ref[head].astype(BF)
 
 
-def mixer_kernel(count, lengths_ref, tokens_ref, gain_ref, live_ref, taps_ref, small_ref, rate_heads_ref, inlet_heads_ref,
+def mixer_kernel(count, lengths_ref, tokens_ref, gain_ref, live_ref, taps_ref, shift_ref, rate_bias_ref,
+                 inlet_bias_ref, decay_ref, rate_heads_ref, inlet_heads_ref,
                  cot_hbm, value_hbm, gate_hbm, out_hbm,
                  middle_ref, stat_ref, mask_ref, vec_ref, rate_ref, inlet_ref,
                  normed_all, cot_all, mixed_out, vp_out, gp_out, state_out, conv_out, forget_out, input_out,
@@ -561,8 +568,10 @@
     fill_square(rate_heads_ref, rate_ref)
     fill_square(inlet_heads_ref, inlet_ref)
     vec_ref[0:4, :] = taps_ref[...]
-    vec_ref[V_BIAS:V_DECAY, :] = small_ref[0:3, :]
-    vec_ref[V_DECAY:V_DECAY + 1, :] = -8.0 * jnp.log1p(jnp.exp(-small_ref[3:4, :]))
+    vec_ref[V_BIAS:V_BIAS + 1, :] = shift_ref[...].reshape(1, channels)
+    vec_ref[V_RATE:V_RATE + 1, :] = rate_bias_ref[...].reshape(1, channels)
+    vec_ref[V_INLET:V_INLET + 1, :] = inlet_bias_ref[...].reshape(1, channels)
+    vec_ref[V_DECAY:V_DECAY + 1, :] = -8.0 * jnp.log1p(jnp.exp(-decay_ref[...].reshape(1, channels)))
     own_copy.wait()
     for load in loads:
         load.wait()
@@ -645,7 +654,7 @@
     scatter.drain()
 
 
-def call_mixer(count, lengths, tokens, gain, live, taps, small, rate_heads, inlet_heads, cotangent, value_proj, gate_proj, mixer_out):
+def call_mixer(count, lengths, tokens, gain, live, taps, vectors, rate_heads, inlet_heads, cotangent, value_proj, gate_proj, mixer_out):
     rows, columns = tokens.shape
     channels = value_proj.shape[1]
     total = count * rows
@@ -660,7 +669,7 @@
             jax.ShapeDtypeStruct((total + 8, 8), F32), jax.ShapeDtypeStruct((8, channels), F32), square, square,
             blocks, blocks, jax.ShapeDtypeStruct((total, channels), BF), ahead, wide, ahead, wide, wide, wide,
         ),
-        in_specs=[pl.BlockSpec(memory_space=pltpu.SMEM)] + [IN_VMEM] * 7 + [ANYWHERE] * 4,
+        in_specs=[pl.BlockSpec(memory_space=pltpu.SMEM)] + [IN_VMEM] * 10 + [ANYWHERE] * 4,
         out_specs=(IN_VMEM,) * 6 + (ANYWHERE,) * 9,
         scratch_shapes=[
             pltpu.VMEM((count, rows, columns), BF),
@@ -685,14 +694,15 @@
         compiler_params=pltpu.CompilerParams(vmem_limit_bytes=VMEM_LIMIT, collective_id=1, has_side_effects=True),
         cost_estimate=pl.CostEstimate(flops=6 * total * columns * channels, bytes_accessed=40 * total * channels,
                                       transcendentals=6 * total * channels),
-    )(lengths, tokens, gain, live, taps, small, rate_heads, inlet_heads, cotangent,
+    )(lengths, tokens, gain, live, taps, *vectors, rate_heads, inlet_heads, cotangent,
       value_proj, gate_proj, mixer_out)
 
 
 def middle_kernel(count, groups, middle_grad_ref, middle_ref, live_ref, terms_hbm, out_hbm, mixed_hbm,
-                  layer_ref, stat_ref, out_grad_ref, dm_hbm,
-                  low, out_w, mixed, dm, held, slots, cube_a, slots_a, cube_b, slots_b,
-                  load_sem, dm_sem, ag_send, ag_recv, rs_send, rs_recv, a_send, a_recv, b_send, b_recv):
+                  gate_hbm, value_hbm, layer_ref, stat_ref, out_grad_ref, gate_sum_ref, value_sum_ref, dm_hbm,
+                  low, out_w, mixed, dm, held, slots, cube_a, slots_a, cube_b, slots_b, gate_held, gate_slots, value_held, value_slots,
+                  load_sem, dm_sem, ag_send, ag_recv, rs_send, rs_recv, a_send, a_recv, b_send, b_recv,
+                  gate_send, gate_recv, value_send, value_recv):
     me = lax.axis_index("mp")
     rows, columns = middle_ref.shape
     channels = out_w.shape[0]
@@ -700,7 +710,7 @@
     chunk = columns // groups
     half = channels // 2
     loads = [pltpu.make_async_copy(source, target, load_sem.at[index]) for index, (source, target) in enumerate(
-        ((out_hbm, out_w), (mixed_hbm, mixed), (terms_hbm, held)))]
+        ((gate_hbm, gate_held), (value_hbm, value_held), (out_hbm, out_w), (mixed_hbm, mixed), (terms_hbm, held)))]
     for load in loads:
         load.start()
     low[me] = middle_grad_ref[...].astype(BF)
@@ -710,9 +720,20 @@
     order_a, order_b = orders(groups)
     cubes = (Cube(groups, order_a, cube_a, slots_a, a_send, a_recv),
              Cube(groups, order_b, cube_b, slots_b, b_send, b_recv))
+    dense_cubes = (Cube(groups, order_a, gate_held, gate_slots, gate_send, gate_recv),
+                   Cube(groups, order_b, value_held, value_slots, value_send, value_recv))
+    levels = len(order_a)
     gather.start()
     for load in loads:
         load.wait()
+    for cube in dense_cubes:
+        cube.start(0)
+
+    def dense_advance(level):
+        for cube in dense_cubes:
+            cube.finish(level)
+            if level + 1 < levels:
+                cube.start(level + 1)
 
     def dm_copy(block):
         return pltpu.make_async_copy(dm.at[block], dm_hbm.at[pl.ds(pl.multiple_of(block * rows, rows), rows)],
@@ -723,6 +744,7 @@
         dm_copy(block).start()
 
     back(me)
+    dense_advance(0)
     for distance in range(1, count):
         gather.take(distance)
         if distance == 1:
@@ -732,6 +754,9 @@
                     pl.when(me == count - 1)(scatter.copy(step, part, -1).start)
         pl.when(me - distance >= 0)(lambda: back(me - distance))
         pl.when(me + distance < count)(lambda: back(me + distance))
+        if distance == count - 2:
+            scatter.pass_on(1, False, False)
+            dense_advance(1)
 
     def out_grad(index, unused):
         right = low[:, :, pl.ds(pl.multiple_of(index * chunk, chunk), chunk)].reshape(count * rows, chunk)
@@ -741,13 +766,17 @@
         return unused
 
     lax.fori_loop(0, groups, out_grad, 0)
-    levels = len(order_a)
     for cube in cubes:
         cube.start(0)
     level = 0
-    for time in scatter.times():
+    for time in list(scatter.times())[1:]:
         scatter.pass_on(time, False, False)
-        if level < levels and time > 1:
+        if time == 2:
+            for rest in range(2, levels):
+                dense_advance(rest)
+            dense_cubes[0].result(gate_sum_ref)
+            dense_cubes[1].result(value_sum_ref)
+        if level < levels:
             for cube in cubes:
                 cube.finish(level)
                 if level + 1 < levels:
@@ -774,19 +803,22 @@
     scatter.drain()
 
 
-def call_middle(count, groups, middle_grad, middle, live, terms, mixer_out, mixed):
+def call_middle(count, groups, middle_grad, middle, live, terms, mixer_out, mixed, gate_weights, value_weights):
     rows, columns = middle.shape
     channels = mixer_out.shape[0]
     total = count * rows
     chunk = columns // groups
+    units = gate_weights.shape[1]
+    split = (groups, chunk, units)
     return pl.pallas_call(
         functools.partial(middle_kernel, count, groups),
         out_shape=(
             jax.ShapeDtypeStruct((rows, columns), BF), jax.ShapeDtypeStruct((8, 128), F32),
-            jax.ShapeDtypeStruct((channels, chunk), F32), jax.ShapeDtypeStruct((total, channels), F32),
+            jax.ShapeDtypeStruct((channels, chunk), F32), jax.ShapeDtypeStruct((chunk, units), F32),
+            jax.ShapeDtypeStruct((chunk, units), F32), jax.ShapeDtypeStruct((total, channels), F32),
         ),
-        in_specs=[IN_VMEM] * 3 + [ANYWHERE] * 3,
-        out_specs=(IN_VMEM, IN_VMEM, IN_VMEM, ANYWHERE),
+        in_specs=[IN_VMEM] * 3 + [ANYWHERE] * 5,
+        out_specs=(IN_VMEM,) * 5 + (ANYWHERE,),
         scratch_shapes=[
             pltpu.VMEM((count, rows, columns), BF),
             pltpu.VMEM((channels, columns), BF),
@@ -798,13 +830,16 @@
             pltpu.VMEM((groups - 1, channels // 2, chunk), BF),
             pltpu.VMEM((groups, channels // 2, chunk), BF),
             pltpu.VMEM((groups - 1, channels // 2, chunk), BF),
-            DMA((3,)), DMA((count,)), DMA((2, count)), DMA((count,)), DMA((count, PARTS)), DMA((count + 1, PARTS)),
+            pltpu.VMEM(split, BF), pltpu.VMEM((groups - 1, chunk, units), BF),
+            pltpu.VMEM(split, BF), pltpu.VMEM((groups - 1, chunk, units), BF),
+            DMA((5,)), DMA((count,)), DMA((2, count)), DMA((count,)), DMA((count, PARTS)), DMA((count + 1, PARTS)),
+            DMA((groups - 1,)), DMA((groups - 1,)), DMA((groups - 1,)), DMA((groups - 1,)),
             DMA((groups - 1,)), DMA((groups - 1,)), DMA((groups - 1,)), DMA((groups - 1,)),
         ],
         compiler_params=pltpu.CompilerParams(vmem_limit_bytes=VMEM_LIMIT, collective_id=2, has_side_effects=True),
         cost_estimate=pl.CostEstimate(flops=4 * total * columns * channels, bytes_accessed=40 * total * channels,
                                       transcendentals=0),
-    )(middle_grad, middle, live, terms, mixer_out, mixed)
+    )(middle_grad, middle, live, terms, mixer_out, mixed, gate_weights.reshape(split), value_weights.reshape(split))
 
 
 def input_kernel(count, groups, heads, tokens_ref, gain_ref, middle_grad_ref, mask_ref, vec_ref, rate_ref, inlet_ref,
@@ -965,13 +1000,19 @@
             if back_level > 0:
                 spread.start(back_level - 1)
 
+    stages = max(2 * levels, len(peers))
+    slots_all = [(time, part) for time in scatter.times() for part in range(PARTS)]
+    early = max(len(slots_all) - 5 - 2 * (stages - 4), 0)
+    for time in range(1, early // PARTS + 1):
+        scatter.pass_on(time, False, True)
     level = 0
-    for time in scatter.times():
-        scatter.pass_on(time, False, True)
-        if time > 1:
+    for index in range(early // PARTS * PARTS, len(slots_all)):
+        scatter.pass_one(*slots_all[index], False, True)
+        turn = len(slots_all) - index - 1
+        if level < stages and (turn <= 4 or turn % 2 == 0) and turn > 0 and stages - level >= min(turn, 4):
             advance(level)
             level += 1
-    for rest in range(level, max(2 * levels, len(peers))):
+    for rest in range(level, stages):
         advance(rest)
     flat_ref[...] = flat_held[...]
     def write(span, change):
@@ -1223,12 +1264,13 @@
     live = live_mask[None, :]
     middle, stat, masks, vec, rate_square, inlet_square, normed_all, cot_all, mixed, *saved = call_mixer(
         count, lengths, tokens, mixer_gain[None, :], live, conv_taps,
-        jnp.stack([conv_bias, rate_bias, inlet_bias, decay_param]), rate_weight, inlet_weight, cotangent,
+        (conv_bias, rate_bias, inlet_bias, decay_param), rate_weight, inlet_weight, cotangent,
         value_proj, gate_proj, mixer_out)
     middle_grad, dense_gain_grad, dense_terms, gate_weights, value_weights, down_weights = call_dense(
         count, groups, middle, dense_gain[None, :], cot_all, dense_gate, dense_value, dense_down)
-    layer_out, dense_stat, mixer_out_sum, dm = call_middle(
-        count, groups, middle_grad, middle, live, dense_terms, mixer_out, mixed)
+    layer_out, dense_stat, mixer_out_sum, gate_sum, value_sum, dm = call_middle(
+        count, groups, middle_grad, middle, live, dense_terms, mixer_out, mixed, gate_weights, value_weights)
+    dm, down_weights = lax.optimization_barrier((dm, down_weights))
     input_grad, flat, value_proj_sum, gate_proj_sum, small, vec_sum = call_input(
         count, groups, head_count, tokens, mixer_gain[None, :], middle_grad, masks, vec, rate_square, inlet_square,
         dense_gain_grad, stat, dense_stat, value_proj, gate_proj, normed_all, dm, *saved)
@@ -1249,8 +1291,8 @@
         vec_sum[V_DECAY] * decay_scale,
         mixer_out_sum,
         flat[1],
-        scatter_dp(gate_weights, 0),
-        scatter_dp(value_weights, 0),
+        gate_sum,
+        value_sum,
         scatter_dp(down_weights, 1),
         branch_rms,
     )

time: 599 us -> 580 us (0.968)
  Pallas kernels: 551 us -> 540 us
    pallas_call x1, Pallas kernels: 112 us -> 104 us  [call_middle(): pl.pallas_call(functools.partial(middle_kernel, count, groups), out_shape...]
  transfers between devices with their start and end apart: 3 -> 1, of which waited for: 0 -> 0; matrix products, arithmetic and copies ran while one was open for 3% -> 2% of each run, Pallas kernels for 40% -> 22%
where the time goes in v5:
time: 580 us; the launch traced here: 575 us
  Pallas kernels  540 us (93%)
  local copies, waits for them, and re-layouts  15.7 us (3%)
  between operations  15 us (3%)
    pallas_call x1, Pallas kernels, call_mixer(): pl.pallas_call(functools.partial(mixer_kernel, count), out_shape=(jax.Sha...  181 us
    pallas_call x1, Pallas kernels, call_dense(): pl.pallas_call(functools.partial(dense_kernel, count, groups), out_shape=...  132 us
    pallas_call x1, Pallas kernels, call_input(): pl.pallas_call(functools.partial(input_kernel, count, groups, heads), out...  124 us
    pallas_call x1, Pallas kernels, call_middle(): pl.pallas_call(functools.partial(middle_kernel, count, groups), out_shape...  104 us
  transfers between devices with their start and end apart: 1, of which 0 were waited for; matrix products, arithmetic and copies ran while one was open for 2% of the time, Pallas kernels for 22%

profile of v5, /device:TPU:0, one launch (start us, length us, event | category | flops | bytes accessed | tf_op | source)
XLA Modules:
  0.0 574.5 jit_solution(11830876814029323402)
XLA Ops:
  7.2 0.0 reduce-scatter.2.cloned.1.call-start
  7.2 181.1 %shard_map.322 = (f32[256,2048]{1,0:T(8,128)}, f32[8,128]{1,0:T(8,128)}, f32[1032,8]{1,0:T(8,128)}, f32[8,640]{1,0:T(8,128)}, bf16[640,640]{1,0:T(8,128)(2,1)}, ...) custom-call(s32[1,4]{1,0:T(1,128)} %lengths_ref.1, ...), custom_call_target="tpu_custom_call" | custom-call | flops 8053063680 | bytes 26214400 | tf_op jit(solution)/shard_map/pallas_call | solution.py:665
  188.4 131.7 %shard_map.323 = (f32[256,2048]{1,0:T(8,128)}, f32[1,2048]{1,0:T(1,128)}, bf16[4,4,256,512]{3,2,1,0:T(8,128)(2,1)}, bf16[2048,1536]{1,0:T(8,128)(2,1)}, bf16[204...) custom-call(f32[256,2048]{1,0:T(8,128)} %get-tuple-element.53.middle_ref, f32[1,2048]{1,0:T(1,128)} %bitcast.16, ...), custom_call_target="tpu_custom_call" | custom-call | flops 57982058496 | bytes 37748736 | tf_op jit(solution)/shard_map/pallas_call | solution.py:1218
  320.1 103.8 %shard_map.324 = (bf16[256,2048]{1,0:T(8,128)(2,1)}, f32[8,128]{1,0:T(8,128)}, f32[640,256]{1,0:T(8,128)}, f32[256,1536]{1,0:T(8,128)}, f32[256,1536]{1,0:T(8,128)}, /*index=5*/f32[1024,640]{1,0:T(8,128)}) custom-call(f32[256,2048]{1,0:T(8,128)} %get-tuple-element.55.middle_grad_ref, f32[256,2048]{1,0:T(8,128)} %get-tuple-element.53.middle_ref, ...), custom_call_target="tpu_custom_call" | custom-call | flops 5368709120 | bytes 26214400 | tf_op jit(solution)/shard_map/pallas_call | solution.py:813
  424.0 0.0 reduce-scatter.2.cloned.1.call-update
  424.0 0.0 copy-start.7
  424.0 123.6 %shard_map.325 = (bf16[256,2048]{1,0:T(8,128)(2,1)}, f32[8,2048]{1,0:T(8,128)}, f32[256,640]{1,0:T(8,128)}, f32[256,640]{1,0:T(8,128)}, f32[8,160,160]{2,1,0:T(8,128)}, /*index=5*/f32[8,640]{1,0:T(8,128)}) custom-call(bf16[256,2048]{1,0:T(8,128)(2,1)} %tokens_ref.3, f32[1,2048]{1,0:T(1,128)} %bitcast.18, f32[256,2048]{1,0:T(8,128)} %get-tuple-element.55.middle_grad_ref, ...), custom_call_target="tpu_custom_call" | custom-call | flops 10737418240 | bytes 39321600 | tf_op jit(solution)/shard_map/pallas_call | solution.py:1038
  547.6 0.0 copy-start.2
  547.6 1.3 slice.43
  548.9 0.8 slice.42
  549.7 1.3 slice.34
  551.7 1.5 slice_reduce_fusion
  553.2 0.5 sqrt_bitcast_fusion
  553.7 0.0 copy-done.7
  553.7 0.6 multiply_multiply_fusion
  554.3 2.4 fusion
  556.8 1.6 fusion.1
  558.3 2.4 convert_element_type.3
  560.7 0.0 copy-done.2
  560.7 1.0 copy.44
  561.7 0.0 copy-done.3
  561.7 1.0 copy.45
  562.7 0.0 copy-done.6
  562.7 0.8 copy.46
  563.5 0.0 copy-done.5
  563.5 0.8 copy.47
  564.4 0.0 copy-done.4
  564.4 0.8 copy.48
  565.2 0.0 copy-done.1
  565.2 1.1 copy.49
  566.4 0.0 copy-done
  566.4 1.1 copy.50
  (7 shorter events, 0.0 us)
Async XLA Ops:
  7.2 551.1 %reduce-scatter.2.cloned.1.call-start = ((), (), s32[]{:S(2)}) async-start(), calls=%async_computation.1 | async-start | bytes 7077888 | tf_op jit(solution)/shard_map/reduce_scatter | solution.py:1254
  424.0 129.7 %copy-start.7 = (f32[640]{0:T(1024)S(1)}, f32[640]{0:T(1024)}, u32[]{:S(2)}) copy-start(f32[640]{0:T(1024)} %decay_ref.1) | copy-start | bytes 7684
  547.6 13.1 %copy-start.2 = (bf16[256,2048]{1,0:T(8,128)(2,1)S(1)}, bf16[256,2048]{1,0:T(8,128)(2,1)}, u32[]{:S(2)}) copy-start(bf16[256,2048]{1,0:T(8,128)(2,1)} %get-tuple-element.114) | copy-start | bytes 3145732
  556.8 4.9 copy-start.3
  560.7 2.0 copy-start.6
  560.7 2.8 copy-start.5
  561.7 2.7 copy-start.4
  561.7 3.5 copy-start.1
  563.5 2.8 copy-start
Sparse Core Ops, SparseCore 0:
  424.1 70.2 reduce-scatter.1

commit v6 on v5

--- a/solution.py
+++ b/solution.py
@@ -373,18 +373,25 @@
         self.hand_on(self.me, 1)
         self.hand_on(self.me, -1)
 
-    def take(self, distance):
-        low, high = self.me - distance, self.me + distance
+    def take_low(self, distance):
+        low = self.me - distance
 
         @pl.when(low >= 0)
         def _():
             self.copy(low, -1).wait_recv()
             self.hand_on(low, 1)
 
+    def take_high(self, distance):
+        high = self.me + distance
+
         @pl.when(high < self.count)
         def _():
             self.copy(high, 1).wait_recv()
             self.hand_on(high, -1)
+
+    def take(self, distance):
+        self.take_low(distance)
+        self.take_high(distance)
 
     def drain(self):
         def step(block, unused):
@@ -439,7 +446,8 @@
     def passing(self, time, up_near, down_near):
         last = self.count - 1
         up = time + 1 - self.me if up_near else last + self.me - time
-        down = 2 * last - 1 - self.me - time if down_near else time - last + self.me
+        down = {True: 2 * last - 1 - self.me - time, False: time - last + self.me, None: time - self.count + self.me}[
+            down_near]
         up_here = (self.me > 0) & (up > self.me) & (up <= last)
         down_here = (self.me < last) & (down < self.me) & (down >= 0)
         return up, up_here, down, down_here
@@ -623,14 +631,20 @@
          (forget, forget_out), (inlet_gate, input_out)))]
     for save in saves:
         save.start()
-    taken = 1
+    cots.take(1)
+    below, above = 2, 2
     for time in scatter.times():
-        if taken < count and time >= 2 * taken - 1:
-            cots.take(taken)
-            taken += 1
+        if below < count and time >= 2 * below - 2:
+            cots.take_low(below)
+            below += 1
+        if above < count and time >= 2 * above - 1:
+            cots.take_high(above)
+            above += 1
         scatter.pass_on(time, True, False)
-    for distance in range(taken, count):
-        cots.take(distance)
+    for distance in range(below, count):
+        cots.take_low(distance)
+    for distance in range(above, count):
+        cots.take_high(distance)
     row_sums = jnp.zeros((rows, 1), F32)
     token_sums = jnp.zeros((rows, 1), F32)
     for part in range(PARTS):
@@ -908,7 +922,8 @@
             span = slice(part * width, (part + 1) * width)
             held[block, part] = (dot_nt(vlow[window, :], value_w[span, :])
                                  + dot_nt(glow[window, :], gate_w[span, :])).astype(BF)
-            scatter.first(block, part)
+            pl.when((me == 0) & (block > 0))(scatter.copy(block, part, 1).start)
+            pl.when((me == count - 1) & (block == count - 2))(scatter.copy(block, part, -1).start)
         return unused
 
     def normed_copy(index, slot):
@@ -918,6 +933,9 @@
 
     normed_copy(0, 0).start()
     lax.fori_loop(0, count, back, 0)
+    for block in range(count - 2):
+        for part in range(PARTS):
+            pl.when(me == count - 1)(scatter.copy(block, part, -1).start)
 
     def weights(index, unused):
         slot = index % 2
@@ -1004,10 +1022,10 @@
     slots_all = [(time, part) for time in scatter.times() for part in range(PARTS)]
     early = max(len(slots_all) - 5 - 2 * (stages - 4), 0)
     for time in range(1, early // PARTS + 1):
-        scatter.pass_on(time, False, True)
+        scatter.pass_on(time, False, None)
     level = 0
     for index in range(early // PARTS * PARTS, len(slots_all)):
-        scatter.pass_one(*slots_all[index], False, True)
+        scatter.pass_one(*slots_all[index], False, None)
         turn = len(slots_all) - index - 1
         if level < stages and (turn <= 4 or turn % 2 == 0) and turn > 0 and stages - level >= min(turn, 4):
             advance(level)

time: 580 us -> 575 us (level)
  transfers between devices with their start and end apart: 1 -> 1, of which waited for: 0 -> 0; matrix products, arithmetic and copies ran while one was open for 2% -> 2% of each run, Pallas kernels for 22% -> 21%
where the time goes in v6:
time: 575 us; the launch traced here: 569 us
  Pallas kernels  535 us (93%)
  local copies, waits for them, and re-layouts  15.7 us (3%)
  between operations  15 us (3%)
    pallas_call x1, Pallas kernels, call_mixer(): pl.pallas_call(functools.partial(mixer_kernel, count), out_shape=(jax.Sha...  181 us
    pallas_call x1, Pallas kernels, call_dense(): pl.pallas_call(functools.partial(dense_kernel, count, groups), out_shape=...  132 us
    pallas_call x1, Pallas kernels, call_input(): pl.pallas_call(functools.partial(input_kernel, count, groups, heads), out...  118 us
    pallas_call x1, Pallas kernels, call_middle(): pl.pallas_call(functools.partial(middle_kernel, count, groups), out_shape...  104 us
  transfers between devices with their start and end apart: 1, of which 0 were waited for; matrix products, arithmetic and copies ran while one was open for 2% of the time, Pallas kernels for 21%

profile of v6, /device:TPU:0, one launch (start us, length us, event | category | flops | bytes accessed | tf_op | source)
XLA Modules:
  0.0 569.2 jit_solution(7558619782782776297)
XLA Ops:
  7.2 0.0 reduce-scatter.2.cloned.1.call-start
  7.2 181.1 %shard_map.322 = (f32[256,2048]{1,0:T(8,128)}, f32[8,128]{1,0:T(8,128)}, f32[1032,8]{1,0:T(8,128)}, f32[8,640]{1,0:T(8,128)}, bf16[640,640]{1,0:T(8,128)(2,1)}, ...) custom-call(s32[1,4]{1,0:T(1,128)} %lengths_ref.1, ...), custom_call_target="tpu_custom_call" | custom-call | flops 8053063680 | bytes 26214400 | tf_op jit(solution)/shard_map/pallas_call | solution.py:679
  188.4 131.7 %shard_map.323 = (f32[256,2048]{1,0:T(8,128)}, f32[1,2048]{1,0:T(1,128)}, bf16[4,4,256,512]{3,2,1,0:T(8,128)(2,1)}, bf16[2048,1536]{1,0:T(8,128)(2,1)}, bf16[204...) custom-call(f32[256,2048]{1,0:T(8,128)} %get-tuple-element.53.middle_ref, f32[1,2048]{1,0:T(1,128)} %bitcast.16, ...), custom_call_target="tpu_custom_call" | custom-call | flops 57982058496 | bytes 37748736 | tf_op jit(solution)/shard_map/pallas_call | solution.py:1236
  320.1 104.0 %shard_map.324 = (bf16[256,2048]{1,0:T(8,128)(2,1)}, f32[8,128]{1,0:T(8,128)}, f32[640,256]{1,0:T(8,128)}, f32[256,1536]{1,0:T(8,128)}, f32[256,1536]{1,0:T(8,128)}, /*index=5*/f32[1024,640]{1,0:T(8,128)}) custom-call(f32[256,2048]{1,0:T(8,128)} %get-tuple-element.55.middle_grad_ref, f32[256,2048]{1,0:T(8,128)} %get-tuple-element.53.middle_ref, ...), custom_call_target="tpu_custom_call" | custom-call | flops 5368709120 | bytes 26214400 | tf_op jit(solution)/shard_map/pallas_call | solution.py:827
  424.1 0.0 reduce-scatter.2.cloned.1.call-update
  424.2 0.0 copy-start.7
  424.2 118.2 %shard_map.325 = (bf16[256,2048]{1,0:T(8,128)(2,1)}, f32[8,2048]{1,0:T(8,128)}, f32[256,640]{1,0:T(8,128)}, f32[256,640]{1,0:T(8,128)}, f32[8,160,160]{2,1,0:T(8,128)}, /*index=5*/f32[8,640]{1,0:T(8,128)}) custom-call(bf16[256,2048]{1,0:T(8,128)(2,1)} %tokens_ref.3, f32[1,2048]{1,0:T(1,128)} %bitcast.18, f32[256,2048]{1,0:T(8,128)} %get-tuple-element.55.middle_grad_ref, ...), custom_call_target="tpu_custom_call" | custom-call | flops 10737418240 | bytes 39321600 | tf_op jit(solution)/shard_map/pallas_call | solution.py:1056
  542.3 0.0 copy-start.2
  542.4 1.3 slice.43
  543.6 0.8 slice.42
  544.4 1.3 slice.34
  546.4 1.5 slice_reduce_fusion
  547.9 0.5 sqrt_bitcast_fusion
  548.4 0.0 copy-done.7
  548.4 0.6 multiply_multiply_fusion
  549.1 2.4 fusion
  551.5 1.6 fusion.1
  553.0 2.4 convert_element_type.3
  555.4 0.0 copy-done.2
  555.4 1.0 copy.44
  556.4 0.0 copy-done.3
  556.4 1.0 copy.45
  557.4 0.0 copy-done.6
  557.4 0.8 copy.46
  558.2 0.0 copy-done.5
  558.2 0.8 copy.47
  559.1 0.0 copy-done.4
  559.1 0.8 copy.48
  559.9 0.0 copy-done.1
  559.9 1.1 copy.49
  561.1 0.0 copy-done
  561.1 1.1 copy.50
  (7 shorter events, 0.0 us)
Async XLA Ops:
  7.2 545.9 %reduce-scatter.2.cloned.1.call-start = ((), (), s32[]{:S(2)}) async-start(), calls=%async_computation.1 | async-start | bytes 7077888 | tf_op jit(solution)/shard_map/reduce_scatter | solution.py:1272
  424.2 124.3 %copy-start.7 = (f32[640]{0:T(1024)S(1)}, f32[640]{0:T(1024)}, u32[]{:S(2)}) copy-start(f32[640]{0:T(1024)} %decay_ref.1) | copy-start | bytes 7684
  542.3 13.1 %copy-start.2 = (bf16[256,2048]{1,0:T(8,128)(2,1)S(1)}, bf16[256,2048]{1,0:T(8,128)(2,1)}, u32[]{:S(2)}) copy-start(bf16[256,2048]{1,0:T(8,128)(2,1)} %get-tuple-element.114) | copy-start | bytes 3145732
  551.5 4.9 copy-start.3
  555.4 2.0 copy-start.6
  555.4 2.8 copy-start.5
  556.4 2.7 copy-start.4
  556.4 3.5 copy-start.1
  558.2 2.8 copy-start
Sparse Core Ops, SparseCore 0:
  424.3 70.7 reduce-scatter.1

commit v7 on v6

--- a/solution.py
+++ b/solution.py
@@ -712,11 +712,12 @@
       value_proj, gate_proj, mixer_out)
 
 
-def middle_kernel(count, groups, middle_grad_ref, middle_ref, live_ref, terms_hbm, out_hbm, mixed_hbm,
-                  gate_hbm, value_hbm, layer_ref, stat_ref, out_grad_ref, gate_sum_ref, value_sum_ref, dm_hbm,
+def middle_kernel(count, groups, middle_grad_ref, live_ref, middle_hbm, terms_hbm, out_hbm, mixed_hbm,
+                  gate_hbm, value_hbm, layer_ref, stat_ref, out_grad_ref, gate_out, value_out, dm_hbm,
                   low, out_w, mixed, dm, held, slots, cube_a, slots_a, cube_b, slots_b, gate_held, gate_slots, value_held, value_slots,
+                  middle_ref, gate_sum_ref, value_sum_ref,
                   load_sem, dm_sem, ag_send, ag_recv, rs_send, rs_recv, a_send, a_recv, b_send, b_recv,
-                  gate_send, gate_recv, value_send, value_recv):
+                  gate_send, gate_recv, value_send, value_recv, own_sem):
     me = lax.axis_index("mp")
     rows, columns = middle_ref.shape
     channels = out_w.shape[0]
@@ -727,6 +728,10 @@
         ((gate_hbm, gate_held), (value_hbm, value_held), (out_hbm, out_w), (mixed_hbm, mixed), (terms_hbm, held)))]
     for load in loads:
         load.start()
+    middle_load = pltpu.make_async_copy(middle_hbm, middle_ref, own_sem.at[0])
+    middle_load.start()
+    sum_saves = [pltpu.make_async_copy(gate_sum_ref, gate_out, own_sem.at[1]),
+                 pltpu.make_async_copy(value_sum_ref, value_out, own_sem.at[2])]
     low[me] = middle_grad_ref[...].astype(BF)
     greet(count, groups)
     gather = Gather(count, low, ag_send, ag_recv)
@@ -790,6 +795,8 @@
                 dense_advance(rest)
             dense_cubes[0].result(gate_sum_ref)
             dense_cubes[1].result(value_sum_ref)
+            for save in sum_saves:
+                save.start()
         if level < levels:
             for cube in cubes:
                 cube.finish(level)
@@ -803,6 +810,7 @@
                 cube.start(rest + 1)
     cubes[0].result(out_grad_ref.at[0:half])
     cubes[1].result(out_grad_ref.at[half:channels])
+    middle_load.wait()
     row_sums = jnp.zeros((rows, 1), F32)
     for part in range(PARTS):
         span = slice(part * width, (part + 1) * width)
@@ -811,6 +819,8 @@
         row_sums = row_sums + jnp.sum(total * total, axis=1, keepdims=True)
         layer_ref[:, span] = (middle_ref[:, span] + total).astype(BF)
     stat_ref[...] = jnp.zeros(stat_ref.shape, F32) + live_total(live_ref, row_sums)
+    for save in sum_saves:
+        save.wait()
     for block in range(count):
         dm_copy(block).wait()
     gather.drain()
@@ -831,8 +841,8 @@
             jax.ShapeDtypeStruct((channels, chunk), F32), jax.ShapeDtypeStruct((chunk, units), F32),
             jax.ShapeDtypeStruct((chunk, units), F32), jax.ShapeDtypeStruct((total, channels), F32),
         ),
-        in_specs=[IN_VMEM] * 3 + [ANYWHERE] * 5,
-        out_specs=(IN_VMEM,) * 5 + (ANYWHERE,),
+        in_specs=[IN_VMEM] * 2 + [ANYWHERE] * 6,
+        out_specs=(IN_VMEM,) * 3 + (ANYWHERE,) * 3,
         scratch_shapes=[
             pltpu.VMEM((count, rows, columns), BF),
             pltpu.VMEM((channels, columns), BF),
@@ -846,24 +856,25 @@
             pltpu.VMEM((groups - 1, channels // 2, chunk), BF),
             pltpu.VMEM(split, BF), pltpu.VMEM((groups - 1, chunk, units), BF),
             pltpu.VMEM(split, BF), pltpu.VMEM((groups - 1, chunk, units), BF),
+            pltpu.VMEM((rows, columns), F32), pltpu.VMEM((chunk, units), F32), pltpu.VMEM((chunk, units), F32),
             DMA((5,)), DMA((count,)), DMA((2, count)), DMA((count,)), DMA((count, PARTS)), DMA((count + 1, PARTS)),
             DMA((groups - 1,)), DMA((groups - 1,)), DMA((groups - 1,)), DMA((groups - 1,)),
-            DMA((groups - 1,)), DMA((groups - 1,)), DMA((groups - 1,)), DMA((groups - 1,)),
+            DMA((groups - 1,)), DMA((groups - 1,)), DMA((groups - 1,)), DMA((groups - 1,)), DMA((3,)),
         ],
         compiler_params=pltpu.CompilerParams(vmem_limit_bytes=VMEM_LIMIT, collective_id=2, has_side_effects=True),
         cost_estimate=pl.CostEstimate(flops=4 * total * columns * channels, bytes_accessed=40 * total * channels,
                                       transcendentals=0),
-    )(middle_grad, middle, live, terms, mixer_out, mixed, gate_weights.reshape(split), value_weights.reshape(split))
-
-
-def input_kernel(count, groups, heads, tokens_ref, gain_ref, middle_grad_ref, mask_ref, vec_ref, rate_ref, inlet_ref,
+    )(middle_grad, live, middle, terms, mixer_out, mixed, gate_weights.reshape(split), value_weights.reshape(split))
+
+
+def input_kernel(count, groups, heads, tokens_hbm, gain_ref, middle_grad_hbm, mask_ref, vec_ref, rate_ref, inlet_ref,
                  dense_gain_ref, stat_ref, dense_stat_ref, value_hbm, gate_hbm, normed_hbm, dm_hbm, vp_hbm, gp_hbm, state_hbm, conv_hbm, forget_hbm, input_hbm,
                  input_grad_ref, flat_ref, value_grad_ref, gate_grad_ref, full, vec_grad_ref,
                  value_w, gate_w, dm, vp, gp, state, conv, forget, inlet_gate, normed, vlow, glow, dzf, dzi, dconv,
                  clow, sums, carry, held, slots, cube_a, slots_a, cube_b, slots_b, cube_c, slots_c,
-                 vec_held, vec_slots, flat_held, flat_slots,
+                 vec_held, vec_slots, flat_held, flat_slots, tokens_ref, middle_grad_ref,
                  load_sem, block_sem, normed_sem, rs_send, rs_recv, a_send, a_recv, b_send, b_recv, c_send, c_recv,
-                 f_send, f_recv, v_send, v_recv, flat_send, flat_recv):
+                 f_send, f_recv, v_send, v_recv, flat_send, flat_recv, own_sem):
     me = lax.axis_index("mp")
     rows, columns = tokens_ref.shape
     channels = value_w.shape[1]
@@ -876,6 +887,9 @@
     for load in loads:
         load.start()
 
+    own_loads = [pltpu.make_async_copy(tokens_hbm, tokens_ref, own_sem.at[0]),
+                 pltpu.make_async_copy(middle_grad_hbm, middle_grad_ref, own_sem.at[1])]
+
     def block_loads(block, slot):
         at = pl.multiple_of(block * rows, rows)
         plain = pl.ds(at, rows)
@@ -886,6 +900,8 @@
                     (conv_hbm, plain, conv), (forget_hbm, plain, forget), (input_hbm, plain, inlet_gate)))]
 
     for load in block_loads(count - 1, 0):
+        load.start()
+    for load in own_loads:
         load.start()
     zeros = jnp.zeros((8, channels), F32)
     dconv[rows:rows + 8, :] = zeros
@@ -1036,6 +1052,8 @@
     def write(span, change):
         input_grad_ref[:, span] = (middle_grad_ref[:, span] + change).astype(BF)
 
+    for load in own_loads:
+        load.wait()
     norm_back(tokens_ref, gain_ref, scatter, None, write)
     scatter.drain()
 
@@ -1060,7 +1078,7 @@
             jax.ShapeDtypeStruct((chunk, channels), F32), jax.ShapeDtypeStruct((chunk, channels), F32),
             jax.ShapeDtypeStruct((groups, slab, head), F32), jax.ShapeDtypeStruct((8, channels), F32),
         ),
-        in_specs=[IN_VMEM] * 10 + [ANYWHERE] * 10,
+        in_specs=[ANYWHERE, IN_VMEM, ANYWHERE] + [IN_VMEM] * 7 + [ANYWHERE] * 10,
         out_specs=(IN_VMEM,) * 6,
         scratch_shapes=[
             pltpu.VMEM((columns, channels), BF),
@@ -1079,10 +1097,11 @@
             pltpu.VMEM((groups, slab, head), F32), pltpu.VMEM((groups - 1, slab, head), F32),
             pltpu.VMEM((levels, 8, channels), F32), pltpu.VMEM((levels, 8, channels), F32),
             pltpu.VMEM((8, columns), F32), pltpu.VMEM((flats, 8, columns), F32),
+            pltpu.VMEM((rows, columns), BF), pltpu.VMEM((rows, columns), F32),
             DMA((2,)), DMA((2, 7)), DMA((2,)), DMA((count, PARTS)), DMA((count + 1, PARTS)),
             DMA((groups - 1,)), DMA((groups - 1,)), DMA((groups - 1,)), DMA((groups - 1,)),
             DMA((groups - 1,)), DMA((groups - 1,)), DMA((groups - 1,)), DMA((groups - 1,)),
-            DMA((levels,)), DMA((levels,)), DMA((flats,)), DMA((flats,)),
+            DMA((levels,)), DMA((levels,)), DMA((flats,)), DMA((flats,)), DMA((2,)),
         ],
         compiler_params=pltpu.CompilerParams(vmem_limit_bytes=VMEM_LIMIT, collective_id=3, has_side_effects=True),
         cost_estimate=pl.CostEstimate(flops=8 * total * columns * channels, bytes_accessed=60 * total * channels,

time: 575 us -> 572 us (level)
  no operation moved by 1% of the time
where the time goes in v7:
time: 572 us; the launch traced here: 567 us
  Pallas kernels  533 us (93%)
  local copies, waits for them, and re-layouts  15.7 us (3%)
  between operations  15 us (3%)
    pallas_call x1, Pallas kernels, call_mixer(): pl.pallas_call(functools.partial(mixer_kernel, count), out_shape=(jax.Sha...  181 us
    pallas_call x1, Pallas kernels, call_dense(): pl.pallas_call(functools.partial(dense_kernel, count, groups), out_shape=...  132 us
    pallas_call x1, Pallas kernels, call_input(): pl.pallas_call(functools.partial(input_kernel, count, groups, heads), out...  117 us
    pallas_call x1, Pallas kernels, call_middle(): pl.pallas_call(functools.partial(middle_kernel, count, groups), out_shape...  102 us
  transfers between devices with their start and end apart: 1, of which 0 were waited for; matrix products, arithmetic and copies ran while one was open for 2% of the time, Pallas kernels for 21%

profile of v7, /device:TPU:0, one launch (start us, length us, event | category | flops | bytes accessed | tf_op | source)
XLA Modules:
  0.0 566.8 jit_solution(8153545710270545040)
XLA Ops:
  7.2 0.0 reduce-scatter.2.cloned.1.call-start
  7.2 181.1 %shard_map.322 = (f32[256,2048]{1,0:T(8,128)}, f32[8,128]{1,0:T(8,128)}, f32[1032,8]{1,0:T(8,128)}, f32[8,640]{1,0:T(8,128)}, bf16[640,640]{1,0:T(8,128)(2,1)}, ...) custom-call(s32[1,4]{1,0:T(1,128)} %lengths_ref.1, ...), custom_call_target="tpu_custom_call" | custom-call | flops 8053063680 | bytes 26214400 | tf_op jit(solution)/shard_map/pallas_call | solution.py:679
  188.4 131.7 %shard_map.323 = (f32[256,2048]{1,0:T(8,128)}, f32[1,2048]{1,0:T(1,128)}, bf16[4,4,256,512]{3,2,1,0:T(8,128)(2,1)}, bf16[2048,1536]{1,0:T(8,128)(2,1)}, bf16[204...) custom-call(f32[256,2048]{1,0:T(8,128)} %get-tuple-element.53.middle_ref.middle_hbm, f32[1,2048]{1,0:T(1,128)} %bitcast.16, ...), custom_call_target="tpu_custom_call" | custom-call | flops 57982058496 | bytes 37748736 | tf_op jit(solution)/shard_map/pallas_call | solution.py:1255
  320.1 102.4 %shard_map.324 = (bf16[256,2048]{1,0:T(8,128)(2,1)}, f32[8,128]{1,0:T(8,128)}, f32[640,256]{1,0:T(8,128)}, f32[256,1536]{1,0:T(8,128)}, f32[256,1536]{1,0:T(8,128)}, /*index=5*/f32[1024,640]{1,0:T(8,128)}) custom-call(f32[256,2048]{1,0:T(8,128)} %get-tuple-element.55.middle_grad_ref.middle_grad_hbm, s32[1,256]{1,0:T(1,128)} %bitcast.15, ...), custom_call_target="tpu_custom_call" | custom-call | flops 5368709120 | bytes 26214400 | tf_op jit(solution)/shard_map/pallas_call | solution.py:837
  422.5 0.0 reduce-scatter.2.cloned.1.call-update
  422.6 0.0 copy-start.7
  422.6 117.3 %shard_map.325 = (bf16[256,2048]{1,0:T(8,128)(2,1)}, f32[8,2048]{1,0:T(8,128)}, f32[256,640]{1,0:T(8,128)}, f32[256,640]{1,0:T(8,128)}, f32[8,160,160]{2,1,0:T(8,128)}, /*index=5*/f32[8,640]{1,0:T(8,128)}) custom-call(bf16[256,2048]{1,0:T(8,128)(2,1)} %tokens_hbm.1, f32[1,2048]{1,0:T(1,128)} %bitcast.18, ...), custom_call_target="tpu_custom_call" | custom-call | flops 10737418240 | bytes 39321600 | tf_op jit(solution)/shard_map/pallas_call | solution.py:1074
  539.9 0.0 copy-start.2
  539.9 1.3 slice.43
  541.1 0.8 slice.42
  541.9 1.3 slice.34
  543.9 1.5 slice_reduce_fusion
  545.4 0.5 sqrt_bitcast_fusion
  546.0 0.0 copy-done.7
  546.0 0.6 multiply_multiply_fusion
  546.6 2.4 fusion
  549.0 1.6 fusion.1
  550.6 2.4 convert_element_type.3
  553.0 0.0 copy-done.2
  553.0 1.0 copy.44
  553.9 0.0 copy-done.3
  553.9 1.0 copy.45
  554.9 0.0 copy-done.6
  554.9 0.8 copy.46
  555.8 0.0 copy-done.5
  555.8 0.8 copy.47
  556.6 0.0 copy-done.4
  556.6 0.8 copy.48
  557.4 0.0 copy-done.1
  557.4 1.1 copy.49
  558.6 0.0 copy-done
  558.6 1.1 copy.50
  (7 shorter events, 0.0 us)
Async XLA Ops:
  7.2 543.4 %reduce-scatter.2.cloned.1.call-start = ((), (), s32[]{:S(2)}) async-start(), calls=%async_computation.1 | async-start | bytes 7077888 | tf_op jit(solution)/shard_map/reduce_scatter | solution.py:1291
  422.6 123.4 %copy-start.7 = (f32[640]{0:T(1024)S(1)}, f32[640]{0:T(1024)}, u32[]{:S(2)}) copy-start(f32[640]{0:T(1024)} %decay_ref.1) | copy-start | bytes 7684
  539.9 13.1 %copy-start.2 = (bf16[256,2048]{1,0:T(8,128)(2,1)S(1)}, bf16[256,2048]{1,0:T(8,128)(2,1)}, u32[]{:S(2)}) copy-start(bf16[256,2048]{1,0:T(8,128)(2,1)} %get-tuple-element.114) | copy-start | bytes 3145732
  549.0 4.9 copy-start.3
  553.0 2.0 copy-start.6
  553.0 2.8 copy-start.5
  553.9 2.7 copy-start.4
  553.9 3.5 copy-start.1
  555.8 2.8 copy-start
Sparse Core Ops, SparseCore 0:
  422.7 70.7 reduce-scatter.1
